TPU v7x, 32 devices: a whole 2x2x4 slice. The times are simulated.
32 devices in a mesh: dp: 4 (over y, x), expert: 8 (over z, core).
Axes of the slice: x: 2, y: 2, z: 4, core: 2. Of those that a mesh axis runs over, the one named last changes fastest.
Arguments:
- tokens: bfloat16 [8192, 768], P(('dp', 'expert')), may hold values from -6 to 6
- cotangent: bfloat16 [8192, 768], P(('dp', 'expert')), may hold values from -6 to 6
- routes: int32 [8192, 1], P(('dp', 'expert')), may hold values from 0 to 7; in each aligned block of 256 rows (0 to 255, 256 to 511, ...) at most 64 rows name the same one
- buckets: int32 [511], replicated, may hold values from 0 to 31
- norm_attn: float32 [768], replicated, may hold values from 0.1 to 1.9
- norm_ffn: float32 [768], replicated, may hold values from 0.1 to 1.9
- rel_table: float32 [32, 12], replicated, may hold values from -6 to 6
- query_weight: bfloat16 [768, 768], P(('dp', 'expert')), may hold values from -0.078125 to 0.078125
- key_weight: bfloat16 [768, 768], P(('dp', 'expert')), may hold values from -0.078125 to 0.078125
- value_weight: bfloat16 [768, 768], P(('dp', 'expert')), may hold values from -0.21875 to 0.21875
- out_weight: bfloat16 [768, 768], P(('dp', 'expert')), may hold values from -1.75 to 1.75
- router_weight: bfloat16 [768, 8], P(('dp', 'expert')), may hold values from -0.109375 to 0.109375
- expert_in: bfloat16 [8, 768, 3072], P('expert'), may hold values from -0.21875 to 0.21875
- expert_out: bfloat16 [8, 3072, 768], P('expert'), may hold values from -3.359375 to 3.359375
Outputs:
- output: bfloat16 [8192, 768], P(('dp', 'expert'))
- input_grad: float32 [8192, 768], P(('dp', 'expert'))
- grad_norm_attn: float32 [768], replicated
- grad_norm_ffn: float32 [768], replicated
- grad_rel: float32 [32, 12], replicated
- grad_query: float32 [768, 768], P(('dp', 'expert'))
- grad_key: float32 [768, 768], P(('dp', 'expert'))
- grad_value: float32 [768, 768], P(('dp', 'expert'))
- grad_out: float32 [768, 768], P(('dp', 'expert'))
- grad_router: float32 [768, 8], P(('dp', 'expert'))
- grad_expert_in: float32 [8, 768, 3072], P('expert', None, 'dp')
- grad_expert_out: float32 [8, 3072, 768], P('expert', 'dp')
Inputs may be any that keep to these rules, and one draw needn't show every extreme that they name: `routes`: within the 256 rows of one device no expert is named by more than 64 rows, and in every draw some expert is named by exactly 64 rows of some device.
All inputs are finite; a program needn't handle non-finite values.
Results may differ from a plain program's by a relative error of at most 0.017.
Values may be sent and summed in bfloat16 or wider, within the bound.
No kernel may reach another device: no remote copies, remote signals or barrier semaphores. Data moves between devices by JAX's collectives and lax.ppermute only.
A program may use at most 192 MiB of HBM per device.

v0:
```python
import jax
import jax.numpy as jnp
from jax import lax
from jax.sharding import PartitionSpec as P

PRECISE = lax.Precision.HIGHEST
EPSILON = 1e-06


def rms_norm(values_in, gain_in):
    return (
        values_in
        * lax.rsqrt(jnp.mean(values_in * values_in, axis=-1, keepdims=True) + EPSILON)
        * gain_in
    )


def gelu_tanh(values_in):
    return jax.nn.gelu(values_in, approximate=True)


def toeplitz(segment, row_count, col_count):
    full_width = row_count + col_count
    padded = jnp.pad(segment, ((0, 0), (0, 1)))
    tiled = jnp.tile(padded, (1, row_count + 1))
    skewed = tiled[:, : row_count * (full_width + 1)].reshape(
        segment.shape[0], row_count, full_width + 1
    )
    return skewed[:, ::-1, :col_count]


def rows_forward(rows, first_part, second_part):
    hidden = gelu_tanh(jnp.dot(rows, first_part, preferred_element_type=jnp.float32)).astype(
        jnp.bfloat16
    )
    return jnp.dot(hidden, second_part, preferred_element_type=jnp.float32)


def rows_backward(rows, grads, first_part, second_part):
    pre_act = jnp.dot(rows, first_part, preferred_element_type=jnp.float32)
    hidden_full, gelu_pull = jax.vjp(gelu_tanh, pre_act)
    hidden_back = hidden_full.astype(jnp.bfloat16)
    grad_second = jnp.einsum("rf,rd->fd", hidden_back, grads, preferred_element_type=jnp.float32)
    hidden_grad = jnp.einsum("rd,fd->rf", grads, second_part, preferred_element_type=jnp.float32)
    pre_grad = gelu_pull(hidden_grad)[0].astype(jnp.bfloat16)
    grad_first = jnp.einsum("rd,rf->df", rows, pre_grad, preferred_element_type=jnp.float32)
    back_rows = jnp.einsum("rf,df->rd", pre_grad, first_part, preferred_element_type=jnp.float32)
    return (grad_first, grad_second, back_rows)


def per_device(
    tokens,
    cotangent,
    routes,
    buckets,
    norm_attn,
    norm_ffn,
    rel_table,
    query_weight,
    key_weight,
    value_weight,
    out_weight,
    router_weight,
    expert_in,
    expert_out,
):
    seq_length, model_width = tokens.shape
    head_count = rel_table.shape[1]
    head_size = model_width // head_count
    bucket_count = rel_table.shape[0]
    expert_count = router_weight.shape[1]
    slot_room = max(2, 2 * seq_length // lax.axis_size("expert"))
    block_rows = min(seq_length, 512)
    span = block_rows + seq_length - 1
    weights = (
        lax.all_gather(query_weight, ("dp", "expert"), axis=0, tiled=True),
        lax.all_gather(key_weight, ("dp", "expert"), axis=0, tiled=True),
        lax.all_gather(value_weight, ("dp", "expert"), axis=0, tiled=True),
        lax.all_gather(out_weight, ("dp", "expert"), axis=0, tiled=True),
        lax.all_gather(router_weight, ("dp", "expert"), axis=0, tiled=True),
    )
    joint_weight = jnp.concatenate([weights[0], weights[1], weights[2]], axis=1)
    proj_weight = weights[3]
    route_weight = weights[4]
    inputs = tokens.astype(jnp.float32)
    normed_full, norm_pull = jax.vjp(rms_norm, inputs, norm_attn)
    normed = normed_full.astype(jnp.bfloat16)
    joint = jnp.dot(normed, joint_weight, preferred_element_type=jnp.float32).astype(jnp.bfloat16)
    queries = joint[:, :model_width].reshape(seq_length, head_count, head_size)
    keys_all = joint[:, model_width : 2 * model_width].reshape(seq_length, head_count, head_size)
    values_all = joint[:, 2 * model_width :].reshape(seq_length, head_count, head_size)
    onehot_bucket = (buckets[:, None] == jnp.arange(bucket_count, dtype=jnp.int32)[None, :]).astype(
        jnp.float32
    )
    bias_along = jnp.dot(onehot_bucket, rel_table, precision=PRECISE).T
    start_row = 0
    offset = seq_length - block_rows - start_row
    bias_block = toeplitz(bias_along, block_rows, seq_length)
    scores = (
        jnp.einsum("qhd,khd->hqk", queries, keys_all, preferred_element_type=jnp.float32)
        + bias_block
    )
    row_top = jnp.max(scores, axis=-1, keepdims=True)
    exponent = jnp.exp(scores - row_top)
    row_total = jnp.sum(exponent, axis=-1, keepdims=True)
    prob_low = (exponent / row_total).astype(jnp.bfloat16)
    mixed_parts = jnp.einsum(
        "hqk,khd->qhd", prob_low, values_all, preferred_element_type=jnp.float32
    ).astype(jnp.bfloat16)
    totals = [row_top + jnp.log(row_total)]
    mixed_rows = mixed_parts.reshape(seq_length, model_width)
    middle = inputs + jnp.dot(mixed_rows, proj_weight, preferred_element_type=jnp.float32)
    ffn_full, ffn_pull = jax.vjp(rms_norm, middle, norm_ffn)
    ffn_in = ffn_full.astype(jnp.bfloat16)
    logits = jnp.dot(ffn_in, route_weight, preferred_element_type=jnp.float32)
    exponent_gate = jnp.exp(logits - jnp.max(logits, axis=-1, keepdims=True))
    router_probs = exponent_gate / jnp.sum(exponent_gate, axis=-1, keepdims=True)
    chosen = routes[:, 0]
    picked = (chosen[:, None] == jnp.arange(expert_count, dtype=jnp.int32)[None, :]).astype(
        jnp.int32
    )
    picked_float = picked.astype(jnp.float32)
    gate_prob = jnp.sum(router_probs * picked_float, axis=1)
    slot_rank = jnp.sum((jnp.cumsum(picked, axis=0) - 1) * picked, axis=1)
    slot_index = chosen * slot_room + slot_rank
    dispatch = (
        jnp.arange(expert_count * slot_room, dtype=jnp.int32)[:, None] == slot_index[None, :]
    ).astype(jnp.bfloat16)
    outgoing = (
        jnp.dot(dispatch, ffn_in, preferred_element_type=jnp.float32)
        .astype(jnp.bfloat16)
        .reshape(expert_count, slot_room, model_width)
    )
    arrived = lax.all_to_all(outgoing, "expert", split_axis=0, concat_axis=0, tiled=True)
    w_first = expert_in[0]
    w_second = expert_out[0]
    rows_all = arrived.reshape(-1, model_width)
    partial_value = rows_forward(rows_all, w_first, w_second)
    produced = partial_value.astype(jnp.bfloat16).reshape(arrived.shape)
    returned_rows = lax.all_to_all(
        produced, "expert", split_axis=0, concat_axis=0, tiled=True
    ).reshape(-1, model_width)
    expert_result = jnp.einsum(
        "st,sd->td", dispatch, returned_rows, preferred_element_type=jnp.float32
    )
    result = middle + gate_prob[:, None] * expert_result
    upstream = cotangent.astype(jnp.float32)
    gate_grad = jnp.sum(upstream * expert_result, axis=1)
    branch_grad = (upstream * gate_prob[:, None]).astype(jnp.bfloat16)
    outgoing_grad = (
        jnp.dot(dispatch, branch_grad, preferred_element_type=jnp.float32)
        .astype(jnp.bfloat16)
        .reshape(expert_count, slot_room, model_width)
    )
    arrived_grad = lax.all_to_all(outgoing_grad, "expert", split_axis=0, concat_axis=0, tiled=True)
    grads_all = arrived_grad.reshape(-1, model_width)
    grad_first, grad_second, back_rows = rows_backward(rows_all, grads_all, w_first, w_second)
    sent_back = back_rows.astype(jnp.bfloat16).reshape(arrived.shape)
    grad_first, grad_second = (
        lax.psum_scatter(
            grad_first.astype(jnp.bfloat16), "dp", scatter_dimension=1, tiled=True
        ).astype(jnp.float32),
        lax.psum_scatter(
            grad_second.astype(jnp.bfloat16), "dp", scatter_dimension=0, tiled=True
        ).astype(jnp.float32),
    )
    returned_grad = lax.all_to_all(
        sent_back, "expert", split_axis=0, concat_axis=0, tiled=True
    ).reshape(-1, model_width)
    expert_in_grad = jnp.einsum(
        "st,sd->td", dispatch, returned_grad, preferred_element_type=jnp.float32
    )
    logit_grad = (router_probs * (picked_float - gate_prob[:, None]) * gate_grad[:, None]).astype(
        jnp.bfloat16
    )
    grad_router = jnp.einsum("td,te->de", ffn_in, logit_grad, preferred_element_type=jnp.float32)
    ffn_grad = (
        jnp.einsum("te,de->td", logit_grad, route_weight, preferred_element_type=jnp.float32)
        + expert_in_grad
    )
    middle_norm_grad, gain_ffn_grad = ffn_pull(ffn_grad)
    middle_grad = upstream + middle_norm_grad
    attn_grad = middle_grad.astype(jnp.bfloat16)
    grad_proj = jnp.einsum("td,te->de", mixed_rows, attn_grad, preferred_element_type=jnp.float32)
    mixed_grad = (
        jnp.einsum("te,de->td", attn_grad, proj_weight, preferred_element_type=jnp.float32)
        .astype(jnp.bfloat16)
        .reshape(seq_length, head_count, head_size)
    )
    query_parts = []
    key_grad = jnp.zeros((seq_length, head_count, head_size), jnp.float32)
    value_grad = jnp.zeros((seq_length, head_count, head_size), jnp.float32)
    along_grad = jnp.zeros(bias_along.shape, jnp.float32)
    for block_number, start_row in enumerate(range(0, seq_length, block_rows)):
        offset = seq_length - block_rows - start_row

        def make_bias(segment_in):
            return toeplitz(segment_in, block_rows, seq_length)

        bias_block, bias_pull = jax.vjp(make_bias, bias_along)
        scores = (
            jnp.einsum("qhd,khd->hqk", queries, keys_all, preferred_element_type=jnp.float32)
            + bias_block
        )
        prob_full = jnp.exp(scores - totals[block_number])
        prob_low = prob_full.astype(jnp.bfloat16)
        value_grad = jnp.einsum(
            "hqk,qhd->khd", prob_low, mixed_grad, preferred_element_type=jnp.float32
        )
        prob_grad = jnp.einsum(
            "qhd,khd->hqk", mixed_grad, values_all, preferred_element_type=jnp.float32
        )
        inner_sum = jnp.sum(prob_full * prob_grad, axis=-1, keepdims=True)
        score_grad = (prob_full * (prob_grad - inner_sum)).astype(jnp.bfloat16)
        query_parts.append(
            jnp.einsum("hqk,khd->qhd", score_grad, keys_all, preferred_element_type=jnp.float32)
        )
        key_grad = jnp.einsum(
            "hqk,qhd->khd", score_grad, queries, preferred_element_type=jnp.float32
        )
        along_grad = along_grad.at[:, offset : offset + span].add(
            bias_pull(score_grad.astype(jnp.float32))[0]
        )
    query_grad = query_parts[0].reshape(seq_length, model_width)
    joint_grad = jnp.concatenate(
        [
            query_grad,
            key_grad.reshape(seq_length, model_width),
            value_grad.reshape(seq_length, model_width),
        ],
        axis=1,
    ).astype(jnp.bfloat16)
    grad_joint = jnp.einsum("td,te->de", normed, joint_grad, preferred_element_type=jnp.float32)
    normed_grad = jnp.einsum(
        "te,de->td", joint_grad, joint_weight, preferred_element_type=jnp.float32
    )
    input_norm_grad, gain_attn_grad = norm_pull(normed_grad)
    input_grad = middle_grad + input_norm_grad
    rel_grad = jnp.dot(onehot_bucket.T, along_grad.T, precision=PRECISE)
    dense_sums = (
        lax.psum_scatter(
            grad_joint[:, :model_width], ("dp", "expert"), scatter_dimension=0, tiled=True
        ),
        lax.psum_scatter(
            grad_joint[:, model_width : 2 * model_width],
            ("dp", "expert"),
            scatter_dimension=0,
            tiled=True,
        ),
        lax.psum_scatter(
            grad_joint[:, 2 * model_width :], ("dp", "expert"), scatter_dimension=0, tiled=True
        ),
        lax.psum_scatter(grad_proj, ("dp", "expert"), scatter_dimension=0, tiled=True),
        lax.psum_scatter(grad_router, ("dp", "expert"), scatter_dimension=0, tiled=True),
    )
    small_sums = lax.psum((gain_attn_grad, gain_ffn_grad, rel_grad), ("dp", "expert"))
    return (
        result.astype(jnp.bfloat16),
        input_grad,
        small_sums[0],
        small_sums[1],
        small_sums[2],
        dense_sums[0],
        dense_sums[1],
        dense_sums[2],
        dense_sums[3],
        dense_sums[4],
        grad_first[None],
        grad_second[None],
    )


def solution(mesh):
    in_specs = (
        P(("dp", "expert"), None),
        P(("dp", "expert"), None),
        P(("dp", "expert"), None),
        P(),
        P(),
        P(),
        P(),
        P(("dp", "expert"), None),
        P(("dp", "expert"), None),
        P(("dp", "expert"), None),
        P(("dp", "expert"), None),
        P(("dp", "expert"), None),
        P("expert", None, None),
        P("expert", None, None),
    )
    out_specs = (
        P(("dp", "expert"), None),
        P(("dp", "expert"), None),
        P(),
        P(),
        P(),
        P(("dp", "expert"), None),
        P(("dp", "expert"), None),
        P(("dp", "expert"), None),
        P(("dp", "expert"), None),
        P(("dp", "expert"), None),
        P("expert", None, "dp"),
        P("expert", "dp", None),
    )
    return jax.shard_map(
        per_device, mesh=mesh, in_specs=in_specs, out_specs=out_specs, check_vma=False
    )
```

profile of v0, /device:TPU:0, one launch (start us, length us, event | category | flops | bytes accessed | tf_op | source)
XLA Modules:
  0.0 885.6 jit_solution(13464131860101243146)
XLA Ops:
  17.6 4.9 copy.68
  22.5 3.6 slice.60
  26.1 15.7 %reshape.200 = f32[12,256,513]{2,1,0:T(8,128)} reshape(f32[12,131328]{1,0:T(8,128)} %slice.60) | data formatting | bytes 12607488 | tf_op jit(solution)/shard_map/reshape | solution.py:26
  46.1 25.9 %rev.7 = f32[12,256,256]{1,2,0:T(8,128)} reverse(f32[12,256,256]{1,2,0:T(8,128)} %copy.66), dimensions={1} | reverse | bytes 6291456 | tf_op jit(solution)/shard_map/rev | solution.py:29
  74.5 49.6 %all-gather.8.cloned.1.call-done = bf16[768,768]{1,0:T(8,128)(2,1)} async-done(((bf16[24,768]{1,0:T(8,128)(2,1)}), bf16[768,768]{1,0:T(8,128)(2,1)}) %all-gather.8.cloned.1.call-update) | async-done | bytes 1179664 | tf_op jit(solution)/shard_map/all_gather | solution.py:77
  126.6 53.7 %all-gather.10.cloned.1.call-done = bf16[768,768]{1,0:T(8,128)(2,1)} async-done(((bf16[24,768]{1,0:T(8,128)(2,1)}), bf16[768,768]{1,0:T(8,128)(2,1)}) %all-gather.10.cloned.1.call-update) | async-done | bytes 1179664 | tf_op jit(solution)/shard_map/all_gather | solution.py:78
  194.1 42.2 %all-gather.12.cloned.1.call-done = bf16[768,768]{1,0:T(8,128)(2,1)} async-done(((bf16[24,768]{1,0:T(8,128)(2,1)}), bf16[768,768]{1,0:T(8,128)(2,1)}) %all-gather.12.cloned.1.call-update) | async-done | bytes 1179664 | tf_op jit(solution)/shard_map/all_gather | solution.py:79
  241.4 4.2 all-to-all-start
  245.6 50.3 %all-gather = bf16[32,24,8]{1,2,0:T(8,128)(2,1)S(1)} all-gather(bf16[1,24,8]{1,2,0:T(8,128)(2,1)} %bitcast.122), channel_id=1, replica_groups=mesh['dp'=4,'expert'=8] {'dp','expert'}, dimensions={0}, use_global_device_ids=true | all-gather | bytes 12672 | tf_op jit(solution)/shard_map/all_gather | solution.py:80
  304.1 4.2 all-to-all-start.2
  308.3 7.8 fusion.13
  316.2 13.1 %all-to-all-done.2 = bf16[8,64,768]{2,1,0:T(8,128)(2,1)} async-done(((bf16[8,64,768]{2,1,0:T(8,128)(2,1)}), bf16[8,64,768]{2,1,0:T(8,128)(2,1)}, u32[]{:S(2)}, u32[]{:S(2)}) %all-to-all-start.2) | async-done | bytes 786464 | tf_op jit(solution)/shard_map/all_to_all | solution.py:155
  329.3 8.6 fusion.6
  339.6 5.5 convolution_convert_fusion.1
  345.4 8.4 convolution_convert_fusion
  353.8 9.1 %fusion.26 = bf16[512,768]{1,0:T(8,128)(2,1)} fusion(bf16[1,3072,768]{2,1,0:T(8,128)(2,1)} %param.31, f32[512,3072]{1,0:T(8,128)} %fusion.13), kind=kOutput, calls=%fused_computation.38 | convolution fusion | flops 2430468096 | bytes 11796480 | tf_op jit(solution)/shard_map/dot_general | solution.py:36
  362.9 4.2 all-to-all-start.1
  367.1 6.9 fusion.23
  374.0 14.0 %all-to-all-done.1 = bf16[8,64,768]{2,1,0:T(8,128)(2,1)} async-done(((bf16[8,64,768]{2,1,0:T(8,128)(2,1)}), bf16[8,64,768]{2,1,0:T(8,128)(2,1)}, u32[]{:S(2)}, u32[]{:S(2)}) %all-to-all-start.1) | async-done | bytes 786464 | tf_op jit(solution)/shard_map/all_to_all | solution.py:140
  388.1 4.2 all-to-all-start.3
  397.4 15.9 %all-to-all-done.3 = bf16[8,64,768]{2,1,0:T(8,128)(2,1)} async-done(((bf16[8,64,768]{2,1,0:T(8,128)(2,1)}), bf16[8,64,768]{2,1,0:T(8,128)(2,1)}, u32[]{:S(2)}, u32[]{:S(2)}) %all-to-all-start.3) | async-done | bytes 786464 | tf_op jit(solution)/shard_map/all_to_all | solution.py:167
  438.2 17.2 %rev.8 = f32[12,256,256]{1,2,0:T(8,128)} reverse(bf16[12,256,256]{1,2,0:T(8,128)(2,1)S(1)} %copy-done.3), dimensions={1} | reverse | bytes 4718592 | tf_op jit(solution)/shard_map/transpose(jvp())/rev | solution.py:29
  457.8 3.9 pad.21.clone
  461.6 13.1 %reshape.215 = f32[12,131328]{1,0:T(8,128)} reshape(f32[12,256,513]{2,1,0:T(8,128)} %pad.21.clone) | data formatting | bytes 12607488 | tf_op jit(solution)/shard_map/transpose(jvp())/reshape | solution.py:26
  474.8 6.0 pad.22
  480.7 9.7 %reshape.216 = f32[12,257,512]{2,1,0:T(8,128)} reshape(f32[12,131584]{1,0:T(8,128)} %pad.22) | data formatting | bytes 12632064 | tf_op jit(solution)/shard_map/transpose(jvp())/reshape | solution.py:25
  490.5 3.8 reduce_sum.145
  498.3 38.3 %all-reduce.4 = (f32[768]{0:T(1024)}, f32[768]{0:T(1024)}, f32[32,12]{0,1:T(8,128)}, f32[768,8]{0,1:T(8,128)S(1)}) all-reduce(f32[768]{0:T(1024)S(1)} %get-tuple-element.34, f32[768]{0:T(1024)S(1)} %copy-done.40, f32[32,12]{0,1:T(8,128)S(1)} %fusion.51, f32[768,8]{0,1:T(8,128)S(1)} %fusion.72), channel_id=1, replica_groups=mesh['dp'=4,'expert'=8] {'dp','expert'}, use_global_device_ids=true, to_apply=%region_15.16 | all-reduce | flops 8064 | bytes 64512 | tf_op jit(solution)/shard_map/psum | solution.py:256
  544.1 20.9 %reduce-scatter.14.cloned.1.call-done = f32[24,768]{1,0:T(8,128)} async-done(((f32[768,768]{1,0:T(8,128)}), f32[24,768]{1,0:T(8,128)}) %reduce-scatter.14.cloned.1.call-update) | async-done | bytes 73744 | tf_op jit(solution)/shard_map/reduce_scatter | solution.py:253
  565.0 104.7 %reduce-scatter.12.cloned.1.call-done = f32[24,768]{1,0:T(8,128)} async-done(((f32[768,768]{1,0:T(8,128)}), f32[24,768]{1,0:T(8,128)}) %reduce-scatter.12.cloned.1.call-update) | async-done | bytes 73744 | tf_op jit(solution)/shard_map/reduce_scatter | solution.py:250
  669.7 104.0 %reduce-scatter.10.cloned.1.call-done = f32[24,768]{1,0:T(8,128)} async-done(((f32[768,768]{1,0:T(8,128)}), f32[24,768]{1,0:T(8,128)}) %reduce-scatter.10.cloned.1.call-update) | async-done | bytes 73744 | tf_op jit(solution)/shard_map/reduce_scatter | solution.py:244
  773.7 104.6 %reduce-scatter.8.cloned.1.call-done = f32[24,768]{1,0:T(8,128)} async-done(((f32[768,768]{1,0:T(8,128)}), f32[24,768]{1,0:T(8,128)}) %reduce-scatter.8.cloned.1.call-update) | async-done | bytes 73744 | tf_op jit(solution)/shard_map/reduce_scatter | solution.py:241
  (188 shorter events, 92.1 us)
Async XLA Ops:
  7.2 7.5 copy-start
  7.2 64.8 %all-gather.6.cloned.1.call-start = ((), (), s32[]{:S(2)}) async-start(), calls=%async_computation.10 | async-start | bytes 1216512 | tf_op jit(solution)/shard_map/all_gather | solution.py:76
  7.9 116.2 %all-gather.8.cloned.1.call-start = ((), (), s32[]{:S(2)}) async-start(), calls=%async_computation.11 | async-start | bytes 1216512 | tf_op jit(solution)/shard_map/all_gather | solution.py:77
  8.7 171.6 %all-gather.10.cloned.1.call-start = ((), (), s32[]{:S(2)}) async-start(), calls=%async_computation.12 | async-start | bytes 1216512 | tf_op jit(solution)/shard_map/all_gather | solution.py:78
  9.4 226.9 %all-gather.12.cloned.1.call-start = ((), (), s32[]{:S(2)}) async-start(), calls=%async_computation.13 | async-start | bytes 1216512 | tf_op jit(solution)/shard_map/all_gather | solution.py:79
  11.1 5.4 copy-start.47
  15.7 167.1 %copy-start.38 = (f32[256]{0:T(256)}, f32[256]{0:T(256)S(1)}, u32[]{:S(2)}) copy-start(f32[256]{0:T(256)S(1)} %fusion.64) | copy-start | bytes 3076
  72.0 110.8 %copy-start.8 = (bf16[256,768]{1,0:T(8,128)(2,1)S(1)}, bf16[256,768]{1,0:T(8,128)(2,1)}, u32[]{:S(2)}) copy-start(bf16[256,768]{1,0:T(8,128)(2,1)} %param.18) | copy-start | bytes 1179652
  72.0 110.8 %copy-start.26 = (f32[768]{0:T(1024)S(1)}, f32[768]{0:T(1024)}, u32[]{:S(2)}) copy-start(f32[768]{0:T(1024)} %param.22) | copy-start | bytes 9220
  192.7 46.5 %copy-start.28 = (f32[768]{0:T(1024)S(1)}, f32[768]{0:T(1024)}, u32[]{:S(2)}) copy-start(f32[768]{0:T(1024)} %param.23) | copy-start | bytes 9220
  194.1 46.0 %copy-start.30 = (s32[256]{0:T(256)S(1)}, s32[256]{0:T(256)}, u32[]{:S(2)}) copy-start(s32[256]{0:T(256)} %multiply_add_fusion) | copy-start | bytes 3076
  238.9 57.6 %copy-start.36 = (f32[256]{0:T(256)}, f32[256]{0:T(256)S(1)}, u32[]{:S(2)}) copy-start(f32[256]{0:T(256)S(1)} %fusion.65) | copy-start | bytes 3076
  241.4 62.7 %all-to-all-start = ((bf16[8,64,768]{2,1,0:T(8,128)(2,1)}), bf16[8,64,768]{2,1,0:T(8,128)(2,1)}, u32[]{:S(2)}, u32[]{:S(2)}) async-start(bf16[8,64,768]{2,1,0:T(8,128)(2,1)} %bitcast.103), calls=%async_computation | async-start | bytes 1572864 | tf_op jit(solution)/shard_map/all_to_all | solution.py:134
  304.1 25.2 %all-to-all-start.2 = ((bf16[8,64,768]{2,1,0:T(8,128)(2,1)}), bf16[8,64,768]{2,1,0:T(8,128)(2,1)}, u32[]{:S(2)}, u32[]{:S(2)}) async-start(bf16[8,64,768]{2,1,0:T(8,128)(2,1)} %bitcast.102), calls=%async_computation.2 | async-start | bytes 1572864 | tf_op jit(solution)/shard_map/all_to_all | solution.py:155
  308.3 230.1 %reduce-scatter.16.cloned.1.call-start = ((), (), s32[]{:S(2)}) async-start(), calls=%async_computation.18 | async-start | bytes 5898240 | tf_op jit(solution)/shard_map/reduce_scatter | solution.py:160
  345.1 196.2 %reduce-scatter.18.cloned.1.call-start = ((), (), s32[]{:S(2)}) async-start(), calls=%async_computation.19 | async-start | bytes 5898240 | tf_op jit(solution)/shard_map/reduce_scatter | solution.py:163
  362.9 25.2 %all-to-all-start.1 = ((bf16[8,64,768]{2,1,0:T(8,128)(2,1)}), bf16[8,64,768]{2,1,0:T(8,128)(2,1)}, u32[]{:S(2)}, u32[]{:S(2)}) async-start(bf16[8,64,768]{2,1,0:T(8,128)(2,1)} %bitcast.115), calls=%async_computation.1 | async-start | bytes 1572864 | tf_op jit(solution)/shard_map/all_to_all | solution.py:140
  388.1 25.2 %all-to-all-start.3 = ((bf16[8,64,768]{2,1,0:T(8,128)(2,1)}), bf16[8,64,768]{2,1,0:T(8,128)(2,1)}, u32[]{:S(2)}, u32[]{:S(2)}) async-start(bf16[8,64,768]{2,1,0:T(8,128)(2,1)} %bitcast.114), calls=%async_computation.3 | async-start | bytes 1572864 | tf_op jit(solution)/shard_map/all_to_all | solution.py:167
  392.3 172.7 %reduce-scatter.14.cloned.1.call-start = ((), (), s32[]{:S(2)}) async-start(), calls=%async_computation.17 | async-start | bytes 2433024 | tf_op jit(solution)/shard_map/reduce_scatter | solution.py:253
  413.3 5.0 copy-start.20
  420.2 249.6 %reduce-scatter.12.cloned.1.call-start = ((), (), s32[]{:S(2)}) async-start(), calls=%async_computation.16 | async-start | bytes 2433024 | tf_op jit(solution)/shard_map/reduce_scatter | solution.py:250
  436.8 337.0 %reduce-scatter.10.cloned.1.call-start = ((), (), s32[]{:S(2)}) async-start(), calls=%async_computation.15 | async-start | bytes 2433024 | tf_op jit(solution)/shard_map/reduce_scatter | solution.py:244
  437.5 440.8 %reduce-scatter.8.cloned.1.call-start = ((), (), s32[]{:S(2)}) async-start(), calls=%async_computation.14 | async-start | bytes 2433024 | tf_op jit(solution)/shard_map/reduce_scatter | solution.py:241
  490.4 4.2 copy-start.35
  490.4 4.2 copy-start.42
  490.5 4.2 copy-start.46
  490.5 4.3 copy-start.17
  490.5 4.3 copy-start.19
  490.5 4.3 copy-start.22
  494.8 42.4 %copy-start.48 = (f32[256]{0:T(256)S(1)}, f32[256]{0:T(256)}, u32[]{:S(2)}) copy-start(f32[256]{0:T(256)} %copy-done.47) | copy-start | bytes 3076
  494.8 42.4 %copy-start.5 = (f32[256,768]{1,0:T(8,128)S(1)}, f32[256,768]{1,0:T(8,128)}, u32[]{:S(2)}) copy-start(f32[256,768]{1,0:T(8,128)} %copy-done.4) | copy-start | bytes 2359300
  537.3 341.0 %copy-start.1 = (f32[32,12]{0,1:T(8,128)S(1)}, f32[32,12]{0,1:T(8,128)}, u32[]{:S(2)}) copy-start(f32[32,12]{0,1:T(8,128)} %param.24) | copy-start | bytes 4612
  (34 other events, 63.2 us)
Sparse Core Ops, SparseCore 0:
  11.0 56.8 all-gather.5
  71.0 53.0 all-gather.7
  127.2 53.1 all-gather.9
  183.2 53.1 all-gather.11
  345.2 54.9 reduce-scatter.15
  403.1 57.0 reduce-scatter.17
  466.1 98.9 reduce-scatter.13
  571.8 97.9 reduce-scatter.11
  675.6 98.0 reduce-scatter.9
  780.3 97.9 reduce-scatter.7
where the time goes:
time: 895 us; the launch traced here: 886 us
  waiting for transfers between devices  527 us (59%)
  local copies, waits for them, and re-layouts  135 us (15%)
  blocking collectives  88.6 us (10%)
  matrix products  82.5 us (9%)
  other arithmetic  19.5 us (2%)
  starting transfers between devices  17.7 us (2%)
  between operations  15.3 us (2%)
    reduce_scatter x1, waiting for transfers between devices, per_device(): lax.psum_scatter(grad_joint[:, 2 * model_width:], ('dp', 'expert'), scatt...  105 us
    reduce_scatter x1, waiting for transfers between devices, per_device(): lax.psum_scatter(grad_joint[:, :model_width], ('dp', 'expert'), scatter_d...  105 us
    reduce_scatter x1, waiting for transfers between devices, per_device(): lax.psum_scatter(grad_joint[:, model_width:2 * model_width], ('dp', 'expe...  104 us
    all_gather x1, waiting for transfers between devices, per_device(): lax.all_gather(value_weight, ('dp', 'expert'), axis=0, tiled=True)  53.7 us
    all_gather x1, blocking collectives, per_device(): lax.all_gather(router_weight, ('dp', 'expert'), axis=0, tiled=True)  50.3 us
    all_gather x1, waiting for transfers between devices, per_device(): lax.all_gather(key_weight, ('dp', 'expert'), axis=0, tiled=True)  49.6 us
    rev x2, local copies, waits for them, and re-layouts, toeplitz(): return skewed[:, ::-1, :col_count]  43.1 us
    all_gather x1, waiting for transfers between devices, per_device(): lax.all_gather(out_weight, ('dp', 'expert'), axis=0, tiled=True)  42.2 us
  transfers between devices with their start and end apart: 14, of which 10 were waited for; matrix products, arithmetic and copies ran while one was open for 24% of the time, Pallas kernels for 0%

commit v1 on v0

v1 whole, which is shorter than its diff:
```python
import functools

import jax
import jax.numpy as jnp
from jax import lax
from jax.experimental import pallas as pl
from jax.experimental.pallas import tpu as pltpu
from jax.sharding import PartitionSpec as P

PRECISE = lax.Precision.HIGHEST
EPSILON = 1e-06
BF = jnp.bfloat16
F32 = jnp.float32
VMEM_BYTES = 56 * 1024 * 1024
GROUP = 256


def mm(a, b):
    return jnp.dot(a, b, preferred_element_type=F32)


def mm_nt(a, b):
    return lax.dot_general(a, b, (((1,), (1,)), ((), ())), preferred_element_type=F32)


def mm_tn(a, b):
    return lax.dot_general(a, b, (((0,), (0,)), ((), ())), preferred_element_type=F32)


def full(shape):
    return pl.BlockSpec(shape, lambda *_: (0,) * len(shape))


def cols(rows, width):
    return pl.BlockSpec((rows, width), lambda g, *_: (0, g))


def shape_of(shape, dtype):
    return jax.ShapeDtypeStruct(shape, dtype)


def params():
    return pltpu.CompilerParams(vmem_limit_bytes=VMEM_BYTES)


def cost(flops, nbytes):
    return pl.CostEstimate(flops=int(flops), bytes_accessed=int(nbytes), transcendentals=0)


def gelu_parts(v):
    square = v * v
    bent = jnp.tanh(0.7978845608 * v * (1.0 + 0.044715 * square))
    half = 0.5 * (1.0 + bent)
    slope = half + 0.5 * v * (1.0 - bent * bent) * (0.7978845608 * (1.0 + 0.134145 * square))
    return v * half, slope


def routed(rows, router, own):
    logits = mm(rows, router)
    exponent = jnp.exp(logits - jnp.max(logits, axis=-1, keepdims=True))
    router_probs = exponent / jnp.sum(exponent, axis=-1, keepdims=True)
    picked = (lax.broadcasted_iota(jnp.int32, logits.shape, 1) == own).astype(F32)
    gate = jnp.sum(router_probs * picked, axis=-1, keepdims=True)
    return router_probs, picked, gate


def route_kernel(room, nz, where_ref, routes_ref, dy_ref, order_ref, slots_t_ref, keep_ref, send_ref, perm_ref):
    tokens = routes_ref.shape[0]
    slots = slots_t_ref.shape[1]
    z, c = where_ref[0], where_ref[1]
    expert = routes_ref[...]
    lanes = lax.broadcasted_iota(jnp.int32, (tokens, 128), 1)
    picked = (lanes == expert).astype(F32)
    lower = (
        lax.broadcasted_iota(jnp.int32, (tokens, tokens), 0)
        >= lax.broadcasted_iota(jnp.int32, (tokens, tokens), 1)
    ).astype(BF)
    counts = mm(lower, picked.astype(BF))
    rank = jnp.sum(picked * (counts - 1.0), axis=1, keepdims=True).astype(jnp.int32)
    to_z, to_c = expert >> 1, expert & 1
    ahead = jnp.where(to_z >= z, to_z - z, to_z - z + nz)
    other = jnp.where(to_c == c, 0, 1)
    slot = (other * nz + ahead) * room + rank
    slots_t = (lax.broadcasted_iota(jnp.int32, (tokens, slots), 1) == slot).astype(F32).astype(BF)
    slots_t_ref[...] = slots_t
    dy_rows = mm_tn(slots_t, dy_ref[...]).astype(BF)
    keep_ref[...] = dy_rows[: slots // 2]
    send_ref[...] = dy_rows[slots // 2 :]
    width = perm_ref.shape[0]
    perm_ref[...] = (
        (lax.broadcasted_iota(jnp.int32, (width, width), 0) == order_ref[...]).astype(F32).astype(BF)
    )


def bias_kernel(along_ref, bias_ref):
    rows = bias_ref.shape[1]
    span = along_ref.shape[2]
    line = jnp.broadcast_to(along_ref[0], (rows, span))
    bias_ref[0] = pltpu.roll(line, span - rows + 1, 1, stride=1, stride_axis=0)[:, :rows]


def fill_x_first(pieces, out_ref):
    half = pieces[0].shape[0]
    for number, piece in enumerate(pieces):
        out_ref[number * half : (number + 1) * half, :] = piece[...]


def fill_y_first(pieces, out_ref):
    half = pieces[0].shape[0]
    part = half // 2
    for side in range(2):
        own, other = pieces[2 * side], pieces[2 * side + 1]
        base = side * 2 * half
        out_ref[base : base + part, :] = own[:part, :]
        out_ref[base + part : base + half, :] = other[:part, :]
        out_ref[base + half : base + half + part, :] = own[part:, :]
        out_ref[base + half + part : base + 2 * half, :] = other[part:, :]


def scores_kernel(head, *refs):
    x_ref, gain_ref, perm_ref, bias_ref = refs[:4]
    wq_refs, wk_refs = refs[4:8], refs[8:12]
    normed_ref, q_ref, k_ref, probs_ref, wq, wk = refs[12:]

    @pl.when(pl.program_id(0) == 0)
    def _():
        x = x_ref[...].astype(F32)
        scale = lax.rsqrt(jnp.mean(x * x, axis=-1, keepdims=True) + EPSILON)
        normed = (x * scale * gain_ref[...]).astype(BF)
        normed_ref[...] = mm(normed, perm_ref[...]).astype(BF)

    fill_x_first(wq_refs, wq)
    fill_y_first(wk_refs, wk)
    normed = normed_ref[...]
    q = mm(normed, wq[...]).astype(BF)
    k = mm(normed, wk[...]).astype(BF)
    q_ref[...] = q
    k_ref[...] = k
    for h in range(q.shape[1] // head):
        part = slice(h * head, (h + 1) * head)
        scores = mm_nt(q[:, part], k[:, part]) + bias_ref[h]
        exponent = jnp.exp(scores - jnp.max(scores, axis=-1, keepdims=True))
        probs_ref[h] = exponent / jnp.sum(exponent, axis=-1, keepdims=True)


def mix_kernel(head, *refs):
    normed_ref, perm_ref, probs_ref, x_ref, gain_ref, slots_t_ref, routes_ref = refs[:7]
    wv_refs, wo_refs = refs[7:11], refs[11:15]
    v_ref, mixed_ref, middle_ref, router_ref, gate_ref, keep_ref, send_ref, wv, wo, mixed = refs[15:]
    step = pl.program_id(0)
    experts = router_ref.shape[1]

    fill_x_first(wv_refs, wv)
    v = mm(normed_ref[...], wv[...]).astype(BF)
    v_ref[...] = v
    width = v.shape[1]
    rows = [
        mm(probs_ref[h].astype(BF), v[:, h * head : (h + 1) * head]) for h in range(width // head)
    ]
    mixed[step] = jnp.concatenate(rows, axis=1).astype(BF)

    @pl.when(step == pl.num_programs(0) - 1)
    def _():
        fill_y_first(wo_refs, wo)
        perm = perm_ref[...]
        every = jnp.concatenate([mixed[g] for g in range(mixed.shape[0])], axis=1)
        mixed_in_order = mm(every, perm).astype(BF)
        mixed_ref[...] = mixed_in_order
        model = x_ref.shape[1]
        middle = x_ref[...].astype(F32) + mm(mixed_in_order, wo[:, :model])
        middle_ref[...] = middle
        scale = lax.rsqrt(jnp.mean(middle * middle, axis=-1, keepdims=True) + EPSILON)
        ffn_in = (middle * scale * gain_ref[...]).astype(BF)
        router = mm(perm, wo[:, model:]).astype(BF)[:, :experts]
        router_ref[...] = router
        gate_ref[...] = routed(ffn_in, router, routes_ref[...])[2]
        rows = mm_tn(slots_t_ref[...], ffn_in).astype(BF)
        half = rows.shape[0] // 2
        keep_ref[...] = rows[:half]
        send_ref[...] = rows[half:]


def expert_kernel(own_ref, rows_ref, dy_ref, router_ref, w1_ref, w2_ref, back_ref, result_ref, router_grad_ref, branch, probs_ref, gate_ref, result, back):
    step = pl.program_id(0)
    rows = rows_ref[...]
    own = own_ref[0]

    @pl.when(step == 0)
    def _():
        router_probs, _, gate = routed(rows, router_ref[...], own)
        probs_ref[...] = router_probs
        gate_ref[...] = gate
        branch[...] = (dy_ref[...].astype(F32) * gate).astype(BF)
        result[...] = jnp.zeros_like(result)
        back[...] = jnp.zeros_like(back)

    w1, w2 = w1_ref[0], w2_ref[0]
    hidden, slope = gelu_parts(mm(rows, w1))
    result[...] += mm(hidden.astype(BF), w2)
    pre_grad = (mm_nt(branch[...], w2) * slope).astype(BF)
    back[...] += mm_nt(pre_grad, w1)

    @pl.when(step == pl.num_programs(0) - 1)
    def _():
        returned = result[...].astype(BF)
        result_ref[...] = returned
        gate_grad = jnp.sum(dy_ref[...].astype(F32) * returned.astype(F32), axis=-1, keepdims=True)
        router_probs, gate = probs_ref[...], gate_ref[...]
        picked = (lax.broadcasted_iota(jnp.int32, router_probs.shape, 1) == own).astype(F32)
        logit_grad = (router_probs * (picked - gate) * gate_grad).astype(BF)
        router_grad_ref[...] = mm_tn(rows, logit_grad)
        back_ref[...] = (back[...] + mm_nt(logit_grad, router_ref[...])).astype(BF)


def expert_grad_kernel(pieces, place_ref, *refs):
    rows_refs, dy_refs = refs[:pieces], refs[pieces : 2 * pieces]
    own_ref, router_ref, w1_ref, w2_ref, g1_ref, g2_ref, rows_all, branch_all, hidden_all, pre_all = refs[2 * pieces :]
    del place_ref
    own = own_ref[0]
    chunk = 256
    base = 0
    for rows_ref, dy_ref in zip(rows_refs, dy_refs, strict=True):

        def body(i, _, rows_ref=rows_ref, dy_ref=dy_ref, base=base):
            here = pl.ds(i * chunk, chunk)
            there = pl.ds(base + i * chunk, chunk)
            rows = rows_ref[here, :]
            gate = routed(rows, router_ref[...], own)[2]
            branch = (dy_ref[here, :].astype(F32) * gate).astype(BF)
            hidden, slope = gelu_parts(mm(rows, w1_ref[0]))
            pre_grad = mm_nt(branch, w2_ref[0]) * slope
            rows_all[there, :] = rows
            branch_all[there, :] = branch
            hidden_all[there, :] = hidden.astype(BF)
            pre_all[there, :] = pre_grad.astype(BF)
            return 0

        lax.fori_loop(0, rows_ref.shape[0] // chunk, body, 0)
        base += rows_ref.shape[0]
    g1_ref[0] = mm_tn(rows_all[...], pre_all[...])
    g2_ref[0] = mm_tn(hidden_all[...], branch_all[...])


def middle_kernel(head, *refs):
    (keep_ref, send_ref, slots_t_ref, dy_ref, middle_ref, gain_ref, mixed_ref, normed_ref, perm_ref, probs_ref) = refs[:10]
    wo_refs = refs[10:14]
    (middle_grad_ref, gain_grad_ref, mixed_grad_ref, value_grad_ref, mine_ref, theirs_ref, wo, mixed_grad) = refs[14:]
    step = pl.program_id(0)
    half = keep_ref.shape[0]
    model = dy_ref.shape[1]

    @pl.when(step == 0)
    def _():
        fill_y_first(wo_refs, wo)
        back = jnp.concatenate([keep_ref[...], send_ref[...]], axis=0)
        ffn_grad = mm(slots_t_ref[...], back)
        middle = middle_ref[...]
        scale = lax.rsqrt(jnp.mean(middle * middle, axis=-1, keepdims=True) + EPSILON)
        gain_grad_ref[...] = jnp.sum(ffn_grad * middle * scale, axis=0, keepdims=True)
        scaled = ffn_grad * gain_ref[...]
        along = jnp.mean(scaled * middle, axis=-1, keepdims=True)
        middle_grad = dy_ref[...].astype(F32) + scale * scaled - middle * (scale * scale * scale * along)
        middle_grad_ref[...] = middle_grad
        attn_grad = middle_grad.astype(BF)
        in_order = mm_nt(attn_grad, wo[...]).astype(BF)
        every = mm_nt(in_order, perm_ref[...]).astype(BF)
        mixed_grad_ref[...] = every
        for g in range(mixed_grad.shape[0]):
            mixed_grad[g] = every[:, g * GROUP : (g + 1) * GROUP]
        out_grad = mm_tn(mixed_ref[...], attn_grad)
        own = out_grad.shape[0] // 2
        mine_ref[1] = out_grad[:own]
        theirs_ref[1] = out_grad[own:].astype(BF)

    grads = mixed_grad[step]
    parts = [
        mm_tn(probs_ref[h].astype(BF), grads[:, h * head : (h + 1) * head]) for h in range(GROUP // head)
    ]
    value_grad = jnp.concatenate(parts, axis=1).astype(BF)
    value_grad_ref[...] = value_grad
    weight_grad = mm_tn(normed_ref[...], value_grad)
    own = weight_grad.shape[0] // 2
    at = pl.ds(pl.multiple_of(step * GROUP, GROUP), GROUP)
    mine_ref[0, :, at] = weight_grad[:own]
    theirs_ref[0, :, at] = weight_grad[own:].astype(BF)


def score_grad_kernel(head, mixed_grad_ref, v_ref, q_ref, k_ref, probs_ref, normed_ref, dq_ref, dk_ref, along_ref, mine_ref, theirs_ref):
    rows = q_ref.shape[0]
    flip = (
        lax.broadcasted_iota(jnp.int32, (rows, rows), 0) + lax.broadcasted_iota(jnp.int32, (rows, rows), 1)
        == rows - 1
    ).astype(F32).astype(BF)
    q_parts, k_parts = [], []
    for h in range(GROUP // head):
        part = slice(h * head, (h + 1) * head)
        probs = probs_ref[h]
        prob_grad = mm_nt(mixed_grad_ref[:, part], v_ref[:, part])
        inner = jnp.sum(probs * prob_grad, axis=-1, keepdims=True)
        score_grad = (probs * (prob_grad - inner)).astype(BF)
        q_parts.append(mm(score_grad, k_ref[:, part]))
        k_parts.append(mm_tn(score_grad, q_ref[:, part]))
        flipped = mm(flip, score_grad)
        wide = jnp.concatenate([flipped, jnp.zeros_like(flipped)], axis=1)
        along_ref[h] = jnp.sum(pltpu.roll(wide, 0, 1, stride=1, stride_axis=0), axis=0, keepdims=True)
    dq = jnp.concatenate(q_parts, axis=1).astype(BF)
    dk = jnp.concatenate(k_parts, axis=1).astype(BF)
    dq_ref[...] = dq
    dk_ref[...] = dk
    normed = normed_ref[...]
    for number, grad in enumerate((dq, dk)):
        weight_grad = mm_tn(normed, grad)
        own = weight_grad.shape[0] // 2
        mine_ref[number] = weight_grad[:own]
        theirs_ref[number] = weight_grad[own:].astype(BF)


def input_kernel(*refs):
    dq_ref, dk_ref, dv_ref, x_ref, gain_ref, perm_ref, middle_grad_ref = refs[:7]
    wq_refs, wk_refs, wv_refs = refs[7:11], refs[11:15], refs[15:19]
    input_grad_ref, gain_grad_ref, weight = refs[19:]
    fill_x_first(wq_refs, weight)
    total = mm_nt(dq_ref[...], weight[...])
    fill_y_first(wk_refs, weight)
    total += mm_nt(dk_ref[...], weight[...])
    fill_x_first(wv_refs, weight)
    total += mm_nt(dv_ref[...], weight[...])
    perm = perm_ref[...]
    high = total.astype(BF)
    low = (total - high.astype(F32)).astype(BF)
    normed_grad = mm_nt(high, perm) + mm_nt(low, perm)
    x = x_ref[...].astype(F32)
    scale = lax.rsqrt(jnp.mean(x * x, axis=-1, keepdims=True) + EPSILON)
    gain_grad_ref[...] = jnp.sum(normed_grad * x * scale, axis=0, keepdims=True)
    scaled = normed_grad * gain_ref[...]
    along = jnp.mean(scaled * x, axis=-1, keepdims=True)
    input_grad_ref[...] = middle_grad_ref[...] + scale * scaled - x * (scale * scale * scale * along)


class Places:
    def __init__(self):
        self.experts = lax.axis_size("expert")
        self.nz = self.experts // 2
        self.dp = lax.axis_size("dp")
        self.near = self.nz <= 4
        me = lax.axis_index("expert")
        self.z, self.c = me // 2, me % 2
        self.row = lax.axis_index("dp")
        self.columns = [[2 * z + c for z in range(self.nz)] for c in range(2)]

    def core(self, v):
        return lax.ppermute(v, "expert", [(i, i ^ 1) for i in range(self.experts)])

    def x(self, v):
        return lax.ppermute(v, "dp", [(i, i ^ 1) for i in range(self.dp)])

    def y(self, v):
        return lax.ppermute(v, "dp", [(i, i ^ 2) for i in range(self.dp)])

    def shift(self, v, k):
        size = self.experts
        return lax.ppermute(v, "expert", [(i, (i + 2 * k) % size) for i in range(size)])

    def shifts(self):
        middle = self.nz // 2
        return [middle] + [k for k in range(1, self.nz) if k != middle]

    def gather_z(self, v):
        if self.near:
            got = {k: self.shift(v, k) for k in self.shifts()}
            return jnp.concatenate([v] + [got[k] for k in range(1, self.nz)], axis=0)
        return lax.all_gather(v, "expert", axis=0, tiled=True, axis_index_groups=self.columns)

    def z_order(self):
        steps = jnp.arange(self.nz, dtype=jnp.int32)
        return (self.z - steps) % self.nz if self.near else steps

    def scatter_z(self, v):
        if self.near:
            size = v.shape[0] // self.nz
            total = v[:size]
            low = v.astype(BF)
            for k in self.shifts():
                total = total + self.shift(low[k * size : (k + 1) * size], -k).astype(F32)
            return total
        blocks = v.astype(BF).reshape(self.nz, v.shape[0] // self.nz, v.shape[1])
        got = lax.all_to_all(
            blocks, "expert", split_axis=0, concat_axis=0, tiled=True, axis_index_groups=self.columns
        )
        return jnp.sum(got.astype(F32), axis=0)

    def send_out(self, keep, send):
        got = self.core(send)
        room = keep.shape[0] // self.nz
        both = jnp.concatenate(
            [v.reshape(self.nz, room, keep.shape[1]) for v in (keep, got)], axis=1
        )
        if self.near:
            moved = {k: self.shift(both[k], k) for k in self.shifts()}
            return jnp.concatenate([both[0]] + [moved[k] for k in range(1, self.nz)], axis=0)
        placed = jnp.roll(both, self.z, axis=0)
        moved = lax.all_to_all(
            placed, "expert", split_axis=0, concat_axis=0, tiled=True, axis_index_groups=self.columns
        )
        return moved.reshape(-1, keep.shape[1])

    def send_home(self, rows):
        blocks = rows.reshape(self.nz, rows.shape[0] // self.nz, rows.shape[1])
        if self.near:
            moved = {k: self.shift(blocks[k], -k) for k in self.shifts()}
            both = jnp.stack([blocks[0]] + [moved[k] for k in range(1, self.nz)], axis=0)
        else:
            moved = lax.all_to_all(
                blocks, "expert", split_axis=0, concat_axis=0, tiled=True, axis_index_groups=self.columns
            )
            both = jnp.roll(moved, -self.z, axis=0)
        room = both.shape[1] // 2
        keep, other = both[:, :room].reshape(-1, rows.shape[1]), both[:, room:].reshape(-1, rows.shape[1])
        return keep, self.core(other)

    def gather_two(self, first, second):
        width = first.shape[1]
        line = self.gather_z(jnp.concatenate([first, second], axis=1))
        a, b = line[:, :width], line[:, width:]
        ax, by = self.x(a), self.y(b)
        a2, b2 = jnp.concatenate([a, ax], axis=0), jnp.concatenate([b, by], axis=0)
        a3, b3 = self.y(a2), self.x(b2)
        return (a2, a3, self.core(a2), self.core(a3)), (b2, b3, self.core(b2), self.core(b3))

    def scatter_two(self, mine, theirs):
        total = mine + self.core(theirs).astype(F32)
        half = total.shape[1] // 2
        quarter = half // 2
        low = total.astype(BF)
        a = total[0, :half] + self.y(low[0, half:]).astype(F32)
        b_low = low[1].reshape(2, 2, quarter, -1)
        b = total[1].reshape(2, 2, quarter, -1)[:, 0] + self.x(b_low[:, 1]).astype(F32)
        a = a[:quarter] + self.x(a[quarter:].astype(BF)).astype(F32)
        b = b[0] + self.y(b[1].astype(BF)).astype(F32)
        both = self.scatter_z(jnp.concatenate([a, b], axis=1))
        return both[:, : a.shape[1]], both[:, a.shape[1] :]

    def gather_rows(self, v):
        half = v.shape[0] // 2
        a, b = v[:half], v[half:]
        ax, by = self.x(a), self.y(b)
        return [v, ax, by, self.y(jnp.concatenate([a, ax], axis=0)), self.x(jnp.concatenate([b, by], axis=0))]

    def sum_small(self, v):
        v = v + self.core(v)
        v = v + self.x(v)
        v = v + self.y(v)
        if not self.near:
            return lax.psum(v, "expert", axis_index_groups=self.columns)
        got = [self.shift(v, k) for k in self.shifts()]
        parts = jnp.stack([v] + [got[self.shifts().index(k)] for k in range(1, self.nz)], axis=0)
        parts = jnp.roll(parts[::-1], self.z + 1, axis=0)
        return jnp.sum(parts, axis=0)


def per_device(
    tokens,
    cotangent,
    routes,
    buckets,
    norm_attn,
    norm_ffn,
    rel_table,
    query_weight,
    key_weight,
    value_weight,
    out_weight,
    router_weight,
    expert_in,
    expert_out,
):
    at = Places()
    rows, model = tokens.shape
    head_count = rel_table.shape[1]
    head = model // head_count
    bucket_count = rel_table.shape[0]
    experts = router_weight.shape[1]
    shard = query_weight.shape[0]
    nz = at.nz
    room = max(2, 2 * rows // at.experts)
    slots = experts * room
    half = slots // 2
    groups = model // GROUP
    per_group = GROUP // head
    hidden = expert_in.shape[2]
    gain_attn, gain_ffn = norm_attn.reshape(1, model), norm_ffn.reshape(1, model)
    own = lax.axis_index("expert").astype(jnp.int32).reshape(1)
    smem = pl.BlockSpec(memory_space=pltpu.SMEM)

    core_of = at.c ^ jnp.arange(2, dtype=jnp.int32)
    row_of = at.row ^ jnp.arange(4, dtype=jnp.int32)
    device_of = (
        row_of[None, :, None] * at.experts + at.z_order()[None, None, :] * 2 + core_of[:, None, None]
    )
    order = (
        device_of[..., None] * shard + jnp.arange(shard, dtype=jnp.int32)
    ).reshape(1, model).astype(jnp.int32)

    qk_pieces = at.gather_two(query_weight, key_weight)
    padded_router = jnp.pad(router_weight, ((0, 0), (0, 128 - experts)))
    vo_pieces = at.gather_two(
        value_weight, jnp.concatenate([out_weight, padded_router], axis=1)
    )
    wq, wk = qk_pieces
    wv, wo = vo_pieces

    slots_t, dy_keep, dy_send, perm = pl.pallas_call(
        functools.partial(route_kernel, room, nz),
        out_shape=(
            shape_of((rows, slots), BF),
            shape_of((half, model), BF),
            shape_of((half, model), BF),
            shape_of((model, model), BF),
        ),
        in_specs=[smem] + [pl.BlockSpec(memory_space=pltpu.VMEM)] * 3,
        compiler_params=params(),
        cost_estimate=cost(2 * rows * slots * model, 4 * rows * model),
        name="route",
    )(jnp.stack([at.z, at.c]).astype(jnp.int32), routes, cotangent, order)
    dy_rows = at.send_out(dy_keep, dy_send)

    onehot_bucket = (buckets[:, None] == jnp.arange(bucket_count, dtype=jnp.int32)[None, :]).astype(F32)
    along = jnp.pad(jnp.dot(onehot_bucket, rel_table, precision=PRECISE).T, ((0, 0), (0, 1)))
    span = along.shape[1]
    bias = pl.pallas_call(
        bias_kernel,
        grid=(head_count,),
        out_shape=shape_of((head_count, rows, rows), F32),
        in_specs=[pl.BlockSpec((1, 1, span), lambda g: (g, 0, 0))],
        out_specs=pl.BlockSpec((1, rows, rows), lambda g: (g, 0, 0)),
        compiler_params=params(),
        cost_estimate=cost(1 << 20, 4 * head_count * rows * rows),
        name="bias",
    )(along.reshape(head_count, 1, span))

    quarter = wq[0].shape[0]
    head_block = pl.BlockSpec((per_group, rows, rows), lambda g: (g, 0, 0))
    normed, q, k, probs = pl.pallas_call(
        functools.partial(scores_kernel, head),
        grid=(groups,),
        out_shape=(
            shape_of((rows, model), BF),
            shape_of((rows, model), BF),
            shape_of((rows, model), BF),
            shape_of((head_count, rows, rows), F32),
        ),
        in_specs=[full((rows, model)), full((1, model)), full((model, model)), head_block]
        + [cols(quarter, GROUP)] * 8,
        out_specs=(full((rows, model)), cols(rows, GROUP), cols(rows, GROUP), head_block),
        scratch_shapes=[pltpu.VMEM((model, GROUP), BF), pltpu.VMEM((model, GROUP), BF)],
        compiler_params=params(),
        cost_estimate=cost(6 * rows * model * model, 12 * model * model),
        name="scores",
    )(tokens, gain_attn, perm, bias, *wq, *wk)

    wide = wo[0].shape[1]
    v, mixed, middle, router, gate, keep, send = pl.pallas_call(
        functools.partial(mix_kernel, head),
        grid=(groups,),
        out_shape=(
            shape_of((rows, model), BF),
            shape_of((rows, model), BF),
            shape_of((rows, model), F32),
            shape_of((model, experts), BF),
            shape_of((rows, 1), F32),
            shape_of((half, model), BF),
            shape_of((half, model), BF),
        ),
        in_specs=[
            full((rows, model)),
            full((model, model)),
            head_block,
            full((rows, model)),
            full((1, model)),
            full((rows, slots)),
            full((rows, 1)),
        ]
        + [cols(quarter, GROUP)] * 4
        + [full((quarter, wide))] * 4,
        out_specs=(
            cols(rows, GROUP),
            full((rows, model)),
            full((rows, model)),
            full((model, experts)),
            full((rows, 1)),
            full((half, model)),
            full((half, model)),
        ),
        scratch_shapes=[
            pltpu.VMEM((model, GROUP), BF),
            pltpu.VMEM((model, wide), BF),
            pltpu.VMEM((groups, rows, GROUP), BF),
        ],
        compiler_params=params(),
        cost_estimate=cost(8 * rows * model * model, 12 * model * model),
        name="mix",
    )(normed, perm, probs, tokens, gain_ffn, slots_t, routes, *wv, *wo)

    rows_all = at.send_out(keep, send)
    part = 512
    back, returned, router_grad = pl.pallas_call(
        expert_kernel,
        grid=(hidden // part,),
        out_shape=(
            shape_of((slots, model), BF),
            shape_of((slots, model), BF),
            shape_of((model, experts), F32),
        ),
        in_specs=[
            smem,
            full((slots, model)),
            full((slots, model)),
            full((model, experts)),
            pl.BlockSpec((1, model, part), lambda f: (0, 0, f)),
            pl.BlockSpec((1, part, model), lambda f: (0, f, 0)),
        ],
        out_specs=(full((slots, model)), full((slots, model)), full((model, experts))),
        scratch_shapes=[
            pltpu.VMEM((slots, model), BF),
            pltpu.VMEM((slots, experts), F32),
            pltpu.VMEM((slots, 1), F32),
            pltpu.VMEM((slots, model), F32),
            pltpu.VMEM((slots, model), F32),
        ],
        compiler_params=params(),
        cost_estimate=cost(8 * slots * model * hidden, 4 * model * hidden),
        name="expert",
    )(own, rows_all, dy_rows, router, expert_in, expert_out)

    back_keep, back_send = at.send_home(back)
    returned_keep, returned_send = at.send_home(returned)
    rows_dp = at.gather_rows(rows_all)
    dy_dp = at.gather_rows(dy_rows)
    every = sum(v.shape[0] for v in rows_dp)
    slice_width = hidden // at.dp
    grad_in, grad_out_w = pl.pallas_call(
        functools.partial(expert_grad_kernel, len(rows_dp)),
        grid_spec=pltpu.PrefetchScalarGridSpec(
            num_scalar_prefetch=1,
            grid=(1,),
            in_specs=[full(v.shape) for v in rows_dp]
            + [full(v.shape) for v in dy_dp]
            + [
                smem,
                full((model, experts)),
                pl.BlockSpec((1, model, slice_width), lambda g, place: (0, 0, place[0])),
                pl.BlockSpec((1, slice_width, model), lambda g, place: (0, place[0], 0)),
            ],
            out_specs=(full((1, model, slice_width)), full((1, slice_width, model))),
            scratch_shapes=[
                pltpu.VMEM((every, model), BF),
                pltpu.VMEM((every, model), BF),
                pltpu.VMEM((every, slice_width), BF),
                pltpu.VMEM((every, slice_width), BF),
            ],
        ),
        out_shape=(shape_of((1, model, slice_width), F32), shape_of((1, slice_width, model), F32)),
        compiler_params=params(),
        cost_estimate=cost(8 * every * model * slice_width, 20 * model * slice_width),
        name="expert_grads",
    )(at.row.astype(jnp.int32).reshape(1), *rows_dp, *dy_dp, own, router, expert_in, expert_out)

    pair = model // 2
    middle_grad, gain_ffn_grad, mixed_grad, value_grad, vo_mine, vo_theirs = pl.pallas_call(
        functools.partial(middle_kernel, head),
        grid=(groups,),
        out_shape=(
            shape_of((rows, model), F32),
            shape_of((1, model), F32),
            shape_of((rows, model), BF),
            shape_of((rows, model), BF),
            shape_of((2, pair, model), F32),
            shape_of((2, pair, model), BF),
        ),
        in_specs=[
            full((half, model)),
            full((half, model)),
            full((rows, slots)),
            full((rows, model)),
            full((rows, model)),
            full((1, model)),
            full((rows, model)),
            full((rows, model)),
            full((model, model)),
            head_block,
        ]
        + [pl.BlockSpec((quarter, model), lambda g: (0, 0))] * 4,
        out_specs=(
            full((rows, model)),
            full((1, model)),
            full((rows, model)),
            cols(rows, GROUP),
            full((2, pair, model)),
            full((2, pair, model)),
        ),
        scratch_shapes=[pltpu.VMEM((model, model), BF), pltpu.VMEM((groups, rows, GROUP), BF)],
        compiler_params=params(),
        cost_estimate=cost(10 * rows * model * model, 12 * model * model),
        name="middle",
    )(back_keep, back_send, slots_t, cotangent, middle, gain_ffn, mixed, normed, perm, probs, *wo)
    grad_value, grad_proj = at.scatter_two(vo_mine, vo_theirs)

    dq, dk, along_grad, qk_mine, qk_theirs = pl.pallas_call(
        functools.partial(score_grad_kernel, head),
        grid=(groups,),
        out_shape=(
            shape_of((rows, model), BF),
            shape_of((rows, model), BF),
            shape_of((head_count, 1, span), F32),
            shape_of((2, pair, model), F32),
            shape_of((2, pair, model), BF),
        ),
        in_specs=[cols(rows, GROUP)] * 4 + [head_block, full((rows, model))],
        out_specs=(
            cols(rows, GROUP),
            cols(rows, GROUP),
            pl.BlockSpec((per_group, 1, span), lambda g: (g, 0, 0)),
            pl.BlockSpec((2, pair, GROUP), lambda g: (0, 0, g)),
            pl.BlockSpec((2, pair, GROUP), lambda g: (0, 0, g)),
        ),
        compiler_params=params(),
        cost_estimate=cost(8 * rows * model * model, 12 * model * model),
        name="score_grads",
    )(mixed_grad, v, q, k, probs, normed)
    grad_query, grad_key = at.scatter_two(qk_mine, qk_theirs)

    input_grad, gain_attn_grad = pl.pallas_call(
        input_kernel,
        grid=(1,),
        out_shape=(shape_of((rows, model), F32), shape_of((1, model), F32)),
        in_specs=[full((rows, model))] * 4
        + [full((1, model)), full((model, model)), full((rows, model))]
        + [full((quarter, model))] * 8
        + [pl.BlockSpec((quarter, model), lambda g: (0, 0))] * 4,
        out_specs=(full((rows, model)), full((1, model))),
        scratch_shapes=[pltpu.VMEM((model, model), BF)],
        compiler_params=params(),
        cost_estimate=cost(10 * rows * model * model, 12 * model * model),
        name="inputs",
    )(dq, dk, value_grad, tokens, gain_attn, perm, middle_grad, *wq, *wk, *wv)

    rel_grad = jnp.dot(along_grad[:, 0, : span - 1], onehot_bucket, precision=PRECISE).T
    small = [gain_attn_grad, gain_ffn_grad, rel_grad, router_grad]
    flat = jnp.concatenate([v.reshape(-1) for v in small])
    summed = at.sum_small(jnp.pad(flat, (0, -flat.shape[0] % 1024)).reshape(-1, 128)).reshape(-1)
    outs, base = [], 0
    for v in small:
        outs.append(summed[base : base + v.size].reshape(v.shape))
        base += v.size
    device = at.row * at.experts + lax.axis_index("expert")
    grad_router = lax.dynamic_slice_in_dim(outs[3], device * shard, shard, axis=0)

    expert_result = mm(slots_t, jnp.concatenate([returned_keep, returned_send], axis=0))
    output = (middle + gate * expert_result).astype(BF)
    return (
        output,
        input_grad,
        outs[0].reshape(model),
        outs[1].reshape(model),
        outs[2],
        grad_query,
        grad_key,
        grad_value,
        grad_proj,
        grad_router,
        grad_in,
        grad_out_w,
    )


def solution(mesh):
    in_specs = (
        P(("dp", "expert"), None),
        P(("dp", "expert"), None),
        P(("dp", "expert"), None),
        P(),
        P(),
        P(),
        P(),
        P(("dp", "expert"), None),
        P(("dp", "expert"), None),
        P(("dp", "expert"), None),
        P(("dp", "expert"), None),
        P(("dp", "expert"), None),
        P("expert", None, None),
        P("expert", None, None),
    )
    out_specs = (
        P(("dp", "expert"), None),
        P(("dp", "expert"), None),
        P(),
        P(),
        P(),
        P(("dp", "expert"), None),
        P(("dp", "expert"), None),
        P(("dp", "expert"), None),
        P(("dp", "expert"), None),
        P(("dp", "expert"), None),
        P("expert", None, "dp"),
        P("expert", "dp", None),
    )
    return jax.shard_map(
        per_device, mesh=mesh, in_specs=in_specs, out_specs=out_specs, check_vma=False
    )
```

time: 895 us -> 310 us (0.35)
  waiting for transfers between devices: 527 us -> 95 us
  local copies, waits for them, and re-layouts: 135 us -> 17 us
  Pallas kernels: 0 us -> 88.7 us
  blocking collectives: 88.6 us -> 0 us
  matrix products: 82.5 us -> 2.8 us
  starting transfers between devices: 17.7 us -> 95.2 us
  between operations: 15.3 us -> 1.46 us
  other arithmetic: 19.5 us -> 9 us
    reduce_scatter x6 -> x0, waiting for transfers between devices: 334 us -> none  [the longest x1 105 us: per_device(): lax.psum_scatter(grad_joint[:, 2 * model_width:], ('dp', 'expert'), scatt...]
    all_gather x4 -> x0, waiting for transfers between devices: 146 us -> none  [the longest x1 53.7 us: per_device(): lax.all_gather(value_weight, ('dp', 'expert'), axis=0, tiled=True)]
    ppermute x0 -> x68, starting transfers between devices: none -> 95.2 us  [the longest x27 58.7 us: shift(): lax.ppermute(v, 'expert', [(i, (i + 2 * k) % size) for i in range(size)])]
    ppermute x0 -> x68, waiting for transfers between devices: none -> 95 us  [the longest x27 52.1 us: shift(): lax.ppermute(v, 'expert', [(i, (i + 2 * k) % size) for i in range(size)])]
    pallas_call x0 -> x9, Pallas kernels: none -> 88.7 us  [the longest x1 18.8 us: per_device(): pl.pallas_call(functools.partial(expert_grad_kernel, len(rows_dp)), grid_...]
    dot_general x27 -> x3, matrix products: 82.5 us -> 2.8 us  [the longest x1 2.13 us: mm(): return jnp.dot(a, b, preferred_element_type=F32)]
    all_gather x1 -> x0, blocking collectives: 50.3 us -> none  [per_device(): lax.all_gather(router_weight, ('dp', 'expert'), axis=0, tiled=True)]
    rev x2 -> x1, local copies, waits for them, and re-layouts: 43.1 us -> 0.01 us  [sum_small(): parts = jnp.roll(parts[::-1], self.z + 1, axis=0)]
  transfers between devices with their start and end apart: 14 -> 68, of which waited for: 10 -> 28; matrix products, arithmetic and copies ran while one was open for 24% -> 6% of each run, Pallas kernels for 0% -> 15%
where the time goes in v1:
time: 310 us; the launch traced here: 309 us
  starting transfers between devices  95.2 us (31%)
  waiting for transfers between devices  95 us (31%)
  Pallas kernels  88.7 us (29%)
  local copies, waits for them, and re-layouts  17 us (5%)
  other arithmetic  9 us (3%)
    ppermute x27, starting transfers between devices, shift(): lax.ppermute(v, 'expert', [(i, (i + 2 * k) % size) for i in range(size)])  58.7 us
    ppermute x27, waiting for transfers between devices, shift(): lax.ppermute(v, 'expert', [(i, (i + 2 * k) % size) for i in range(size)])  52.1 us
    ppermute x13, waiting for transfers between devices, y(): return lax.ppermute(v, 'dp', [(i, i ^ 2) for i in range(self.dp)])  24.8 us
    pallas_call x1, Pallas kernels, per_device(): pl.pallas_call(functools.partial(expert_grad_kernel, len(rows_dp)), grid_...  18.8 us
    ppermute x13, waiting for transfers between devices, x(): return lax.ppermute(v, 'dp', [(i, i ^ 1) for i in range(self.dp)])  18 us
    pallas_call x1, Pallas kernels, per_device(): pl.pallas_call(expert_kernel, grid=(hidden // part,), out_shape=(shape_of...  17.6 us
    ppermute x13, starting transfers between devices, x(): return lax.ppermute(v, 'dp', [(i, i ^ 1) for i in range(self.dp)])  17.2 us
    ppermute x13, starting transfers between devices, y(): return lax.ppermute(v, 'dp', [(i, i ^ 2) for i in range(self.dp)])  16.1 us
  transfers between devices with their start and end apart: 68, of which 28 were waited for; matrix products, arithmetic and copies ran while one was open for 6% of the time, Pallas kernels for 15%

profile of v1, /device:TPU:0, one launch (start us, length us, event | category | flops | bytes accessed | tf_op | source)
XLA Modules:
  0.0 309.1 jit_solution(14970783188539847261)
XLA Ops:
  2.2 5.0 %collective-permute-start.2 = (bf16[24,1536]{1,0:T(8,128)(2,1)S(1)}, bf16[24,1536]{1,0:T(8,128)(2,1)S(1)}, u32[]{:S(2)}, u32[]{:S(2)}) collective-permute-start(bf16[24,1536]{1,0:T(8,128)(2,1)S(1)} %constant_dynamic-update-slice_fusion), channel_id=1, source_target_pairs={{0,6},{1,7},{2,0},{3,1},{4,2},{5,3},{6,4},{7,5},{8,14},{9,15},{10,... | collective-permute-start | bytes 221192 | tf_op jit(solution)/shard_map/ppermute | solution.py:362
  9.9 2.8 collective-permute-start.13
  18.2 3.0 collective-permute-done.12
  32.4 3.5 %collective-permute-done.4.refs_5_.refs_8_ = bf16[192,768]{1,0:T(8,128)(2,1)S(1)} collective-permute-done((bf16[192,768]{1,0:T(8,128)(2,1)S(1)}, bf16[192,768]{1,0:T(8,128)(2,1)S(1)}, u32[]{:S(2)}, u32[]{:S(2)}) %collective-permute-start.4) | collective-permute-done | bytes 294944 | tf_op jit(solution)/shard_map/ppermute | solution.py:358
  37.0 4.4 %collective-permute-done.15.refs_8_.refs_16_ = bf16[192,768]{1,0:T(8,128)(2,1)} collective-permute-done((bf16[192,768]{1,0:T(8,128)(2,1)S(1)}, bf16[192,768]{1,0:T(8,128)(2,1)}, u32[]{:S(2)}, u32[]{:S(2)}) %collective-permute-start.15) | collective-permute-done | bytes 294944 | tf_op jit(solution)/shard_map/ppermute | solution.py:358
  45.9 7.0 %bias.1.refs_3_ = f32[12,256,256]{2,1,0:T(8,128)} custom-call(f32[12,1,512]{2,1,0:T(1,128)} %reshape.196.along_ref), custom_call_target="tpu_custom_call" | custom-call | flops 1048576 | bytes 3145728 | tf_op jit(solution)/shard_map/bias/pallas_call | solution.py:530
  53.6 3.2 %route.1 = (bf16[256,512]{1,0:T(8,128)(2,1)}, bf16[256,768]{1,0:T(8,128)(2,1)}, bf16[256,768]{1,0:T(8,128)(2,1)}, bf16[768,768]{1,0:T(8,128)(2,1)}) custom-call(s32[2]{0:T(128)} %pad_add_fusion.where_ref, s32[256,1]{1,0:T(8,128)} %copy.43.routes_ref.refs_6_, bf16[256,768]{1,0:T(8,128)(2,1)} %refs_3_.4, s32[1,768]{1,0:T(1,128)} %add.169.order_ref), custom_call_target="tpu_custom_call" | custom-call | flops 201326592 | bytes 786432 | tf_op jit(solution)/shard_map/route/pallas_call | solution.py:512
  56.8 7.8 %scores.1 = (bf16[256,768]{1,0:T(8,128)(2,1)}, bf16[256,768]{1,0:T(8,128)(2,1)}, bf16[256,768]{1,0:T(8,128)(2,1)}, f32[12,256,256]{2,1,0:T(8,128)}) custom-call(bf16[256,768]{1,0:T(8,128)(2,1)} %refs_3_.5, f32[1,768]{1,0:T(1,128)} %reshape.195.refs_1_.refs_4_, bf16[768,768]{1,0:T(8,128)(2,1)} %get-tuple-element.45.refs_2_.refs_1_.refs_8_.refs_5_, ...), custom_call_target="tpu_custom_call" | custom-call | flops 905969664 | bytes 7077888 | tf_op jit(solution)/shard_map/scores/pallas_call | solution.py:543
  65.6 9.1 %mix.1 = (bf16[256,768]{1,0:T(8,128)(2,1)}, bf16[256,768]{1,0:T(8,128)(2,1)}, f32[256,768]{1,0:T(8,128)}, bf16[768,8]{1,0:T(8,128)(2,1)}, f32[256,1]{1,0:T(8,128...) custom-call(bf16[256,768]{1,0:T(8,128)(2,1)} %get-tuple-element.46.refs_0_.refs_7_.normed_ref, ...), custom_call_target="tpu_custom_call" | custom-call | flops 1207959552 | bytes 7077888 | tf_op jit(solution)/shard_map/mix/pallas_call | solution.py:562
  81.4 3.5 %collective-permute-done.27 = bf16[128,768]{1,0:T(8,128)(2,1)S(1)} collective-permute-done((bf16[128,768]{1,0:T(8,128)(2,1)S(1)}, bf16[128,768]{1,0:T(8,128)(2,1)S(1)}, u32[]{:S(2)}, u32[]{:S(2)}) %collective-permute-start.27) | collective-permute-done | bytes 196640 | tf_op jit(solution)/shard_map/ppermute | solution.py:362
  86.4 5.5 %collective-permute-start.25 = (bf16[128,768]{1,0:T(8,128)(2,1)S(1)}, bf16[128,768]{1,0:T(8,128)(2,1)S(1)}, u32[]{:S(2)}, u32[]{:S(2)}) collective-permute-start(bf16[128,768]{1,0:T(8,128)(2,1)S(1)} %get-tuple-element.124), channel_id=1, source_target_pairs={{0,6},{1,7},{2,0},{3,1},{4,2},{5,3},{6,4},{7,5},{8,14},{9,15},{10,... | collective-permute-start | bytes 589832 | tf_op jit(solution)/shard_map/ppermute | solution.py:362
  91.8 5.1 %collective-permute-start.24 = (bf16[128,768]{1,0:T(8,128)(2,1)S(1)}, bf16[128,768]{1,0:T(8,128)(2,1)S(1)}, u32[]{:S(2)}, u32[]{:S(2)}) collective-permute-start(bf16[128,768]{1,0:T(8,128)(2,1)S(1)} %get-tuple-element.125), channel_id=1, source_target_pairs={{0,4},{1,5},{2,6},{3,7},{4,0},{5,1},{6,2},{7,3},{8,12},{9,13},{10,... | collective-permute-start | bytes 589832 | tf_op jit(solution)/shard_map/ppermute | solution.py:362
  96.9 6.2 %collective-permute-done.28 = bf16[128,768]{1,0:T(8,128)(2,1)S(1)} collective-permute-done((bf16[128,768]{1,0:T(8,128)(2,1)S(1)}, bf16[128,768]{1,0:T(8,128)(2,1)S(1)}, u32[]{:S(2)}, u32[]{:S(2)}) %collective-permute-start.28) | collective-permute-done | bytes 196640 | tf_op jit(solution)/shard_map/ppermute | solution.py:362
  104.8 3.5 %collective-permute-start.60 = (bf16[256,768]{1,0:T(8,128)(2,1)S(1)}, bf16[256,768]{1,0:T(8,128)(2,1)S(1)}, u32[]{:S(2)}, u32[]{:S(2)}) collective-permute-start(bf16[256,768]{1,0:T(8,128)(2,1)S(1)} %pad_maximum_fusion.12), channel_id=1, source_target_pairs={{0,8},{8,0},{16,24},{24,16},{1,9},{9,1},{17,25},{25,17},{2,10},{10... | collective-permute-start | bytes 1179656 | tf_op jit(solution)/shard_map/ppermute | solution.py:355
  108.3 5.2 %collective-permute-done.24 = bf16[128,768]{1,0:T(8,128)(2,1)S(1)} collective-permute-done((bf16[128,768]{1,0:T(8,128)(2,1)S(1)}, bf16[128,768]{1,0:T(8,128)(2,1)S(1)}, u32[]{:S(2)}, u32[]{:S(2)}) %collective-permute-start.24) | collective-permute-done | bytes 196640 | tf_op jit(solution)/shard_map/ppermute | solution.py:362
  116.4 8.3 %collective-permute-done.61.refs_2_ = bf16[256,768]{1,0:T(8,128)(2,1)S(1)} collective-permute-done((bf16[256,768]{1,0:T(8,128)(2,1)S(1)}, bf16[256,768]{1,0:T(8,128)(2,1)S(1)}, u32[]{:S(2)}, u32[]{:S(2)}) %collective-permute-start.61) | collective-permute-done | bytes 393248 | tf_op jit(solution)/shard_map/ppermute | solution.py:358
  126.2 17.6 %expert.1 = (bf16[512,768]{1,0:T(8,128)(2,1)}, bf16[512,768]{1,0:T(8,128)(2,1)}, f32[768,8]{1,0:T(8,128)}) custom-call(s32[1]{0:T(128)} %bitcast.3.own_ref.refs_10_, bf16[512,768]{1,0:T(8,128)(2,1)} %get-tuple-element.130.rows_ref.refs_0_, bf16[512,768]{1,0:T(8,128)(2,1)} %get-tuple-element.127.dy_ref.refs_5_, ...), custom_call_target="tpu_custom_call" | custom-call | flops 9663676416 | bytes 9437184 | tf_op jit(solution)/shard_map/expert/pallas_call | solution.py:606
  149.0 5.9 %collective-permute-done.36 = bf16[128,768]{1,0:T(8,128)(2,1)S(1)} collective-permute-done((bf16[128,768]{1,0:T(8,128)(2,1)S(1)}, bf16[128,768]{1,0:T(8,128)(2,1)S(1)}, u32[]{:S(2)}, u32[]{:S(2)}) %collective-permute-start.36) | collective-permute-done | bytes 196640 | tf_op jit(solution)/shard_map/ppermute | solution.py:362
  154.9 6.7 %collective-permute-done.35 = bf16[128,768]{1,0:T(8,128)(2,1)S(1)} collective-permute-done((bf16[128,768]{1,0:T(8,128)(2,1)S(1)}, bf16[128,768]{1,0:T(8,128)(2,1)S(1)}, u32[]{:S(2)}, u32[]{:S(2)}) %collective-permute-start.35) | collective-permute-done | bytes 196640 | tf_op jit(solution)/shard_map/ppermute | solution.py:362
  163.6 3.8 %collective-permute-start.32 = (bf16[128,768]{1,0:T(8,128)(2,1)}, bf16[128,768]{1,0:T(8,128)(2,1)S(1)}, u32[]{:S(2)}, u32[]{:S(2)}) collective-permute-start(bf16[128,768]{1,0:T(8,128)(2,1)} %get-tuple-element.115), channel_id=1, source_target_pairs={{0,2},{1,3},{2,4},{3,5},{4,6},{5,7},{6,0},{7,1},{8,10},{9,11},{10,... | collective-permute-start | bytes 589832 | tf_op jit(solution)/shard_map/ppermute | solution.py:362
  169.9 3.5 %collective-permute-done.32 = bf16[128,768]{1,0:T(8,128)(2,1)S(1)} collective-permute-done((bf16[128,768]{1,0:T(8,128)(2,1)}, bf16[128,768]{1,0:T(8,128)(2,1)S(1)}, u32[]{:S(2)}, u32[]{:S(2)}) %collective-permute-start.32) | collective-permute-done | bytes 196640 | tf_op jit(solution)/shard_map/ppermute | solution.py:362
  173.5 7.8 %collective-permute-done.31 = bf16[128,768]{1,0:T(8,128)(2,1)S(1)} collective-permute-done((bf16[128,768]{1,0:T(8,128)(2,1)S(1)}, bf16[128,768]{1,0:T(8,128)(2,1)S(1)}, u32[]{:S(2)}, u32[]{:S(2)}) %collective-permute-start.31) | collective-permute-done | bytes 196640 | tf_op jit(solution)/shard_map/ppermute | solution.py:362
  183.9 9.1 %middle.1 = (f32[256,768]{1,0:T(8,128)}, f32[1,768]{1,0:T(1,128)}, bf16[256,768]{1,0:T(8,128)(2,1)}, bf16[256,768]{1,0:T(8,128)(2,1)}, f32[2,384,768]{2,1,0:T(8,128)}, /*index=5*/bf16[2,384,768]{2,1,0:T(8,128)(2,1)}) custom-call(bf16[256,768]{1,0:T(8,128)(2,1)} %bitcast.110, bf16[256,768]{1,0:T(8,128)(2,1)} %copy-done.17, ...), custom_call_target="tpu_custom_call" | custom-call | flops 1509949440 | bytes 7077888 | tf_op jit(solution)/shard_map/middle/pallas_call | solution.py:669
  193.1 9.1 %score_grads.1 = (bf16[256,768]{1,0:T(8,128)(2,1)}, bf16[256,768]{1,0:T(8,128)(2,1)}, f32[12,1,512]{2,1,0:T(1,128)}, f32[2,384,768]{2,1,0:T(8,128)}, bf16[2,384,768]{2,1,0:T(8,128)(2,1)}) custom-call(bf16[256,768]{1,0:T(8,128)(2,1)} %get-tuple-element.59.mixed_grad_ref, bf16[256,768]{1,0:T(8,128)(2,1)} %get-tuple-element.60.v_ref, ...), custom_call_target="tpu_custom_call" | custom-call | flops 1207959552 | bytes 7077888 | tf_op jit(solution)/shard_map/score_grads/pallas_call | solution.py:708
  202.2 6.8 %inputs.1 = (f32[256,768]{1,0:T(8,128)}, f32[1,768]{1,0:T(1,128)}) custom-call(bf16[256,768]{1,0:T(8,128)(2,1)} %get-tuple-element.63.refs_0_, bf16[256,768]{1,0:T(8,128)(2,1)} %get-tuple-element.64.refs_1_, bf16[256,768]{1,0:T(8,128)(2,1)} %get-tuple-element.65.refs_2_, bf16[256,768]{1,0:T(8,128)(2,1)} %refs_3_.5, f32[1,768]{1,0:T(1,128)} %reshape.195.refs_1_.refs_4_, ...), custom_call_target="tpu_custom_call" | custom-call | flops 1509949440 | bytes 7077888 | tf_op jit(solution)/shard_map/inputs/pallas_call | solution.py:732
  221.5 6.8 %collective-permute-start.43 = (f32[64,128]{1,0:T(8,128)S(1)}, f32[64,128]{1,0:T(8,128)S(1)}, u32[]{:S(2)}, u32[]{:S(2)}) collective-permute-start(f32[64,128]{1,0:T(8,128)S(1)} %add.173), channel_id=1, source_target_pairs={{0,6},{1,7},{2,0},{3,1},{4,2},{5,3},{6,4},{7,5},{8,14},{9,15},{10,... | collective-permute-start | bytes 98312 | tf_op jit(solution)/shard_map/ppermute | solution.py:362
  231.8 2.9 collective-permute-done.42
  243.7 8.7 %collective-permute-done.63.refs_4_ = bf16[512,768]{1,0:T(8,128)(2,1)} collective-permute-done((bf16[512,768]{1,0:T(8,128)(2,1)}, bf16[512,768]{1,0:T(8,128)(2,1)}, u32[]{:S(2)}, u32[]{:S(2)}) %collective-permute-start.63) | collective-permute-done | bytes 786464 | tf_op jit(solution)/shard_map/ppermute | solution.py:355
  253.5 18.8 %expert_grads.1 = (f32[1,768,768]{2,1,0:T(8,128)}, f32[1,768,768]{2,1,0:T(8,128)}) custom-call(s32[1]{0:T(128)} %bitcast.51.place_ref, bf16[512,768]{1,0:T(8,128)(2,1)} %get-tuple-element.130.rows_ref.refs_0_, bf16[256,768]{1,0:T(8,128)(2,1)} %copy-done.23, bf16[256,768]{1,0:T(8,128)(2,1)} %copy-done.24, bf16[512,768]{1,0:T(8,128)(2,1)} %collective-permute-done.62.refs_3_, ...), custom_call_target="tpu_custom_call" | custom-call | flops 9663676416 | bytes 11796480 | tf_op jit(solution)/shard_map/expert_grads/pallas_call | solution.py:641
  277.9 4.7 %collective-permute-done.45 = bf16[192,768]{1,0:T(8,128)(2,1)S(1)} collective-permute-done((bf16[192,768]{1,0:T(8,128)(2,1)S(1)}, bf16[192,768]{1,0:T(8,128)(2,1)S(1)}, u32[]{:S(2)}, u32[]{:S(2)}) %collective-permute-start.45) | collective-permute-done | bytes 294944 | tf_op jit(solution)/shard_map/ppermute | solution.py:358
  292.4 3.1 collective-permute-start.49
  295.5 4.3 %collective-permute-start.51 = (bf16[24,1536]{1,0:T(8,128)(2,1)S(1)}, bf16[24,1536]{1,0:T(8,128)(2,1)S(1)}, u32[]{:S(2)}, u32[]{:S(2)}) collective-permute-start(bf16[24,1536]{1,0:T(8,128)(2,1)S(1)} %get-tuple-element.136), channel_id=1, source_target_pairs={{0,2},{1,3},{2,4},{3,5},{4,6},{5,7},{6,0},{7,1},{8,10},{9,11},{10,... | collective-permute-start | bytes 221192 | tf_op jit(solution)/shard_map/ppermute | solution.py:362
  (275 shorter events, 104.8 us)
Async XLA Ops:
  2.2 11.7 %collective-permute-start.2 = (bf16[24,1536]{1,0:T(8,128)(2,1)S(1)}, bf16[24,1536]{1,0:T(8,128)(2,1)S(1)}, u32[]{:S(2)}, u32[]{:S(2)}) collective-permute-start(bf16[24,1536]{1,0:T(8,128)(2,1)S(1)} %constant_dynamic-update-slice_fusion), channel_id=1, source_target_pairs={{0,6},{1,7},{2,0},{3,1},{4,2},{5,3},{6,4},{7,5},{8,14},{9,15},{10,... | collective-permute-start | bytes 221192 | tf_op jit(solution)/shard_map/ppermute | solution.py:362
  24.5 11.3 %collective-permute-start.4 = (bf16[192,768]{1,0:T(8,128)(2,1)S(1)}, bf16[192,768]{1,0:T(8,128)(2,1)S(1)}, u32[]{:S(2)}, u32[]{:S(2)}) collective-permute-start(bf16[192,768]{1,0:T(8,128)(2,1)S(1)} %pad_maximum_fusion.18.refs_4_.refs_7_), channel_id=1, source_target_pairs={{0,16},{8,24},{16,0},{24,8},{1,17},{9,25},{17,1},{25,9},{2,18},{10... | collective-permute-start | bytes 884744 | tf_op jit(solution)/shard_map/ppermute | solution.py:358
  25.1 11.1 %collective-permute-start.9 = (bf16[192,768]{1,0:T(8,128)(2,1)S(1)}, bf16[192,768]{1,0:T(8,128)(2,1)S(1)}, u32[]{:S(2)}, u32[]{:S(2)}) collective-permute-start(bf16[192,768]{1,0:T(8,128)(2,1)S(1)} %pad_maximum_fusion.19.refs_8_.refs_11_), channel_id=1, source_target_pairs={{0,1},{1,0},{2,3},{3,2},{4,5},{5,4},{6,7},{7,6},{8,9},{9,8},{10,11... | collective-permute-start | bytes 884744 | tf_op jit(solution)/shard_map/ppermute | solution.py:352
  29.6 11.8 %collective-permute-start.15 = (bf16[192,768]{1,0:T(8,128)(2,1)S(1)}, bf16[192,768]{1,0:T(8,128)(2,1)}, u32[]{:S(2)}, u32[]{:S(2)}) collective-permute-start(bf16[192,768]{1,0:T(8,128)(2,1)S(1)} %pad_maximum_fusion.20.refs_7_.refs_15_), channel_id=1, source_target_pairs={{0,16},{8,24},{16,0},{24,8},{1,17},{9,25},{17,1},{25,9},{2,18},{10... | collective-permute-start | bytes 884744 | tf_op jit(solution)/shard_map/ppermute | solution.py:358
  36.3 28.4 %collective-permute-start.16 = (bf16[192,768]{1,0:T(8,128)(2,1)S(1)}, bf16[192,768]{1,0:T(8,128)(2,1)}, u32[]{:S(2)}, u32[]{:S(2)}) collective-permute-start(bf16[192,768]{1,0:T(8,128)(2,1)S(1)} %pad_maximum_fusion.20.refs_7_.refs_15_), channel_id=1, source_target_pairs={{0,1},{1,0},{2,3},{3,2},{4,5},{5,4},{6,7},{7,6},{8,9},{9,8},{10,11... | collective-permute-start | bytes 884744 | tf_op jit(solution)/shard_map/ppermute | solution.py:352
  36.9 27.8 %collective-permute-start.20 = (bf16[192,896]{1,0:T(8,128)(2,1)S(1)}, bf16[192,896]{1,0:T(8,128)(2,1)S(1)}, u32[]{:S(2)}, u32[]{:S(2)}) collective-permute-start(bf16[192,896]{1,0:T(8,128)(2,1)S(1)} %pad_maximum_fusion.16.refs_11_.refs_10_), channel_id=1, source_target_pairs={{0,1},{1,0},{2,3},{3,2},{4,5},{5,4},{6,7},{7,6},{8,9},{9,8},{10,11... | collective-permute-start | bytes 1032200 | tf_op jit(solution)/shard_map/ppermute | solution.py:352
  41.4 15.4 %collective-permute-start.10 = (bf16[192,768]{1,0:T(8,128)(2,1)}, bf16[192,768]{1,0:T(8,128)(2,1)}, u32[]{:S(2)}, u32[]{:S(2)}) collective-permute-start(bf16[192,768]{1,0:T(8,128)(2,1)} %collective-permute-done.8.refs_9_.refs_12_), channel_id=1, source_target_pairs={{0,1},{1,0},{2,3},{3,2},{4,5},{5,4},{6,7},{7,6},{8,9},{9,8},{10,11... | collective-permute-start | bytes 884744 | tf_op jit(solution)/shard_map/ppermute | solution.py:352
  42.0 22.7 %collective-permute-start.17 = (bf16[192,768]{1,0:T(8,128)(2,1)}, bf16[192,768]{1,0:T(8,128)(2,1)}, u32[]{:S(2)}, u32[]{:S(2)}) collective-permute-start(bf16[192,768]{1,0:T(8,128)(2,1)} %collective-permute-done.15.refs_8_.refs_16_), channel_id=1, source_target_pairs={{0,1},{1,0},{2,3},{3,2},{4,5},{5,4},{6,7},{7,6},{8,9},{9,8},{10,11... | collective-permute-start | bytes 884744 | tf_op jit(solution)/shard_map/ppermute | solution.py:352
  42.0 22.7 %collective-permute-start.21 = (bf16[192,896]{1,0:T(8,128)(2,1)S(1)}, bf16[192,896]{1,0:T(8,128)(2,1)S(1)}, u32[]{:S(2)}, u32[]{:S(2)}) collective-permute-start(bf16[192,896]{1,0:T(8,128)(2,1)S(1)} %collective-permute-done.19.refs_12_.refs_11_), channel_id=1, source_target_pairs={{0,1},{1,0},{2,3},{3,2},{4,5},{5,4},{6,7},{7,6},{8,9},{9,8},{10,11... | collective-permute-start | bytes 1032200 | tf_op jit(solution)/shard_map/ppermute | solution.py:352
  56.8 18.4 %collective-permute-start.26 = (bf16[256,768]{1,0:T(8,128)(2,1)}, bf16[256,768]{1,0:T(8,128)(2,1)S(1)}, u32[]{:S(2)}, u32[]{:S(2)}) collective-permute-start(bf16[256,768]{1,0:T(8,128)(2,1)} %get-tuple-element.54), channel_id=1, source_target_pairs={{0,1},{1,0},{2,3},{3,2},{4,5},{5,4},{6,7},{7,6},{8,9},{9,8},{10,11... | collective-permute-start | bytes 1179656 | tf_op jit(solution)/shard_map/ppermute | solution.py:352
  76.9 14.9 %collective-permute-start.29 = (bf16[128,768]{1,0:T(8,128)(2,1)S(1)}, bf16[128,768]{1,0:T(8,128)(2,1)S(1)}, u32[]{:S(2)}, u32[]{:S(2)}) collective-permute-start(bf16[128,768]{1,0:T(8,128)(2,1)S(1)} %get-tuple-element.120), channel_id=1, source_target_pairs={{0,6},{1,7},{2,0},{3,1},{4,2},{5,3},{6,4},{7,5},{8,14},{9,15},{10,... | collective-permute-start | bytes 589832 | tf_op jit(solution)/shard_map/ppermute | solution.py:362
  79.2 24.0 %collective-permute-start.28 = (bf16[128,768]{1,0:T(8,128)(2,1)S(1)}, bf16[128,768]{1,0:T(8,128)(2,1)S(1)}, u32[]{:S(2)}, u32[]{:S(2)}) collective-permute-start(bf16[128,768]{1,0:T(8,128)(2,1)S(1)} %get-tuple-element.121), channel_id=1, source_target_pairs={{0,4},{1,5},{2,6},{3,7},{4,0},{5,1},{6,2},{7,3},{8,12},{9,13},{10,... | collective-permute-start | bytes 589832 | tf_op jit(solution)/shard_map/ppermute | solution.py:362
  81.2 23.5 %collective-permute-start.23 = (bf16[128,768]{1,0:T(8,128)(2,1)S(1)}, bf16[128,768]{1,0:T(8,128)(2,1)S(1)}, u32[]{:S(2)}, u32[]{:S(2)}) collective-permute-start(bf16[128,768]{1,0:T(8,128)(2,1)S(1)} %get-tuple-element.123), channel_id=1, source_target_pairs={{0,2},{1,3},{2,4},{3,5},{4,6},{5,7},{6,0},{7,1},{8,10},{9,11},{10,... | collective-permute-start | bytes 589832 | tf_op jit(solution)/shard_map/ppermute | solution.py:362
  84.9 30.2 %collective-permute-start.64 = (bf16[256,768]{1,0:T(8,128)(2,1)S(1)}, bf16[256,768]{1,0:T(8,128)(2,1)S(1)}, u32[]{:S(2)}, u32[]{:S(2)}) collective-permute-start(bf16[256,768]{1,0:T(8,128)(2,1)S(1)} %pad_maximum_fusion.14), channel_id=1, source_target_pairs={{0,8},{8,0},{16,24},{24,16},{1,9},{9,1},{17,25},{25,17},{2,10},{10... | collective-permute-start | bytes 1179656 | tf_op jit(solution)/shard_map/ppermute | solution.py:355
  86.4 21.9 %collective-permute-start.25 = (bf16[128,768]{1,0:T(8,128)(2,1)S(1)}, bf16[128,768]{1,0:T(8,128)(2,1)S(1)}, u32[]{:S(2)}, u32[]{:S(2)}) collective-permute-start(bf16[128,768]{1,0:T(8,128)(2,1)S(1)} %get-tuple-element.124), channel_id=1, source_target_pairs={{0,6},{1,7},{2,0},{3,1},{4,2},{5,3},{6,4},{7,5},{8,14},{9,15},{10,... | collective-permute-start | bytes 589832 | tf_op jit(solution)/shard_map/ppermute | solution.py:362
  91.8 21.7 %collective-permute-start.24 = (bf16[128,768]{1,0:T(8,128)(2,1)S(1)}, bf16[128,768]{1,0:T(8,128)(2,1)S(1)}, u32[]{:S(2)}, u32[]{:S(2)}) collective-permute-start(bf16[128,768]{1,0:T(8,128)(2,1)S(1)} %get-tuple-element.125), channel_id=1, source_target_pairs={{0,4},{1,5},{2,6},{3,7},{4,0},{5,1},{6,2},{7,3},{8,12},{9,13},{10,... | collective-permute-start | bytes 589832 | tf_op jit(solution)/shard_map/ppermute | solution.py:362
  103.2 12.0 %collective-permute-start.65 = (bf16[256,768]{1,0:T(8,128)(2,1)S(1)}, bf16[256,768]{1,0:T(8,128)(2,1)S(1)}, u32[]{:S(2)}, u32[]{:S(2)}) collective-permute-start(bf16[256,768]{1,0:T(8,128)(2,1)S(1)} %pad_maximum_fusion.15), channel_id=1, source_target_pairs={{0,16},{8,24},{16,0},{24,8},{1,17},{9,25},{17,1},{25,9},{2,18},{10... | collective-permute-start | bytes 1179656 | tf_op jit(solution)/shard_map/ppermute | solution.py:358
  104.8 11.6 %collective-permute-start.60 = (bf16[256,768]{1,0:T(8,128)(2,1)S(1)}, bf16[256,768]{1,0:T(8,128)(2,1)S(1)}, u32[]{:S(2)}, u32[]{:S(2)}) collective-permute-start(bf16[256,768]{1,0:T(8,128)(2,1)S(1)} %pad_maximum_fusion.12), channel_id=1, source_target_pairs={{0,8},{8,0},{16,24},{24,16},{1,9},{9,1},{17,25},{25,17},{2,10},{10... | collective-permute-start | bytes 1179656 | tf_op jit(solution)/shard_map/ppermute | solution.py:355
  113.6 11.1 %collective-permute-start.61 = (bf16[256,768]{1,0:T(8,128)(2,1)S(1)}, bf16[256,768]{1,0:T(8,128)(2,1)S(1)}, u32[]{:S(2)}, u32[]{:S(2)}) collective-permute-start(bf16[256,768]{1,0:T(8,128)(2,1)S(1)} %pad_maximum_fusion.13), channel_id=1, source_target_pairs={{0,16},{8,24},{16,0},{24,8},{1,17},{9,25},{17,1},{25,9},{2,18},{10... | collective-permute-start | bytes 1179656 | tf_op jit(solution)/shard_map/ppermute | solution.py:358
  145.2 16.4 %collective-permute-start.35 = (bf16[128,768]{1,0:T(8,128)(2,1)S(1)}, bf16[128,768]{1,0:T(8,128)(2,1)S(1)}, u32[]{:S(2)}, u32[]{:S(2)}) collective-permute-start(bf16[128,768]{1,0:T(8,128)(2,1)S(1)} %get-tuple-element.110), channel_id=1, source_target_pairs={{0,4},{1,5},{2,6},{3,7},{4,0},{5,1},{6,2},{7,3},{8,12},{9,13},{10,... | collective-permute-start | bytes 589832 | tf_op jit(solution)/shard_map/ppermute | solution.py:362
  147.8 13.8 %collective-permute-start.34 = (bf16[128,768]{1,0:T(8,128)(2,1)S(1)}, bf16[128,768]{1,0:T(8,128)(2,1)S(1)}, u32[]{:S(2)}, u32[]{:S(2)}) collective-permute-start(bf16[128,768]{1,0:T(8,128)(2,1)S(1)} %get-tuple-element.111), channel_id=1, source_target_pairs={{0,6},{1,7},{2,0},{3,1},{4,2},{5,3},{6,4},{7,5},{8,14},{9,15},{10,... | collective-permute-start | bytes 589832 | tf_op jit(solution)/shard_map/ppermute | solution.py:362
  162.6 20.5 %collective-permute-start.37 = (bf16[256,768]{1,0:T(8,128)(2,1)}, bf16[256,768]{1,0:T(8,128)(2,1)S(1)}, u32[]{:S(2)}, u32[]{:S(2)}) collective-permute-start(bf16[256,768]{1,0:T(8,128)(2,1)} %bitcast.27), channel_id=1, source_target_pairs={{0,1},{1,0},{2,3},{3,2},{4,5},{5,4},{6,7},{7,6},{8,9},{9,8},{10,11... | collective-permute-start | bytes 1179656 | tf_op jit(solution)/shard_map/ppermute | solution.py:352
  167.4 13.9 %collective-permute-start.31 = (bf16[128,768]{1,0:T(8,128)(2,1)S(1)}, bf16[128,768]{1,0:T(8,128)(2,1)S(1)}, u32[]{:S(2)}, u32[]{:S(2)}) collective-permute-start(bf16[128,768]{1,0:T(8,128)(2,1)S(1)} %get-tuple-element.116), channel_id=1, source_target_pairs={{0,4},{1,5},{2,6},{3,7},{4,0},{5,1},{6,2},{7,3},{8,12},{9,13},{10,... | collective-permute-start | bytes 589832 | tf_op jit(solution)/shard_map/ppermute | solution.py:362
  167.4 13.9 %collective-permute-start.30 = (bf16[128,768]{1,0:T(8,128)(2,1)S(1)}, bf16[128,768]{1,0:T(8,128)(2,1)}, u32[]{:S(2)}, u32[]{:S(2)}) collective-permute-start(bf16[128,768]{1,0:T(8,128)(2,1)S(1)} %get-tuple-element.117), channel_id=1, source_target_pairs={{0,6},{1,7},{2,0},{3,1},{4,2},{5,3},{6,4},{7,5},{8,14},{9,15},{10,... | collective-permute-start | bytes 589832 | tf_op jit(solution)/shard_map/ppermute | solution.py:362
  217.3 25.8 %collective-permute-start.67 = (bf16[512,768]{1,0:T(8,128)(2,1)S(1)}, bf16[512,768]{1,0:T(8,128)(2,1)}, u32[]{:S(2)}, u32[]{:S(2)}) collective-permute-start(bf16[512,768]{1,0:T(8,128)(2,1)S(1)} %get-tuple-element.126), channel_id=1, source_target_pairs={{0,8},{8,0},{16,24},{24,16},{1,9},{9,1},{17,25},{25,17},{2,10},{10... | collective-permute-start | bytes 2359304 | tf_op jit(solution)/shard_map/ppermute | solution.py:355
  218.7 25.0 %collective-permute-start.66 = (bf16[512,768]{1,0:T(8,128)(2,1)S(1)}, bf16[512,768]{1,0:T(8,128)(2,1)}, u32[]{:S(2)}, u32[]{:S(2)}) collective-permute-start(bf16[512,768]{1,0:T(8,128)(2,1)S(1)} %get-tuple-element.128), channel_id=1, source_target_pairs={{0,16},{8,24},{16,0},{24,8},{1,17},{9,25},{17,1},{25,9},{2,18},{10... | collective-permute-start | bytes 2359304 | tf_op jit(solution)/shard_map/ppermute | solution.py:358
  219.2 33.1 %collective-permute-start.63 = (bf16[512,768]{1,0:T(8,128)(2,1)}, bf16[512,768]{1,0:T(8,128)(2,1)}, u32[]{:S(2)}, u32[]{:S(2)}) collective-permute-start(bf16[512,768]{1,0:T(8,128)(2,1)} %get-tuple-element.129), channel_id=1, source_target_pairs={{0,8},{8,0},{16,24},{24,16},{1,9},{9,1},{17,25},{25,17},{2,10},{10... | collective-permute-start | bytes 2359304 | tf_op jit(solution)/shard_map/ppermute | solution.py:355
  219.8 33.7 %collective-permute-start.62 = (bf16[512,768]{1,0:T(8,128)(2,1)}, bf16[512,768]{1,0:T(8,128)(2,1)}, u32[]{:S(2)}, u32[]{:S(2)}) collective-permute-start(bf16[512,768]{1,0:T(8,128)(2,1)} %get-tuple-element.131), channel_id=1, source_target_pairs={{0,16},{8,24},{16,0},{24,8},{1,17},{9,25},{17,1},{25,9},{2,18},{10... | collective-permute-start | bytes 2359304 | tf_op jit(solution)/shard_map/ppermute | solution.py:358
  240.8 31.6 %collective-permute-start.44 = (bf16[2,384,768]{2,1,0:T(8,128)(2,1)}, bf16[2,384,768]{2,1,0:T(8,128)(2,1)S(1)}, u32[]{:S(2)}, u32[]{:S(2)}) collective-permute-start(bf16[2,384,768]{2,1,0:T(8,128)(2,1)} %get-tuple-element.73), channel_id=1, source_target_pairs={{0,1},{1,0},{2,3},{3,2},{4,5},{5,4},{6,7},{7,6},{8,9},{9,8},{10,11... | collective-permute-start | bytes 3538952 | tf_op jit(solution)/shard_map/ppermute | solution.py:352
  243.2 30.5 %collective-permute-start.52 = (bf16[2,384,768]{2,1,0:T(8,128)(2,1)}, bf16[2,384,768]{2,1,0:T(8,128)(2,1)S(1)}, u32[]{:S(2)}, u32[]{:S(2)}) collective-permute-start(bf16[2,384,768]{2,1,0:T(8,128)(2,1)} %get-tuple-element.75), channel_id=1, source_target_pairs={{0,1},{1,0},{2,3},{3,2},{4,5},{5,4},{6,7},{7,6},{8,9},{9,8},{10,11... | collective-permute-start | bytes 3538952 | tf_op jit(solution)/shard_map/ppermute | solution.py:352
  275.8 14.9 %collective-permute-start.55 = (bf16[2,96,768]{2,1,0:T(8,128)(2,1)S(1)}, bf16[2,96,768]{2,1,0:T(8,128)(2,1)S(1)}, u32[]{:S(2)}, u32[]{:S(2)}) collective-permute-start(bf16[2,96,768]{2,1,0:T(8,128)(2,1)S(1)} %slice_bitcast_fusion.5), channel_id=1, source_target_pairs={{0,8},{8,0},{16,24},{24,16},{1,9},{9,1},{17,25},{25,17},{2,10},{10... | collective-permute-start | bytes 884744 | tf_op jit(solution)/shard_map/ppermute | solution.py:355
  288.0 11.7 %collective-permute-start.54 = (bf16[96,768]{1,0:T(8,128)(2,1)S(1)}, bf16[96,768]{1,0:T(8,128)(2,1)S(1)}, u32[]{:S(2)}, u32[]{:S(2)}) collective-permute-start(bf16[96,768]{1,0:T(8,128)(2,1)S(1)} %slice.444), channel_id=1, source_target_pairs={{0,8},{8,0},{16,24},{24,16},{1,9},{9,1},{17,25},{25,17},{2,10},{10... | collective-permute-start | bytes 442376 | tf_op jit(solution)/shard_map/ppermute | solution.py:355
  (71 other events, 751.5 us)

commit v2 on v1

v2 whole, which is shorter than its diff:
```python
import functools

import jax
import jax.numpy as jnp
from jax import lax
from jax.experimental import pallas as pl
from jax.experimental.pallas import tpu as pltpu
from jax.sharding import PartitionSpec as P

PRECISE = lax.Precision.HIGHEST
EPSILON = 1e-06
BF = jnp.bfloat16
F32 = jnp.float32
VMEM_BYTES = 20 * 1024 * 1024
GROUP = 256
FAR_FIRST = (2, 3, 1)


def mm(a, b):
    return jnp.dot(a, b, preferred_element_type=F32)


def mm_nt(a, b):
    return lax.dot_general(a, b, (((1,), (1,)), ((), ())), preferred_element_type=F32)


def mm_tn(a, b):
    return lax.dot_general(a, b, (((0,), (0,)), ((), ())), preferred_element_type=F32)


def full(shape):
    return pl.BlockSpec(shape, lambda *_: (0,) * len(shape))


def cols(rows, width):
    return pl.BlockSpec((rows, width), lambda g, *_: (0, g))


def shape_of(shape, dtype):
    return jax.ShapeDtypeStruct(shape, dtype)


def params():
    return pltpu.CompilerParams(vmem_limit_bytes=VMEM_BYTES)


def cost(flops, nbytes):
    return pl.CostEstimate(flops=1024, bytes_accessed=1024, transcendentals=0)


def after(v, *others):
    return lax.optimization_barrier((v, *others))[0]


def all_after(values, *others):
    return list(lax.optimization_barrier((*values, *others))[: len(values)])


def gelu_parts(v):
    square = v * v
    bent = jnp.tanh(0.7978845608 * v * (1.0 + 0.044715 * square))
    half = 0.5 * (1.0 + bent)
    slope = half + 0.5 * v * (1.0 - bent * bent) * (0.7978845608 * (1.0 + 0.134145 * square))
    return v * half, slope


def gate_of(rows, router, picked):
    logits = mm(rows, router)
    exponent = jnp.exp(logits - jnp.max(logits, axis=-1, keepdims=True))
    router_probs = exponent / jnp.sum(exponent, axis=-1, keepdims=True)
    return router_probs, jnp.sum(router_probs * picked, axis=-1, keepdims=True)


def one_lane(shape, lane):
    return (lax.broadcasted_iota(jnp.int32, shape, 1) == lane).astype(F32)


def pack_kernel(*refs):
    out_ref = refs[-1]
    base = 0
    for ref in refs[:-2]:
        out_ref[:, base : base + ref.shape[1]] = ref[...]
        base += ref.shape[1]
    router = refs[-2][...]
    out_ref[:, base:] = jnp.concatenate(
        [router, jnp.zeros((router.shape[0], out_ref.shape[1] - base - router.shape[1]), router.dtype)], axis=1
    )


def route_kernel(
    room,
    nz,
    near,
    where_ref,
    routes_ref,
    dy_ref,
    order_ref,
    x_ref,
    gain_ref,
    next_gain_ref,
    slots_ref,
    slots_t_ref,
    keep_ref,
    send_ref,
    perm_ref,
    normed_ref,
    picked_ref,
    gain_out_ref,
    gain_next_ref,
):
    slots, tokens = slots_ref.shape
    experts = picked_ref.shape[1]
    z, c = where_ref[0], where_ref[1]
    expert = routes_ref[...]
    lanes = lax.broadcasted_iota(jnp.int32, (128, tokens), 0)
    picked = (lanes == expert).astype(F32)
    upper = (
        lax.broadcasted_iota(jnp.int32, (tokens, tokens), 0)
        <= lax.broadcasted_iota(jnp.int32, (tokens, tokens), 1)
    ).astype(BF)
    counts = mm(picked.astype(BF), upper)
    rank = jnp.sum(picked * (counts - 1.0), axis=0, keepdims=True).astype(jnp.int32)
    to_z, to_c = expert >> 1, expert & 1
    ahead = to_z ^ z if near else to_z
    other = jnp.where(to_c == c, 0, 1)
    slot = (other * nz + ahead) * room + rank
    chosen = (lax.broadcasted_iota(jnp.int32, (slots, tokens), 0) == slot).astype(F32)
    slots_ref[...] = chosen.astype(BF)
    slots_t_ref[...] = chosen.T.astype(BF)
    dy_rows = mm(slots_ref[...], dy_ref[...]).astype(BF)
    keep_ref[...] = dy_rows[: slots // 2]
    send_ref[: slots // 2, :] = dy_rows[slots // 2 :]
    picked_ref[...] = picked.T[:, :experts]
    width = perm_ref.shape[0]
    perm = (lax.broadcasted_iota(jnp.int32, (width, width), 0) == order_ref[...]).astype(F32).astype(BF)
    perm_ref[...] = perm
    x = x_ref[...].astype(F32)
    scale = lax.rsqrt(jnp.mean(x * x, axis=-1, keepdims=True) + EPSILON)
    normed = mm((x * scale * gain_ref[...]).astype(BF), perm).astype(BF)
    normed_ref[...] = normed
    send_ref[slots // 2 :, : width // 2] = normed[: tokens // 2, width // 2 :]
    send_ref[slots // 2 :, width // 2 :] = normed[tokens // 2 :, width // 2 :]
    gain_out_ref[...] = gain_ref[...]
    gain_next_ref[...] = next_gain_ref[...]


def bias_kernel(buckets_ref, table_ref, bias_ref, along):
    heads, rows = bias_ref.shape[0], bias_ref.shape[1]
    half, span = rows // 2, buckets_ref.shape[1]
    step = pl.program_id(0)

    @pl.when(step == 0)
    def _():
        every = table_ref.shape[0]
        onehot = (lax.broadcasted_iota(jnp.int32, (every, span), 0) == buckets_ref[...]).astype(F32)
        values = lax.dot_general(
            table_ref[...], onehot, (((0,), (0,)), ((), ())), precision=PRECISE, preferred_element_type=F32
        )
        for h in range(along.shape[0]):
            along[h] = values[h : h + 1]

    for h in range(heads):
        line = jnp.broadcast_to(along[step * heads + h], (half, span))
        turned = pltpu.roll(line, span - rows + 1, 1, stride=1, stride_axis=0)
        bias_ref[h, :half, :] = turned[:, :rows]
        bias_ref[h, half:, :half] = turned[:, span - half :]
        bias_ref[h, half:, half:] = turned[:, :half]


def fill_x_first(pieces, out_ref):
    half = pieces[0].shape[0]
    for number, piece in enumerate(pieces):
        out_ref[number * half : (number + 1) * half, :] = piece[...]


def fill_y_first(pieces, out_ref, starts=(0, 0, 0, 0)):
    half = pieces[0].shape[0]
    part = half // 2
    width = out_ref.shape[1]
    for side in range(2):
        own, other = pieces[2 * side], pieces[2 * side + 1]
        at, at_other = [slice(start, start + width) for start in starts[2 * side : 2 * side + 2]]
        base = side * 2 * half
        out_ref[base : base + part, :] = own[:part, at]
        out_ref[base + part : base + half, :] = other[:part, at_other]
        out_ref[base + half : base + half + part, :] = own[part:, at]
        out_ref[base + half + part : base + 2 * half, :] = other[part:, at_other]


def near_kernel(qv_ref, qv_x_ref, ko_ref, ko_y_ref, qv_near_ref, ko_near_ref, both_ref):
    part, width = qv_ref.shape
    for number, (left, right) in enumerate(((qv_ref, ko_ref), (qv_x_ref, ko_y_ref))):
        at = slice(number * part, (number + 1) * part)
        qv_near_ref[at, :] = left[...]
        ko_near_ref[at, :] = right[...]
        both_ref[at, :width] = left[...]
        both_ref[at, width:] = right[...]


def attend_kernel(head, *refs):
    normed_ref, bias_ref, perm_ref, x_ref, gain_ref, slots_ref, picked_ref = refs[:7]
    wq_refs, wv_refs, wk_refs, ko_refs = refs[7:11], refs[11:15], refs[15:19], refs[19:23]
    q_ref, k_ref, v_ref, probs_ref, mixed_ref, mixed_other_ref = refs[23:29]
    middle_ref, router_ref, gate_ref, keep_ref, send_ref = refs[29:34]
    wq, wk, wv, wo, mixed = refs[34:]
    step = pl.program_id(0)
    experts = router_ref.shape[1]
    model = x_ref.shape[1]

    fill_x_first(wq_refs, wq)
    fill_y_first(wk_refs, wk)
    fill_x_first(wv_refs, wv)
    normed = normed_ref[...]
    q = mm(normed, wq[...]).astype(BF)
    k = mm(normed, wk[...]).astype(BF)
    v = mm(normed, wv[...]).astype(BF)
    q_ref[...] = q
    k_ref[...] = k
    v_ref[...] = v
    rows = []
    for h in range(q.shape[1] // head):
        part = slice(h * head, (h + 1) * head)
        scores = mm_nt(q[:, part], k[:, part]) + bias_ref[h]
        exponent = jnp.exp(scores - jnp.max(scores, axis=-1, keepdims=True))
        probs = exponent / jnp.sum(exponent, axis=-1, keepdims=True)
        probs_ref[h] = probs
        rows.append(mm(probs.astype(BF), v[:, part]))
    mixed[step] = jnp.concatenate(rows, axis=1).astype(BF)

    @pl.when(step == pl.num_programs(0) - 1)
    def _():
        fill_y_first(ko_refs, wo, (model, model, 3 * model, model))
        perm = perm_ref[...]
        every = jnp.concatenate([mixed[g] for g in range(mixed.shape[0])], axis=1)
        mixed_in_order = mm(every, perm).astype(BF)
        mixed_ref[...] = mixed_in_order[:, : model // 2]
        mixed_other_ref[...] = mixed_in_order[:, model // 2 :]
        middle = x_ref[...].astype(F32) + mm(mixed_in_order, wo[:, :model])
        middle_ref[...] = middle
        scale = lax.rsqrt(jnp.mean(middle * middle, axis=-1, keepdims=True) + EPSILON)
        ffn_in = (middle * scale * gain_ref[...]).astype(BF)
        router = mm(perm, wo[:, model:]).astype(BF)[:, :experts]
        router_ref[...] = router
        rows = mm(slots_ref[...], ffn_in).astype(BF)
        gate_ref[...] = gate_of(ffn_in, router, picked_ref[...])[1]
        half = rows.shape[0] // 2
        keep_ref[...] = rows[:half]
        send_ref[...] = rows[half:]


def join(refs, out_ref):
    base = 0
    for ref in refs:
        size = ref.shape[0]
        out_ref[base : base + size, :] = ref[...]
        base += size


def part_out(v, refs):
    base = 0
    for ref in refs:
        size = ref.shape[0]
        ref[...] = v[base : base + size]
        base += size


def expert_kernel(pieces, extra, own_ref, *refs):
    rows_refs, dy = refs[:pieces], refs[pieces]
    router_ref, w1_ref, w2_ref = refs[pieces + 1 : pieces + 4]
    refs = refs[pieces + 4 :]
    extra_refs, refs = refs[: sum(extra)], refs[sum(extra) :]
    back_refs, result_refs = refs[:pieces], refs[pieces : 2 * pieces]
    router_grad_ref, rows = refs[2 * pieces : 2 * pieces + 2]
    extra_out, refs = refs[2 * pieces + 2 : 2 * pieces + 2 + len(extra)], refs[2 * pieces + 2 + len(extra) :]
    branch, probs_ref, gate_ref, result, back = refs
    step = pl.program_id(0)
    own = own_ref[0]

    @pl.when(step == 0)
    def _():
        join(rows_refs, rows)
        base = 0
        for count, out_ref in zip(extra, extra_out, strict=True):
            join(extra_refs[base : base + count], out_ref)
            base += count
        router_probs, gate = gate_of(rows[...], router_ref[...], one_lane(probs_ref.shape, own))
        probs_ref[...] = router_probs
        gate_ref[...] = gate
        branch[...] = (dy[...].astype(F32) * gate).astype(BF)
        result[...] = jnp.zeros_like(result)
        back[...] = jnp.zeros_like(back)

    w1, w2 = w1_ref[0], w2_ref[0]
    hidden, slope = gelu_parts(mm(rows[...], w1))
    result[...] += mm(hidden.astype(BF), w2)
    pre_grad = (mm_nt(branch[...], w2) * slope).astype(BF)
    back[...] += mm_nt(pre_grad, w1)

    @pl.when(step == pl.num_programs(0) - 1)
    def _():
        returned = result[...].astype(BF)
        part_out(returned, result_refs)
        gate_grad = jnp.sum(dy[...].astype(F32) * returned.astype(F32), axis=-1, keepdims=True)
        router_probs, gate = probs_ref[...], gate_ref[...]
        picked = one_lane(router_probs.shape, own)
        logit_grad = (router_probs * (picked - gate) * gate_grad).astype(BF)
        router_grad_ref[...] = mm_tn(logit_grad, rows[...])
        part_out((back[...] + mm_nt(logit_grad, router_ref[...])).astype(BF), back_refs)


def expert_grad_kernel(pieces, more, place_ref, *refs):
    del place_ref
    rows_refs, dy_refs, refs = refs[:pieces], refs[pieces : 2 * pieces], refs[2 * pieces :]
    own_ref, router_ref, w1_ref, w2_ref = refs[:4]
    g1_ref, g2_ref, rows_all, branch_all = refs[-4:]

    @pl.when(pl.program_id(0) == 0)
    def _():
        join(rows_refs, rows_all)
        join(dy_refs, branch_all)
        picked = one_lane((rows_all.shape[0], router_ref.shape[1]), own_ref[0])
        gate = gate_of(rows_all[...], router_ref[...], picked)[1]
        branch_all[...] = (branch_all[...].astype(F32) * gate).astype(BF)

    rows, branch = rows_all[...], branch_all[...]
    hidden, slope = gelu_parts(mm(rows, w1_ref[0]))
    pre_grad = (mm_nt(branch, w2_ref[0]) * slope).astype(BF)
    g1, g2 = mm_tn(rows, pre_grad), mm_tn(hidden.astype(BF), branch)
    if more:
        g1, g2 = g1 + refs[4][0], g2 + refs[5][0]
    g1_ref[0] = g1
    g2_ref[0] = g2


def middle_kernel(head, pieces, *refs):
    keep_refs, refs = refs[:pieces], refs[pieces:]
    (send_ref, slots_t_ref, dy_ref, middle_ref, gain_ref, perm_ref, probs_ref, other_ref) = refs[:8]
    ko_refs = refs[8:12]
    (middle_grad_ref, gain_grad_ref, mixed_grad_ref, grads_ref, wo, mixed_grad) = refs[12:]
    rows, model = dy_ref.shape
    step = pl.program_id(0)
    keep_rows = send_ref.shape[0] // pieces

    @pl.when(step == 0)
    def _():
        fill_y_first(ko_refs, wo, (model, model, 3 * model, model))
        back = jnp.concatenate([ref[:keep_rows, :] for ref in keep_refs] + [send_ref[...]], axis=0)
        ffn_grad = mm(slots_t_ref[...], back)
        middle = middle_ref[...]
        scale = lax.rsqrt(jnp.mean(middle * middle, axis=-1, keepdims=True) + EPSILON)
        gain_grad_ref[...] = jnp.sum(ffn_grad * middle * scale, axis=0, keepdims=True)
        scaled = ffn_grad * gain_ref[...]
        along = jnp.mean(scaled * middle, axis=-1, keepdims=True)
        middle_grad = dy_ref[...].astype(F32) + scale * scaled - middle * (scale * scale * scale * along)
        middle_grad_ref[...] = middle_grad
        attn_grad = middle_grad.astype(BF)
        grads_ref[rows : 2 * rows, :] = attn_grad
        grads_ref[2 * rows :, : model // 2] = other_ref[: rows // 2, :]
        grads_ref[2 * rows :, model // 2 :] = other_ref[rows // 2 :, :]
        in_order = mm_nt(attn_grad, wo[...]).astype(BF)
        every = mm_nt(in_order, perm_ref[...]).astype(BF)
        mixed_grad_ref[...] = every
        for g in range(mixed_grad.shape[0]):
            mixed_grad[g] = every[:, g * GROUP : (g + 1) * GROUP]

    grads = mixed_grad[step]
    parts = [
        mm_tn(probs_ref[h].astype(BF), grads[:, h * head : (h + 1) * head]) for h in range(GROUP // head)
    ]
    value_grad = jnp.concatenate(parts, axis=1).astype(BF)
    at = pl.ds(pl.multiple_of(step * GROUP, GROUP), GROUP)
    grads_ref[:rows, at] = value_grad


def weight_grad_kernel(normed_ref, side_ref, mixed_ref, vo_ref, vo_side_ref, qk_ref, qk_side_ref, *outs):
    a_ref, a_low_ref, b_ref, b_low_ref = outs
    rows = normed_ref.shape[0]
    width = side_ref.shape[1] // 2
    model = normed_ref.shape[1]
    half, part = width // 2, width // 4

    def unpack(v):
        return [v[:, :width], v[:, width:]]

    normed = jnp.concatenate([normed_ref[:, :width], *unpack(side_ref[...])], axis=0)
    mixed = jnp.concatenate([mixed_ref[...], *unpack(vo_side_ref[2 * rows :, :])], axis=0)
    for number, (left, own, side) in enumerate(
        ((normed, vo_ref, vo_side_ref), (normed, qk_ref, qk_side_ref), (mixed, vo_ref, vo_side_ref), (normed, qk_ref, qk_side_ref))
    ):
        here = slice(0, rows) if number < 2 else slice(rows, 2 * rows)
        total = mm_tn(left, jnp.concatenate([own[here, :], side[here, :]], axis=0))
        at = slice(number % 2 * model, (number % 2 + 1) * model)
        if number < 2:
            a_ref[:, at] = total[:half]
            a_low_ref[:, at] = total[half:].astype(BF)
        else:
            b_ref[:part, at] = total[:part]
            b_ref[part:, at] = total[half : half + part]
            b_low_ref[:part, at] = total[part:half].astype(BF)
            b_low_ref[part:, at] = total[half + part :].astype(BF)


def fold_near_kernel(a_ref, a_got_ref, b_ref, b_got_ref, small_ref, small_got_ref, a2_ref, a2_low_ref, b2_ref, b2_low_ref):
    a = a_ref[...] + a_got_ref[...].astype(F32)
    b = b_ref[...] + b_got_ref[...].astype(F32)
    small = small_ref[...] + small_got_ref[...]
    half = a.shape[0] // 2
    a2_ref[...] = a[:half]
    a2_low_ref[:half, :] = a[half:].astype(BF)
    a2_low_ref[half:, :] = jnp.concatenate([small, jnp.zeros_like(small)], axis=1).astype(BF)
    b2_ref[...] = b[:half]
    b2_low_ref[...] = b[half:].astype(BF)


def fold_sums(a_ref, a_low_ref, a_got_ref, b_ref, b_got_ref):
    rows = a_ref.shape[0]
    a = a_ref[...] + a_got_ref[:rows, :].astype(F32)
    b = b_ref[...] + b_got_ref[...].astype(F32)
    model = a.shape[1] // 2
    return a, b, a_low_ref[rows:, :model].astype(F32) + a_got_ref[rows:, :model].astype(F32)


def fold_far_kernel(a_ref, a_low_ref, a_got_ref, b_ref, b_got_ref, keep_ref, *low_refs):
    a, b, small = fold_sums(a_ref, a_low_ref, a_got_ref, b_ref, b_got_ref)
    model = a.shape[1] // 2
    shard = a.shape[0] // 4
    for k in range(4):
        rows = slice(k * shard, (k + 1) * shard)
        blocks = [v[rows, half * model : (half + 1) * model] for v in (a, b) for half in range(2)]
        if k:
            low_refs[k - 1][...] = jnp.concatenate([small, *blocks], axis=0).astype(BF)
        else:
            keep_ref[...] = jnp.concatenate(blocks, axis=0)


def fold_last_kernel(keep_ref, own_ref, *refs):
    got, outs = [ref[...].astype(F32) for ref in refs[:3]], refs[3:]
    shard = outs[0].shape[0]
    first = outs[4].shape[0]
    total = keep_ref[...] + ((got[0][first:] + got[1][first:]) + got[2][first:])
    for number in range(4):
        outs[number][...] = total[number * shard : (number + 1) * shard]
    outs[4][...] = (own_ref[...][:first].astype(F32) + got[0][:first]) + (got[1][:first] + got[2][:first])


def score_grad_kernel(head, mixed_grad_ref, v_ref, q_ref, k_ref, probs_ref, grads_ref, along_ref):
    rows = q_ref.shape[0]
    flip = (
        lax.broadcasted_iota(jnp.int32, (rows, rows), 0) + lax.broadcasted_iota(jnp.int32, (rows, rows), 1)
        == rows - 1
    ).astype(F32).astype(BF)
    q_parts, k_parts = [], []
    for h in range(GROUP // head):
        part = slice(h * head, (h + 1) * head)
        probs = probs_ref[h]
        prob_grad = mm_nt(mixed_grad_ref[:, part], v_ref[:, part])
        inner = jnp.sum(probs * prob_grad, axis=-1, keepdims=True)
        score_grad = (probs * (prob_grad - inner)).astype(BF)
        q_parts.append(mm(score_grad, k_ref[:, part]))
        k_parts.append(mm_tn(score_grad, q_ref[:, part]))
        flipped = mm(flip, score_grad)
        half = rows // 2
        upper, lower = flipped[:half], flipped[half:]
        wide = jnp.concatenate(
            [upper[:, :half], upper[:, half:] + lower[:, :half], lower[:, half:], jnp.zeros_like(upper[:, :half])], axis=1
        )
        along_ref[h] = jnp.sum(pltpu.roll(wide, 0, 1, stride=1, stride_axis=0), axis=0, keepdims=True)
    grads_ref[:rows, :] = jnp.concatenate(q_parts, axis=1).astype(BF)
    grads_ref[rows:, :] = jnp.concatenate(k_parts, axis=1).astype(BF)


def input_kernel(table_rows, *refs):
    qk_ref, vo_ref, x_ref, gain_ref, perm_ref, middle_grad_ref = refs[:6]
    along_ref, buckets_ref, gain_next_ref, router_a_ref, router_b_ref = refs[6:11]
    qv_refs, wk_refs = refs[11:15], refs[15:19]
    input_grad_ref, small_ref, weight, wide = refs[19:]
    rows = x_ref.shape[0]
    experts, heads = router_a_ref.shape[0], along_ref.shape[0]
    every = table_rows
    onehot = (
        lax.broadcasted_iota(jnp.int32, (every, buckets_ref.shape[1]), 0) == buckets_ref[...]
    ).astype(F32)
    model = x_ref.shape[1]
    small_ref[...] = jnp.zeros_like(small_ref)
    small_ref[:experts, :] = router_a_ref[...] + router_b_ref[...]
    small_ref[experts + 1 : experts + 2, :] = gain_next_ref[...]
    along = jnp.concatenate([along_ref[h] for h in range(heads)], axis=0)
    table = lax.dot_general(
        along, onehot, (((1,), (1,)), ((), ())), precision=PRECISE, preferred_element_type=F32
    )
    small_ref[experts + 2 : experts + 3, : heads * every] = jnp.concatenate(
        [table[h : h + 1] for h in range(heads)], axis=1
    )
    fill_x_first(qv_refs, wide)
    total = mm_nt(jnp.concatenate([qk_ref[:rows, :], vo_ref[:rows, :]], axis=1), wide[...])
    fill_y_first(wk_refs, weight)
    total += mm_nt(qk_ref[rows:, :], weight[...])
    perm = perm_ref[...]
    high = total.astype(BF)
    low = (total - high.astype(F32)).astype(BF)
    normed_grad = mm_nt(high, perm) + mm_nt(low, perm)
    x = x_ref[...].astype(F32)
    scale = lax.rsqrt(jnp.mean(x * x, axis=-1, keepdims=True) + EPSILON)
    small_ref[experts : experts + 1, :] = jnp.sum(normed_grad * x * scale, axis=0, keepdims=True)
    scaled = normed_grad * gain_ref[...]
    along = jnp.mean(scaled * x, axis=-1, keepdims=True)
    input_grad_ref[...] = middle_grad_ref[...] + scale * scaled - x * (scale * scale * scale * along)


class Places:
    def __init__(self):
        self.experts = lax.axis_size("expert")
        self.nz = self.experts // 2
        self.dp = lax.axis_size("dp")
        self.near = self.nz == 4
        me = lax.axis_index("expert")
        self.z, self.c = me // 2, me % 2
        self.row = lax.axis_index("dp")
        self.columns = [[2 * z + c for z in range(self.nz)] for c in range(2)]

    def core(self, v):
        return lax.ppermute(v, "expert", [(i, i ^ 1) for i in range(self.experts)])

    def x(self, v):
        return lax.ppermute(v, "dp", [(i, i ^ 1) for i in range(self.dp)])

    def y(self, v):
        return lax.ppermute(v, "dp", [(i, i ^ 2) for i in range(self.dp)])

    def far(self, v, k):
        return lax.ppermute(v, "expert", [(i, i ^ (2 * k)) for i in range(self.experts)])

    def apart(self, v):
        return lax.all_to_all(
            v, "expert", split_axis=0, concat_axis=0, tiled=True, axis_index_groups=self.columns
        )

    def gather_z(self, v):
        if self.near:
            got = {k: self.far(v, k) for k in FAR_FIRST}
            return jnp.concatenate([v, got[1], got[2], got[3]], axis=0)
        return lax.all_gather(v, "expert", axis=0, tiled=True, axis_index_groups=self.columns)

    def z_order(self):
        steps = jnp.arange(self.nz, dtype=jnp.int32)
        return self.z ^ steps if self.near else steps

    def scatter_z(self, v):
        size = v.shape[0] // self.nz
        if self.near:
            total = v[:size]
            low = v.astype(BF)
            for k in FAR_FIRST:
                total = total + self.far(low[k * size : (k + 1) * size], k).astype(F32)
            return total
        got = self.apart(v.astype(BF).reshape(self.nz, size, v.shape[1]))
        mine = lax.dynamic_slice_in_dim(v, self.z * size, size, axis=0)
        steps = jnp.arange(self.nz, dtype=jnp.int32)[:, None, None]
        return mine + jnp.sum(jnp.where(steps == self.z, 0.0, got.astype(F32)), axis=0)

    def swap(self, blocks):
        got = {k: self.far(blocks[k], k) for k in FAR_FIRST}
        return [blocks[0], got[1], got[2], got[3]]

    def swap_relay(self, blocks, hold):
        size = blocks[0].shape[0]
        first = self.far(jnp.concatenate([blocks[2], blocks[3]], axis=0), 2)
        onward = after(jnp.concatenate([blocks[1], first[size:]], axis=0), *hold)
        second = self.far(onward, 1)
        return [blocks[0], second[:size], first[:size], second[size:]], onward

    def by_z(self, keep, got):
        room = keep.shape[0] // self.nz
        both = jnp.concatenate([v.reshape(self.nz, room, keep.shape[1]) for v in (keep, got)], axis=1)
        return [both[k] for k in range(4)] if self.near else both

    def halves(self, moved):
        moved = moved.reshape(-1, moved.shape[-1])
        half = moved.shape[0] // 2
        return [moved[:half]], [moved[half:]]

    def to_owners(self, keep, got, hold):
        blocks = self.by_z(keep, got)
        if self.near:
            blocks = all_after([blocks[k] for k in range(4)], *hold)
            two, one = self.far(blocks[2], 2), self.far(blocks[1], 1)
            three = self.far(after(blocks[3], two), 3)
            return [blocks[0], two], [one, three]
        return self.halves(self.apart(blocks))

    def send_more(self, blocks, k, hold):
        return self.far(after(blocks[k], *hold), k) if self.near else blocks

    def from_owners(self, first, second):
        width = first[0].shape[1]
        both = self.apart(jnp.concatenate([*first, *second], axis=0).reshape(self.nz, -1, width))
        room = both.shape[1] // 2
        return [both[:, :room].reshape(-1, width)], both[:, room:].reshape(-1, width)

    def to_senders(self, first, second):
        if self.near:
            two = self.far(first[1], 2)
            one, three = all_after(second, two)
            three, one = self.far(three, 3), self.far(one, 1)
            moved = [first[0], one, two, three]
            room = one.shape[0] // 2
            return moved, self.core(jnp.concatenate([v[room:] for v in moved], axis=0))
        keep, other = self.from_owners(first, second)
        return keep, self.core(other)

    def gather_far(self, a, b):
        return self.y(a), self.x(b)


def per_device(
    tokens,
    cotangent,
    routes,
    buckets,
    norm_attn,
    norm_ffn,
    rel_table,
    query_weight,
    key_weight,
    value_weight,
    out_weight,
    router_weight,
    expert_in,
    expert_out,
):
    at = Places()
    rows, model = tokens.shape
    head_count = rel_table.shape[1]
    head = model // head_count
    bucket_count = rel_table.shape[0]
    experts = router_weight.shape[1]
    shard = query_weight.shape[0]
    nz = at.nz
    room = max(2, 2 * rows // at.experts)
    slots = experts * room
    half = slots // 2
    groups = model // GROUP
    per_group = GROUP // head
    hidden = expert_in.shape[2]

    def in_hbm(*values):
        return [pltpu.with_memory_space_constraint(v, pltpu.HBM) for v in values]

    expert_in, expert_out = in_hbm(expert_in, expert_out)
    own = lax.axis_index("expert").astype(jnp.int32).reshape(1)
    smem = pl.BlockSpec(memory_space=pltpu.SMEM)

    core_of = at.c ^ jnp.arange(2, dtype=jnp.int32)
    row_of = at.row ^ jnp.arange(4, dtype=jnp.int32)
    device_of = (
        row_of[None, :, None] * at.experts + at.z_order()[None, None, :] * 2 + core_of[:, None, None]
    )
    order = (
        device_of[..., None] * shard + jnp.arange(shard, dtype=jnp.int32)
    ).reshape(1, model).astype(jnp.int32)

    shards = (query_weight, value_weight, key_weight, out_weight, router_weight)
    packed = pl.pallas_call(
        pack_kernel,
        out_shape=shape_of((shard, 4 * model + 128), BF),
        in_specs=[pl.BlockSpec(memory_space=pltpu.VMEM)] * 5,
        out_specs=pl.BlockSpec(memory_space=pltpu.VMEM),
        name="pack",
    )(*shards)
    line = at.gather_z(packed)
    span = 2 * rows
    bucket_line = jnp.pad(buckets, (0, 1), constant_values=-1).reshape(1, span)
    slots_map, slots_t, dy_keep, dy_send, perm, normed, picked, gain_attn, gain_ffn = pl.pallas_call(
        functools.partial(route_kernel, room, nz, at.near),
        out_shape=(
            shape_of((slots, rows), BF),
            shape_of((rows, slots), BF),
            shape_of((half, model), BF),
            shape_of((half + rows // 2, model), BF),
            shape_of((model, model), BF),
            shape_of((rows, model), BF),
            shape_of((rows, experts), F32),
            shape_of((1, model), F32),
            shape_of((1, model), F32),
        ),
        in_specs=[smem] + [pl.BlockSpec(memory_space=pltpu.VMEM)] * 6,
        compiler_params=params(),
        cost_estimate=cost(2 * rows * slots * model, 4 * rows * model),
        name="route",
    )(
        jnp.stack([at.z, at.c]).astype(jnp.int32),
        routes.reshape(1, rows),
        cotangent,
        order,
        tokens,
        norm_attn.reshape(1, model),
        norm_ffn.reshape(1, model),
    )
    dy_got = at.core(dy_send)
    normed_side = dy_got[half:]
    dy_got = dy_got[:half]
    qv, ko = line[:, : 2 * model], line[:, 2 * model :]
    qv, ko = all_after([qv, ko], dy_got)
    dy_keep, dy_got = all_after([dy_keep, dy_got], qv, ko)
    part_rows = qv.shape[0]
    dy_blocks = at.by_z(dy_keep, dy_got)
    dy_one = at.send_more(dy_blocks, 1, (dy_blocks,))
    qv_near, ko_near, both_near = pl.pallas_call(
        near_kernel,
        out_shape=tuple(shape_of((2 * part_rows, width), BF) for width in (2 * model, 2 * model + 128, 4 * model + 128)),
        in_specs=[pl.BlockSpec(memory_space=pltpu.VMEM)] * 4,
        out_specs=(pl.BlockSpec(memory_space=pltpu.VMEM),) * 3,
        compiler_params=params(),
        name="near",
    )(after(qv, dy_one), at.x(qv), ko, at.y(ko))
    bias = pl.pallas_call(
        bias_kernel,
        grid=(groups,),
        out_shape=shape_of((head_count, rows, rows), F32),
        in_specs=[full((1, span)), full((bucket_count, head_count))],
        out_specs=pl.BlockSpec((per_group, rows, rows), lambda g: (g, 0, 0)),
        scratch_shapes=[pltpu.VMEM((head_count, 1, span), F32)],
        compiler_params=params(),
        cost_estimate=cost(1 << 20, 4 * head_count * rows * rows),
        name="bias",
    )(after(bucket_line, qv, ko), rel_table)
    qv_far, ko_far = at.gather_far(*all_after([qv_near, ko_near], bias))
    both_side = at.core(both_near)
    dy_two = at.send_more(dy_blocks, 2, (qv_near, dy_one))
    qv_far, ko_far, dy_two = all_after([qv_far, ko_far, dy_two], both_side)
    dy_three = at.send_more(dy_blocks, 3, (qv_far, ko_far, dy_two))
    qv_pieces = (qv_near, qv_far, both_side, at.core(qv_far))
    ko_pieces = (ko_near, ko_far, both_side, at.core(ko_far))
    if at.near:
        dy_a = jnp.concatenate([dy_blocks[0], dy_two], axis=0)
    else:
        (dy_a,), (dy_b,) = at.halves(at.apart(dy_blocks))
    dy_a_later = after(dy_a, qv_far, ko_far)
    dy_ax, dy_ay = at.x(dy_a_later), at.y(dy_a_later)

    quarter = qv_near.shape[0]
    wide = ko_near.shape[1]
    side_wide = both_side.shape[1]
    head_block = pl.BlockSpec((per_group, rows, rows), lambda g: (g, 0, 0))
    later = pl.BlockSpec((quarter, GROUP), lambda g: (0, groups + g))
    side_k = pl.BlockSpec((quarter, GROUP), lambda g: (0, 2 * groups + g))
    first_k = cols(quarter, GROUP)
    ko_full = [full((quarter, wide)), full((quarter, wide)), full((quarter, side_wide)), full((quarter, wide))]
    q, k, v, probs, mixed, mixed_other, middle, router, gate, keep, send = pl.pallas_call(
        functools.partial(attend_kernel, head),
        grid=(groups,),
        out_shape=(shape_of((rows, model), BF),) * 3
        + (
            shape_of((head_count, rows, rows), F32),
            shape_of((rows, model // 2), BF),
            shape_of((rows, model // 2), BF),
            shape_of((rows, model), F32),
            shape_of((model, experts), BF),
            shape_of((rows, 1), F32),
            shape_of((half, model), BF),
            shape_of((half, model), BF),
        ),
        in_specs=[
            full((rows, model)),
            head_block,
            full((model, model)),
            full((rows, model)),
            full((1, model)),
            full((slots, rows)),
            full((rows, experts)),
        ]
        + [cols(quarter, GROUP)] * 4
        + [later] * 4
        + [first_k, first_k, side_k, first_k]
        + ko_full,
        out_specs=(cols(rows, GROUP),) * 3
        + (
            head_block,
            full((rows, model // 2)),
            full((rows, model // 2)),
            full((rows, model)),
            full((model, experts)),
            full((rows, 1)),
            full((half, model)),
            full((half, model)),
        ),
        scratch_shapes=[pltpu.VMEM((model, GROUP), BF)] * 3
        + [pltpu.VMEM((model, wide - model), BF), pltpu.VMEM((groups, rows, GROUP), BF)],
        compiler_params=params(),
        cost_estimate=cost(8 * rows * model * model, 12 * model * model),
        name="attend",
    )(normed, bias, perm, *in_hbm(tokens), gain_ffn, *in_hbm(slots_map), picked, *qv_pieces, *qv_pieces, *ko_pieces, *ko_pieces)

    got = at.core(after(send, dy_three))
    first, second = at.to_owners(keep, got, (dy_ax, dy_ay))
    if at.near:
        dy_b = jnp.concatenate([dy_one, dy_three], axis=0)
    dy_b_later = after(dy_b, got, dy_ax, dy_ay)
    dy_by, dy_bx = at.y(dy_b_later), at.x(dy_b_later)
    part = 1024

    def expert(rows_list, dy_rows, router_in, extra=()):
        sizes = [v.shape[0] for v in rows_list]
        count = sum(sizes)
        flat = [v for group in extra for v in group]
        joined = [sum(v.shape[0] for v in group) for group in extra]
        outs = pl.pallas_call(
            functools.partial(expert_kernel, len(sizes), tuple(len(group) for group in extra)),
            grid=(hidden // part,),
            out_shape=tuple(shape_of((n, model), BF) for n in sizes * 2)
            + (shape_of((experts, model), F32),)
            + tuple(shape_of((n, model), BF) for n in [count, *joined]),
            in_specs=[smem]
            + [full((n, model)) for n in [*sizes, count]]
            + [
                full((model, experts)),
                pl.BlockSpec((1, model, part), lambda f: (0, 0, f)),
                pl.BlockSpec((1, part, model), lambda f: (0, f, 0)),
            ]
            + [full(v.shape) for v in flat],
            out_specs=tuple(full((n, model)) for n in sizes * 2)
            + (full((experts, model)),)
            + tuple(full((n, model)) for n in [count, *joined]),
            scratch_shapes=[
                pltpu.VMEM((count, model), BF),
                pltpu.VMEM((count, experts), F32),
                pltpu.VMEM((count, 1), F32),
                pltpu.VMEM((count, model), F32),
                pltpu.VMEM((count, model), F32),
            ],
            compiler_params=params(),
            cost_estimate=cost(8 * count * model * hidden, 4 * model * hidden),
            name="expert",
        )(own, *rows_list, dy_rows, router_in, expert_in, expert_out, *flat)
        n = len(sizes)
        return list(outs[:n]), list(outs[n : 2 * n]), outs[2 * n], outs[2 * n + 1 :]

    dy_ax_later, dy_by_later = all_after([dy_ax, dy_by], first[-1], dy_bx)
    dy_axy, dy_byx = at.y(dy_ax_later), at.x(dy_by_later)
    back_a, returned_a, router_grad_a, (rows_a,) = expert(first, dy_a, after(router, dy_by, dy_bx))
    rows_ax, rows_ay = at.x(rows_a), at.y(rows_a)
    back_b, returned_b, router_grad_b, (rows_b,) = expert(second, dy_b, after(router, router_grad_a, dy_axy, dy_byx))
    rows_b_later = after(rows_b, rows_ax, rows_ay)
    rows_by, rows_bx = at.y(rows_b_later), at.x(rows_b_later)
    back_keep, back_send = at.to_senders(back_a, back_b)

    slice_width = hidden // at.dp
    place = at.row.astype(jnp.int32).reshape(1)

    steps = slice_width // GROUP

    def expert_grads(rows_list, dy_list, router_in, before):
        sizes = [v.shape[0] for v in rows_list]
        count = sum(sizes)
        outs = (
            pl.BlockSpec((1, model, GROUP), lambda g, place: (0, 0, g)),
            pl.BlockSpec((1, GROUP, model), lambda g, place: (0, g, 0)),
        )
        return pl.pallas_call(
            functools.partial(expert_grad_kernel, len(sizes), bool(before)),
            grid_spec=pltpu.PrefetchScalarGridSpec(
                num_scalar_prefetch=1,
                grid=(steps,),
                in_specs=[full((n, model)) for n in sizes * 2]
                + [
                    smem,
                    full((model, experts)),
                    pl.BlockSpec((1, model, GROUP), lambda g, place: (0, 0, place[0] * steps + g)),
                    pl.BlockSpec((1, GROUP, model), lambda g, place: (0, place[0] * steps + g, 0)),
                ]
                + list(outs if before else ()),
                out_specs=outs,
                scratch_shapes=[pltpu.VMEM((count, model), BF), pltpu.VMEM((count, model), BF)],
            ),
            out_shape=(pltpu.HBM((1, model, slice_width), F32), pltpu.HBM((1, slice_width, model), F32)),
            compiler_params=params(),
            cost_estimate=cost(8 * count * model * slice_width, 20 * model * slice_width),
            name="expert_grads",
        )(place, *in_hbm(*rows_list, *dy_list), own, router_in, expert_in, expert_out, *before)

    rows_axy, rows_byx = at.y(after(rows_ax, rows_by, rows_bx, back_send)), at.x(after(rows_by, rows_bx, back_send))

    middle_grad, gain_ffn_grad, mixed_grad, vo_grads = pl.pallas_call(
        functools.partial(middle_kernel, head, len(back_keep)),
        grid=(groups,),
        out_shape=(
            shape_of((rows, model), F32),
            shape_of((1, model), F32),
            shape_of((rows, model), BF),
            shape_of((2 * rows + rows // 2, model), BF),
        ),
        in_specs=[full(v.shape) for v in back_keep]
        + [
            full((half, model)),
            full((rows, slots)),
            full((rows, model)),
            full((rows, model)),
            full((1, model)),
            full((model, model)),
            head_block,
            full((rows, model // 2)),
        ]
        + ko_full,
        out_specs=(
            full((rows, model)),
            full((1, model)),
            full((rows, model)),
            full((2 * rows + rows // 2, model)),
        ),
        scratch_shapes=[pltpu.VMEM((model, model), BF), pltpu.VMEM((groups, rows, GROUP), BF)],
        compiler_params=params(),
        cost_estimate=cost(10 * rows * model * model, 12 * model * model),
        name="middle",
    )(*back_keep, back_send, slots_t, cotangent, middle, after(gain_ffn, rows_by, rows_bx), perm, probs, mixed_other, *ko_pieces)
    vo_side = at.core(vo_grads)
    qk_grads, along_grad = pl.pallas_call(
        functools.partial(score_grad_kernel, head),
        grid=(groups,),
        out_shape=(shape_of((2 * rows, model), BF), shape_of((head_count, 1, span), F32)),
        in_specs=[cols(rows, GROUP)] * 4 + [head_block],
        out_specs=(cols(2 * rows, GROUP), pl.BlockSpec((per_group, 1, span), lambda g: (g, 0, 0))),
        compiler_params=params(),
        cost_estimate=cost(8 * rows * model * model, 12 * model * model),
        name="score_grads",
    )(mixed_grad, v, q, k, probs)
    qk_side = at.core(after(qk_grads, vo_side, rows_axy, rows_byx))
    small_rows = -(-(experts + 3) // 16) * 16
    input_grad, small = pl.pallas_call(
        functools.partial(input_kernel, bucket_count),
        grid=(1,),
        out_shape=(shape_of((rows, model), F32), shape_of((small_rows, model), F32)),
        in_specs=[full((2 * rows, model)), full((2 * rows + rows // 2, model))]
        + [full((rows, model)), full((1, model)), full((model, model)), full((rows, model))]
        + [full((head_count, 1, span)), full((1, span)), full((1, model))]
        + [full((experts, model))] * 2
        + [full((quarter, 2 * model))] * 4
        + [pl.BlockSpec((quarter, model), lambda g, at=at_k: (0, at)) for at_k in (0, 0, 2, 0)],
        out_specs=(full((rows, model)), full((small_rows, model))),
        scratch_shapes=[pltpu.VMEM((model, model), BF), pltpu.VMEM((model, 2 * model), BF)],
        compiler_params=params(),
        cost_estimate=cost(10 * rows * model * model, 12 * model * model),
        name="inputs",
    )(
        qk_grads,
        vo_grads,
        tokens,
        gain_attn,
        perm,
        middle_grad,
        along_grad,
        bucket_line,
        gain_ffn_grad,
        router_grad_a,
        router_grad_b,
        *qv_pieces,
        *ko_pieces,
    )
    quarter_rows = model // 4

    def vmem_call(kernel, name, shapes, *ins):
        return pl.pallas_call(
            kernel,
            out_shape=tuple(shape_of(*v) for v in shapes),
            in_specs=[pl.BlockSpec(v.shape, lambda: (0, 0)) for v in ins],
            out_specs=tuple(pl.BlockSpec(v[0], lambda: (0, 0)) for v in shapes),
            compiler_params=params(),
            name=name,
        )(*ins)

    pair = 2 * model
    a, a_low, b, b_low = vmem_call(
        weight_grad_kernel,
        "weight_grads",
        [((quarter_rows, pair), F32), ((quarter_rows, pair), BF)] * 2,
        normed,
        normed_side,
        mixed,
        vo_grads,
        vo_side,
        qk_grads,
        qk_side,
    )
    small = small + after(at.core(small), a_low)
    a_got, b_got = at.y(a_low), at.x(b_low)
    small_got = at.y(small)
    if at.near:
        home_two = at.far(after(returned_a[1], a_low, b_low), 2)
    else:
        home_two = at.apart(jnp.concatenate([*returned_a, *returned_b], axis=0).reshape(nz, -1, model))
    near_sums = expert_grads(
        [rows_a, rows_b, rows_ax, rows_by, rows_ay, rows_bx],
        [dy_a, dy_b, dy_ax, dy_by, dy_ay, dy_bx],
        after(router, a_low, b_low),
        (),
    )
    eighth = quarter_rows // 2
    a, a_low, b, b_low = vmem_call(
        fold_near_kernel,
        "fold_near",
        [((eighth, pair), F32), ((eighth + small_rows, pair), BF), ((eighth, pair), F32), ((eighth, pair), BF)],
        a,
        after(a_got, near_sums[0], home_two),
        b,
        b_got,
        small,
        small_got,
    )
    a_got, b_got = at.x(a_low), at.y(b_low)
    far_sums = expert_grads(
        [rows_axy, rows_byx],
        [dy_axy, dy_byx],
        after(router, a_low, b_low),
        near_sums,
    )
    if at.near:
        home = [at.far(v, k) for v, k in zip(all_after([returned_b[1], returned_b[0]], a_low, b_low), (3, 1))]
        home_blocks = [returned_a[0], home[1], home_two, home[0]]
        room = half // nz
        returned_keep = home_blocks
        returned_other = jnp.concatenate([v[room:] for v in home_blocks], axis=0)
    else:
        room = home_two.shape[1] // 2
        returned_keep = [home_two[:, :room].reshape(half, model)]
        returned_other = home_two[:, room:].reshape(half, model)
    if at.near:
        keep_sum, *low = vmem_call(
            fold_far_kernel,
            "fold_far",
            [((4 * shard, model), F32)] + [((small_rows + 4 * shard, model), BF)] * 3,
            a,
            a_low,
            after(a_got, far_sums[0], *home),
            b,
            b_got,
        )
        hold = keep_sum
        got_z = {k: at.far(low[k - 1], k) for k in FAR_FIRST}
    else:
        a = a + a_got[:eighth].astype(F32)
        b = b + b_got.astype(F32)
        summed = (a_low[eighth:].astype(F32) + a_got[eighth:].astype(F32))[:, :model]
        hold = jnp.concatenate([a, b], axis=1)
        sums = at.scatter_z(hold)
        grad_value, grad_query, grad_proj, grad_key = [sums[:, n * model : (n + 1) * model] for n in range(4)]
        summed = lax.psum(summed, "expert", axis_index_groups=at.columns)
    returned_send = at.core(after(returned_other, hold))
    grad_in, grad_out_w = far_sums
    keep_rows = half // len(returned_keep)
    expert_result = mm(
        slots_t,
        jnp.concatenate([v[:keep_rows] for v in returned_keep] + [returned_send], axis=0),
    )
    output = (middle + gate * expert_result).astype(BF)
    if at.near:
        grad_value, grad_query, grad_proj, grad_key, summed = vmem_call(
            fold_last_kernel,
            "fold_last",
            [((shard, model), F32)] * 4 + [((small_rows, model), F32)],
            after(keep_sum, output),
            low[0],
            *[got_z[k] for k in (1, 2, 3)],
        )
    device = at.row * at.experts + lax.axis_index("expert")
    grad_router = lax.dynamic_slice_in_dim(summed[:experts], device * shard, shard, axis=1).T
    return (
        output,
        input_grad,
        summed[experts],
        summed[experts + 1],
        summed[experts + 2, : head_count * bucket_count].reshape(head_count, bucket_count).T,
        grad_query,
        grad_key,
        grad_value,
        grad_proj,
        grad_router,
        grad_in,
        grad_out_w,
    )


def solution(mesh):
    in_specs = (
        P(("dp", "expert"), None),
        P(("dp", "expert"), None),
        P(("dp", "expert"), None),
        P(),
        P(),
        P(),
        P(),
        P(("dp", "expert"), None),
        P(("dp", "expert"), None),
        P(("dp", "expert"), None),
        P(("dp", "expert"), None),
        P(("dp", "expert"), None),
        P("expert", None, None),
        P("expert", None, None),
    )
    out_specs = (
        P(("dp", "expert"), None),
        P(("dp", "expert"), None),
        P(),
        P(),
        P(),
        P(("dp", "expert"), None),
        P(("dp", "expert"), None),
        P(("dp", "expert"), None),
        P(("dp", "expert"), None),
        P(("dp", "expert"), None),
        P("expert", None, "dp"),
        P("expert", "dp", None),
    )
    return jax.shard_map(
        per_device, mesh=mesh, in_specs=in_specs, out_specs=out_specs, check_vma=False
    )
```

time: 310 us -> 201 us (0.65)
  starting transfers between devices: 95.2 us -> 51.8 us
  waiting for transfers between devices: 95 us -> 56.8 us
  Pallas kernels: 88.7 us -> 70.2 us
  other arithmetic: 9 us -> 3.39 us
    ppermute x27 -> x18, starting transfers between devices: 58.7 us -> 28.6 us  [far(): lax.ppermute(v, 'expert', [(i, i ^ 2 * k) for i in range(self.experts)])]
    ppermute x13 -> x11, waiting for transfers between devices: 24.8 us -> 4.93 us  [y(): return lax.ppermute(v, 'dp', [(i, i ^ 2) for i in range(self.dp)])]
    pallas_call x8 -> x15, Pallas kernels: 79.6 us -> 64.6 us  [the longest x2 22.1 us: expert_grads(): pl.pallas_call(functools.partial(expert_grad_kernel, len(sizes), bool(bef...]
    ppermute x13 -> x10, waiting for transfers between devices: 18 us -> 5.37 us  [x(): return lax.ppermute(v, 'dp', [(i, i ^ 1) for i in range(self.dp)])]
    ppermute x27 -> x18, waiting for transfers between devices: 52.1 us -> 43.5 us  [far(): lax.ppermute(v, 'expert', [(i, i ^ 2 * k) for i in range(self.experts)])]
    ppermute x13 -> x10, starting transfers between devices: 17.2 us -> 9.78 us  [x(): return lax.ppermute(v, 'dp', [(i, i ^ 1) for i in range(self.dp)])]
    slice x18 -> x13, local copies, waits for them, and re-layouts: 6 us -> 1.88 us  [the longest x1 1.12 us: per_device(): normed_side = dy_got[half:]]
    ppermute x13 -> x11, starting transfers between devices: 16.1 us -> 12.6 us  [y(): return lax.ppermute(v, 'dp', [(i, i ^ 2) for i in range(self.dp)])]
  transfers between devices with their start and end apart: 68 -> 49, of which waited for: 28 -> 20; matrix products, arithmetic and copies ran while one was open for 6% -> 4% of each run, Pallas kernels for 15% -> 31%
where the time goes in v2:
time: 201 us; the launch traced here: 200 us
  Pallas kernels  70.2 us (35%)
  waiting for transfers between devices  56.8 us (28%)
  starting transfers between devices  51.8 us (26%)
  local copies, waits for them, and re-layouts  15.1 us (8%)
  other arithmetic  3.39 us (2%)
    ppermute x18, waiting for transfers between devices, far(): lax.ppermute(v, 'expert', [(i, i ^ 2 * k) for i in range(self.experts)])  43.5 us
    ppermute x18, starting transfers between devices, far(): lax.ppermute(v, 'expert', [(i, i ^ 2 * k) for i in range(self.experts)])  28.6 us
    pallas_call x2, Pallas kernels, expert_grads(): pl.pallas_call(functools.partial(expert_grad_kernel, len(sizes), bool(bef...  22.1 us
    pallas_call x2, Pallas kernels, expert(): pl.pallas_call(functools.partial(expert_kernel, len(sizes), tuple((len(gr...  18.5 us
    ppermute x11, starting transfers between devices, y(): return lax.ppermute(v, 'dp', [(i, i ^ 2) for i in range(self.dp)])  12.6 us
    ppermute x10, starting transfers between devices, x(): return lax.ppermute(v, 'dp', [(i, i ^ 1) for i in range(self.dp)])  9.78 us
    unnamed x89, local copies, waits for them, and re-layouts  9.4 us
    pallas_call x1, Pallas kernels, per_device(): pl.pallas_call(functools.partial(attend_kernel, head), grid=(groups,), ou...  8.73 us
  transfers between devices with their start and end apart: 49, of which 20 were waited for; matrix products, arithmetic and copies ran while one was open for 4% of the time, Pallas kernels for 31%

profile of v2, /device:TPU:0, one launch (start us, length us, event | category | flops | bytes accessed | tf_op | source)
XLA Modules:
  0.0 199.8 jit_solution(11607543616471196227)
XLA Ops:
  3.5 3.0 %collective-permute-start = (bf16[24,3200]{1,0:T(8,128)(2,1)}, bf16[24,3200]{1,0:T(8,128)(2,1)S(1)}, u32[]{:S(2)}, u32[]{:S(2)}) collective-permute-start(bf16[24,3200]{1,0:T(8,128)(2,1)} %pack.1), channel_id=1, source_target_pairs={{0,2},{1,3},{2,0},{3,1},{4,6},{5,7},{6,4},{7,5},{8,10},{9,11},{10,... | collective-permute-start | bytes 460808 | tf_op jit(solution)/shard_map/ppermute | solution.py:531
  6.5 2.6 %collective-permute-start.1 = (bf16[24,3200]{1,0:T(8,128)(2,1)}, bf16[24,3200]{1,0:T(8,128)(2,1)}, u32[]{:S(2)}, u32[]{:S(2)}) collective-permute-start(bf16[24,3200]{1,0:T(8,128)(2,1)} %pack.1), channel_id=1, source_target_pairs={{0,4},{1,5},{2,6},{3,7},{4,0},{5,1},{6,2},{7,3},{8,12},{9,13},{10,... | collective-permute-start | bytes 460808 | tf_op jit(solution)/shard_map/ppermute | solution.py:531
  13.6 1.6 route.1
  15.9 5.3 %collective-permute-done.1 = bf16[24,3200]{1,0:T(8,128)(2,1)} collective-permute-done((bf16[24,3200]{1,0:T(8,128)(2,1)}, bf16[24,3200]{1,0:T(8,128)(2,1)}, u32[]{:S(2)}, u32[]{:S(2)}) %collective-permute-start.1) | collective-permute-done | bytes 153632 | tf_op jit(solution)/shard_map/ppermute | solution.py:531
  24.1 1.5 collective-permute-start.6
  27.9 2.4 %collective-permute-start.4 = (bf16[128,768]{1,0:T(8,128)(2,1)S(1)}, bf16[128,768]{1,0:T(8,128)(2,1)S(1)}, u32[]{:S(2)}, u32[]{:S(2)}) collective-permute-start(bf16[128,768]{1,0:T(8,128)(2,1)S(1)} %get-tuple-element.131), channel_id=1, source_target_pairs={{0,2},{1,3},{2,0},{3,1},{4,6},{5,7},{6,4},{7,5},{8,10},{9,11},{10,... | collective-permute-start | bytes 589832 | tf_op jit(solution)/shard_map/ppermute | solution.py:531
  30.4 3.6 %collective-permute-done.4 = bf16[128,768]{1,0:T(8,128)(2,1)S(1)} collective-permute-done((bf16[128,768]{1,0:T(8,128)(2,1)S(1)}, bf16[128,768]{1,0:T(8,128)(2,1)S(1)}, u32[]{:S(2)}, u32[]{:S(2)}) %collective-permute-start.4) | collective-permute-done | bytes 196640 | tf_op jit(solution)/shard_map/ppermute | solution.py:531
  39.4 3.1 %collective-permute-start.9 = (bf16[128,768]{1,0:T(8,128)(2,1)S(1)}, bf16[128,768]{1,0:T(8,128)(2,1)S(1)}, u32[]{:S(2)}, u32[]{:S(2)}) collective-permute-start(bf16[128,768]{1,0:T(8,128)(2,1)S(1)} %copy-done.38), channel_id=1, source_target_pairs={{0,4},{1,5},{2,6},{3,7},{4,0},{5,1},{6,2},{7,3},{8,12},{9,13},{10,... | collective-permute-start | bytes 589832 | tf_op jit(solution)/shard_map/ppermute | solution.py:531
  42.5 9.2 %collective-permute-done.9 = bf16[128,768]{1,0:T(8,128)(2,1)S(1)} collective-permute-done((bf16[128,768]{1,0:T(8,128)(2,1)S(1)}, bf16[128,768]{1,0:T(8,128)(2,1)S(1)}, u32[]{:S(2)}, u32[]{:S(2)}) %collective-permute-start.9) | collective-permute-done | bytes 196640 | tf_op jit(solution)/shard_map/ppermute | solution.py:531
  51.8 2.6 %collective-permute-done.7.refs_8_.refs_12_ = bf16[192,1536]{1,0:T(8,128)(2,1)S(1)} collective-permute-done((bf16[192,1536]{1,0:T(8,128)(2,1)S(1)}, bf16[192,1536]{1,0:T(8,128)(2,1)S(1)}, u32[]{:S(2)}, u32[]{:S(2)}) %collective-permute-start.7) | collective-permute-done | bytes 589856 | tf_op jit(solution)/shard_map/ppermute | solution.py:528
  55.7 2.5 %collective-permute-start.13 = (bf16[128,768]{1,0:T(8,128)(2,1)S(1)}, bf16[128,768]{1,0:T(8,128)(2,1)S(1)}, u32[]{:S(2)}, u32[]{:S(2)}) collective-permute-start(bf16[128,768]{1,0:T(8,128)(2,1)S(1)} %copy-done.37), channel_id=1, source_target_pairs={{0,6},{1,7},{2,4},{3,5},{4,2},{5,3},{6,0},{7,1},{8,14},{9,15},{10,... | collective-permute-start | bytes 589832 | tf_op jit(solution)/shard_map/ppermute | solution.py:531
  59.5 8.7 %attend.1 = (bf16[256,768]{1,0:T(8,128)(2,1)S(1)}, bf16[256,768]{1,0:T(8,128)(2,1)S(1)}, bf16[256,768]{1,0:T(8,128)(2,1)S(1)}, f32[12,256,256]{2,1,0:T(8,128)S(1...) custom-call(bf16[256,768]{1,0:T(8,128)(2,1)S(1)} %get-tuple-element., ...), custom_call_target="tpu_custom_call" | custom-call | flops 1024 | bytes 1024 | tf_op jit(solution)/shard_map/attend/pallas_call | solution.py:749
  74.0 10.5 %collective-permute-done.17.refs_1_ = bf16[128,768]{1,0:T(8,128)(2,1)S(1)} collective-permute-done((bf16[128,768]{1,0:T(8,128)(2,1)S(1)}, bf16[128,768]{1,0:T(8,128)(2,1)S(1)}, u32[]{:S(2)}, u32[]{:S(2)}) %collective-permute-start.17) | collective-permute-done | bytes 196640 | tf_op jit(solution)/shard_map/ppermute | solution.py:531
  87.2 9.2 %expert.2 = (bf16[128,768]{1,0:T(8,128)(2,1)S(1)}, bf16[128,768]{1,0:T(8,128)(2,1)S(1)}, bf16[128,768]{1,0:T(8,128)(2,1)S(1)}, bf16[128,768]{1,0:T(8,128)(2,1)S(...) custom-call(s32[1]{0:T(128)} %bitcast.10.own_ref.refs_12_.refs_4_, ...), custom_call_target="tpu_custom_call" | custom-call | flops 1024 | bytes 1024 | tf_op jit(solution)/shard_map/expert/pallas_call | solution.py:807
  97.9 1.5 collective-permute-start.29
  99.4 2.1 %collective-permute-start.24 = (bf16[128,768]{1,0:T(8,128)(2,1)S(1)}, bf16[128,768]{1,0:T(8,128)(2,1)S(1)}, u32[]{:S(2)}, u32[]{:S(2)}) collective-permute-start(bf16[128,768]{1,0:T(8,128)(2,1)S(1)} %get-tuple-element.169), channel_id=1, source_target_pairs={{0,4},{1,5},{2,6},{3,7},{4,0},{5,1},{6,2},{7,3},{8,12},{9,13},{10,... | collective-permute-start | bytes 589832 | tf_op jit(solution)/shard_map/ppermute | solution.py:531
  101.5 9.3 %expert.3 = (bf16[128,768]{1,0:T(8,128)(2,1)S(1)}, bf16[128,768]{1,0:T(8,128)(2,1)S(1)}, bf16[128,768]{1,0:T(8,128)(2,1)S(1)}, bf16[128,768]{1,0:T(8,128)(2,1)S(...) custom-call(s32[1]{0:T(128)} %bitcast.10.own_ref.refs_12_.refs_4_, ...), custom_call_target="tpu_custom_call" | custom-call | flops 1024 | bytes 1024 | tf_op jit(solution)/shard_map/expert/pallas_call | solution.py:807
  114.5 3.7 %collective-permute-done.25.refs_1_ = bf16[128,768]{1,0:T(8,128)(2,1)S(1)} collective-permute-done((bf16[128,768]{1,0:T(8,128)(2,1)S(1)}, bf16[128,768]{1,0:T(8,128)(2,1)S(1)}, u32[]{:S(2)}, u32[]{:S(2)}) %collective-permute-start.25) | collective-permute-done | bytes 196640 | tf_op jit(solution)/shard_map/ppermute | solution.py:531
  118.2 2.1 %collective-permute-done.26.refs_3_ = bf16[128,768]{1,0:T(8,128)(2,1)S(1)} collective-permute-done((bf16[128,768]{1,0:T(8,128)(2,1)S(1)}, bf16[128,768]{1,0:T(8,128)(2,1)S(1)}, u32[]{:S(2)}, u32[]{:S(2)}) %collective-permute-start.26) | collective-permute-done | bytes 196640 | tf_op jit(solution)/shard_map/ppermute | solution.py:531
  122.2 3.1 %middle.1 = (f32[256,768]{1,0:T(8,128)S(1)}, f32[1,768]{1,0:T(1,128)S(1)}, bf16[256,768]{1,0:T(8,128)(2,1)S(1)}, bf16[640,768]{1,0:T(8,128)(2,1)S(1)}) custom-call(bf16[128,768]{1,0:T(8,128)(2,1)S(1)} %get-tuple-element.166.refs_0_, bf16[128,768]{1,0:T(8,128)(2,1)S(1)} %collective-permute-done.25.refs_1_, ...), custom_call_target="tpu_custom_call" | custom-call | flops 1024 | bytes 1024 | tf_op jit(solution)/shard_map/middle/pallas_call | solution.py:883
  127.6 5.6 %score_grads.1 = (bf16[512,768]{1,0:T(8,128)(2,1)S(1)}, f32[12,1,512]{2,1,0:T(1,128)S(1)}) custom-call(bf16[256,768]{1,0:T(8,128)(2,1)S(1)} %get-tuple-element.179.mixed_grad_ref, bf16[256,768]{1,0:T(8,128)(2,1)S(1)} %get-tuple-element.180.v_ref, bf16[256,768]{1,0:T(8,128)(2,1)S(1)} %get-tuple-element.181.q_ref, ...), custom_call_target="tpu_custom_call" | custom-call | flops 1024 | bytes 1024 | tf_op jit(solution)/shard_map/score_grads/pallas_call | solution.py:916
  133.2 3.7 %collective-permute-done.34.refs_1_ = bf16[256,768]{1,0:T(8,128)(2,1)S(1)} collective-permute-done((bf16[256,768]{1,0:T(8,128)(2,1)S(1)}, bf16[256,768]{1,0:T(8,128)(2,1)S(1)}, u32[]{:S(2)}, u32[]{:S(2)}) %collective-permute-start.34) | collective-permute-done | bytes 393248 | tf_op jit(solution)/shard_map/ppermute | solution.py:525
  145.0 3.9 %inputs.1 = (f32[256,768]{1,0:T(8,128)}, f32[16,768]{1,0:T(8,128)S(1)}) custom-call(bf16[512,768]{1,0:T(8,128)(2,1)S(1)} %get-tuple-element.186.qk_ref.refs_0_, bf16[640,768]{1,0:T(8,128)(2,1)S(1)} %get-tuple-element.178.vo_ref.refs_1_, bf16[256,768]{1,0:T(8,128)(2,1)S(1)} %copy-done.4, f32[1,768]{1,0:T(1,128)S(1)} %get-tuple-element.196.refs_3_, ...), custom_call_target="tpu_custom_call" | custom-call | flops 1024 | bytes 1024 | tf_op jit(solution)/shard_map/inputs/pallas_call | solution.py:928
  150.1 1.6 collective-permute-start.40
  151.7 14.4 %expert_grads.2 = (f32[1,768,768]{2,1,0:T(8,128)}, f32[1,768,768]{2,1,0:T(8,128)}) custom-call(s32[1]{0:T(128)} %bitcast.17.place_ref, bf16[256,768]{1,0:T(8,128)(2,1)} %copy-done.15, bf16[256,768]{1,0:T(8,128)(2,1)} %copy-done.16, bf16[256,768]{1,0:T(8,128)(2,1)} %copy-done.29, bf16[256,768]{1,0:T(8,128)(2,1)} %copy-done.31, bf16[256,768]{1,0:T(8,128)(2,1)} %copy-done.30, ...), custom_call_target="tpu_custom_call" | custom-call | flops 1024 | bytes 1024 | tf_op jit(solution)/shard_map/expert_grads/pallas_call | solution.py:859
  169.5 1.7 collective-permute-start.42
  171.2 1.7 copy-done.9
  172.8 7.6 %expert_grads.3 = (f32[1,768,768]{2,1,0:T(8,128)}, f32[1,768,768]{2,1,0:T(8,128)}) custom-call(s32[1]{0:T(128)} %bitcast.17.place_ref, bf16[256,768]{1,0:T(8,128)(2,1)} %copy-done.36, bf16[256,768]{1,0:T(8,128)(2,1)} %copy-done.35, bf16[256,768]{1,0:T(8,128)(2,1)} %copy-done.33, bf16[256,768]{1,0:T(8,128)(2,1)} %copy-done.34, ...), custom_call_target="tpu_custom_call" | custom-call | flops 1024 | bytes 1024 | tf_op jit(solution)/shard_map/expert_grads/pallas_call | solution.py:859
  181.5 2.7 %collective-permute-start.47 = (bf16[112,768]{1,0:T(8,128)(2,1)S(1)}, bf16[112,768]{1,0:T(8,128)(2,1)S(1)}, u32[]{:S(2)}, u32[]{:S(2)}) collective-permute-start(bf16[112,768]{1,0:T(8,128)(2,1)S(1)} %get-tuple-element.218), channel_id=1, source_target_pairs={{0,4},{1,5},{2,6},{3,7},{4,0},{5,1},{6,2},{7,3},{8,12},{9,13},{10,... | collective-permute-start | bytes 516104 | tf_op jit(solution)/shard_map/ppermute | solution.py:531
  184.2 1.7 collective-permute-start.48
  188.1 2.6 %collective-permute-done.46.refs_0_ = bf16[112,768]{1,0:T(8,128)(2,1)S(1)} collective-permute-done((bf16[112,768]{1,0:T(8,128)(2,1)S(1)}, bf16[112,768]{1,0:T(8,128)(2,1)S(1)}, u32[]{:S(2)}, u32[]{:S(2)}) %collective-permute-start.46) | collective-permute-done | bytes 172064 | tf_op jit(solution)/shard_map/ppermute | solution.py:531
  190.7 6.4 %collective-permute-done.47.refs_1_ = bf16[112,768]{1,0:T(8,128)(2,1)S(1)} collective-permute-done((bf16[112,768]{1,0:T(8,128)(2,1)S(1)}, bf16[112,768]{1,0:T(8,128)(2,1)S(1)}, u32[]{:S(2)}, u32[]{:S(2)}) %collective-permute-start.47) | collective-permute-done | bytes 172064 | tf_op jit(solution)/shard_map/ppermute | solution.py:531
  (208 shorter events, 57.1 us)
Async XLA Ops:
  3.5 12.4 %collective-permute-start = (bf16[24,3200]{1,0:T(8,128)(2,1)}, bf16[24,3200]{1,0:T(8,128)(2,1)S(1)}, u32[]{:S(2)}, u32[]{:S(2)}) collective-permute-start(bf16[24,3200]{1,0:T(8,128)(2,1)} %pack.1), channel_id=1, source_target_pairs={{0,2},{1,3},{2,0},{3,1},{4,6},{5,7},{6,4},{7,5},{8,10},{9,11},{10,... | collective-permute-start | bytes 460808 | tf_op jit(solution)/shard_map/ppermute | solution.py:531
  6.5 14.7 %collective-permute-start.1 = (bf16[24,3200]{1,0:T(8,128)(2,1)}, bf16[24,3200]{1,0:T(8,128)(2,1)}, u32[]{:S(2)}, u32[]{:S(2)}) collective-permute-start(bf16[24,3200]{1,0:T(8,128)(2,1)} %pack.1), channel_id=1, source_target_pairs={{0,4},{1,5},{2,6},{3,7},{4,0},{5,1},{6,2},{7,3},{8,12},{9,13},{10,... | collective-permute-start | bytes 460808 | tf_op jit(solution)/shard_map/ppermute | solution.py:531
  9.1 12.1 %collective-permute-start.2 = (bf16[24,3200]{1,0:T(8,128)(2,1)}, bf16[24,3200]{1,0:T(8,128)(2,1)}, u32[]{:S(2)}, u32[]{:S(2)}) collective-permute-start(bf16[24,3200]{1,0:T(8,128)(2,1)} %pack.1), channel_id=1, source_target_pairs={{0,6},{1,7},{2,4},{3,5},{4,2},{5,3},{6,0},{7,1},{8,14},{9,15},{10,... | collective-permute-start | bytes 460808 | tf_op jit(solution)/shard_map/ppermute | solution.py:531
  36.7 18.5 %collective-permute-start.10 = (bf16[192,3200]{1,0:T(8,128)(2,1)}, bf16[192,3200]{1,0:T(8,128)(2,1)S(1)}, u32[]{:S(2)}, u32[]{:S(2)}) collective-permute-start(bf16[192,3200]{1,0:T(8,128)(2,1)} %get-tuple-element.138), channel_id=1, source_target_pairs={{0,1},{1,0},{2,3},{3,2},{4,5},{5,4},{6,7},{7,6},{8,9},{9,8},{10,11... | collective-permute-start | bytes 3686408 | tf_op jit(solution)/shard_map/ppermute | solution.py:522
  38.3 16.9 %collective-permute-start.8 = (bf16[192,1664]{1,0:T(8,128)(2,1)S(1)}, bf16[192,1664]{1,0:T(8,128)(2,1)S(1)}, u32[]{:S(2)}, u32[]{:S(2)}) collective-permute-start(bf16[192,1664]{1,0:T(8,128)(2,1)S(1)} %get-tuple-element.136.refs_15_.refs_19_.refs_12_), channel_id=1, source_target_pairs={{0,8},{8,0},{16,24},{24,16},{1,9},{9,1},{17,25},{25,17},{2,10},{10... | collective-permute-start | bytes 1916936 | tf_op jit(solution)/shard_map/ppermute | solution.py:525
  38.9 15.5 %collective-permute-start.7 = (bf16[192,1536]{1,0:T(8,128)(2,1)S(1)}, bf16[192,1536]{1,0:T(8,128)(2,1)S(1)}, u32[]{:S(2)}, u32[]{:S(2)}) collective-permute-start(bf16[192,1536]{1,0:T(8,128)(2,1)S(1)} %copy-done.1), channel_id=1, source_target_pairs={{0,16},{8,24},{16,0},{24,8},{1,17},{9,25},{17,1},{25,9},{2,18},{10... | collective-permute-start | bytes 1769480 | tf_op jit(solution)/shard_map/ppermute | solution.py:528
  39.4 12.3 %collective-permute-start.9 = (bf16[128,768]{1,0:T(8,128)(2,1)S(1)}, bf16[128,768]{1,0:T(8,128)(2,1)S(1)}, u32[]{:S(2)}, u32[]{:S(2)}) collective-permute-start(bf16[128,768]{1,0:T(8,128)(2,1)S(1)} %copy-done.38), channel_id=1, source_target_pairs={{0,4},{1,5},{2,6},{3,7},{4,0},{5,1},{6,2},{7,3},{8,12},{9,13},{10,... | collective-permute-start | bytes 589832 | tf_op jit(solution)/shard_map/ppermute | solution.py:531
  55.7 12.5 %collective-permute-start.13 = (bf16[128,768]{1,0:T(8,128)(2,1)S(1)}, bf16[128,768]{1,0:T(8,128)(2,1)S(1)}, u32[]{:S(2)}, u32[]{:S(2)}) collective-permute-start(bf16[128,768]{1,0:T(8,128)(2,1)S(1)} %copy-done.37), channel_id=1, source_target_pairs={{0,6},{1,7},{2,4},{3,5},{4,2},{5,3},{6,0},{7,1},{8,14},{9,15},{10,... | collective-permute-start | bytes 589832 | tf_op jit(solution)/shard_map/ppermute | solution.py:531
  58.2 10.8 %collective-permute-start.15 = (bf16[256,768]{1,0:T(8,128)(2,1)S(1)}, bf16[256,768]{1,0:T(8,128)(2,1)S(1)}, u32[]{:S(2)}, u32[]{:S(2)}) collective-permute-start(bf16[256,768]{1,0:T(8,128)(2,1)S(1)} %pad_maximum_fusion.refs_2_.refs_6_), channel_id=1, source_target_pairs={{0,8},{8,0},{16,24},{24,16},{1,9},{9,1},{17,25},{25,17},{2,10},{10... | collective-permute-start | bytes 1179656 | tf_op jit(solution)/shard_map/ppermute | solution.py:525
  70.1 14.5 %collective-permute-start.18 = (bf16[256,768]{1,0:T(8,128)(2,1)S(1)}, bf16[256,768]{1,0:T(8,128)(2,1)S(1)}, u32[]{:S(2)}, u32[]{:S(2)}) collective-permute-start(bf16[256,768]{1,0:T(8,128)(2,1)S(1)} %constant_dynamic-update-slice_fusion.refs_2_.refs_7_), channel_id=1, source_target_pairs={{0,16},{8,24},{16,0},{24,8},{1,17},{9,25},{17,1},{25,9},{2,18},{10... | collective-permute-start | bytes 1179656 | tf_op jit(solution)/shard_map/ppermute | solution.py:528
  71.6 13.0 %collective-permute-start.19 = (bf16[256,768]{1,0:T(8,128)(2,1)S(1)}, bf16[256,768]{1,0:T(8,128)(2,1)S(1)}, u32[]{:S(2)}, u32[]{:S(2)}) collective-permute-start(bf16[256,768]{1,0:T(8,128)(2,1)S(1)} %constant_dynamic-update-slice_fusion.refs_2_.refs_7_), channel_id=1, source_target_pairs={{0,8},{8,0},{16,24},{24,16},{1,9},{9,1},{17,25},{25,17},{2,10},{10... | collective-permute-start | bytes 1179656 | tf_op jit(solution)/shard_map/ppermute | solution.py:525
  73.0 11.6 %collective-permute-start.17 = (bf16[128,768]{1,0:T(8,128)(2,1)S(1)}, bf16[128,768]{1,0:T(8,128)(2,1)S(1)}, u32[]{:S(2)}, u32[]{:S(2)}) collective-permute-start(bf16[128,768]{1,0:T(8,128)(2,1)S(1)} %get-tuple-element.151), channel_id=1, source_target_pairs={{0,4},{1,5},{2,6},{3,7},{4,0},{5,1},{6,2},{7,3},{8,12},{9,13},{10,... | collective-permute-start | bytes 589832 | tf_op jit(solution)/shard_map/ppermute | solution.py:531
  84.5 13.3 %collective-permute-start.22 = (bf16[256,768]{1,0:T(8,128)(2,1)S(1)}, bf16[256,768]{1,0:T(8,128)(2,1)S(1)}, u32[]{:S(2)}, u32[]{:S(2)}) collective-permute-start(bf16[256,768]{1,0:T(8,128)(2,1)S(1)} %collective-permute-done.15.refs_8_), channel_id=1, source_target_pairs={{0,16},{8,24},{16,0},{24,8},{1,17},{9,25},{17,1},{25,9},{2,18},{10... | collective-permute-start | bytes 1179656 | tf_op jit(solution)/shard_map/ppermute | solution.py:528
  85.1 14.3 %collective-permute-start.23 = (bf16[256,768]{1,0:T(8,128)(2,1)S(1)}, bf16[256,768]{1,0:T(8,128)(2,1)S(1)}, u32[]{:S(2)}, u32[]{:S(2)}) collective-permute-start(bf16[256,768]{1,0:T(8,128)(2,1)S(1)} %collective-permute-done.18.refs_9_), channel_id=1, source_target_pairs={{0,8},{8,0},{16,24},{24,16},{1,9},{9,1},{17,25},{25,17},{2,10},{10... | collective-permute-start | bytes 1179656 | tf_op jit(solution)/shard_map/ppermute | solution.py:525
  85.8 15.7 %collective-permute-start.20 = (bf16[128,768]{1,0:T(8,128)(2,1)S(1)}, bf16[128,768]{1,0:T(8,128)(2,1)S(1)}, u32[]{:S(2)}, u32[]{:S(2)}) collective-permute-start(bf16[128,768]{1,0:T(8,128)(2,1)S(1)} %get-tuple-element.156), channel_id=1, source_target_pairs={{0,2},{1,3},{2,0},{3,1},{4,6},{5,7},{6,4},{7,5},{8,10},{9,11},{10,... | collective-permute-start | bytes 589832 | tf_op jit(solution)/shard_map/ppermute | solution.py:531
  85.8 15.7 %collective-permute-start.21 = (bf16[128,768]{1,0:T(8,128)(2,1)S(1)}, bf16[128,768]{1,0:T(8,128)(2,1)S(1)}, u32[]{:S(2)}, u32[]{:S(2)}) collective-permute-start(bf16[128,768]{1,0:T(8,128)(2,1)S(1)} %get-tuple-element.158), channel_id=1, source_target_pairs={{0,6},{1,7},{2,4},{3,5},{4,2},{5,3},{6,0},{7,1},{8,14},{9,15},{10,... | collective-permute-start | bytes 589832 | tf_op jit(solution)/shard_map/ppermute | solution.py:531
  96.5 16.8 %collective-permute-start.28 = (bf16[256,768]{1,0:T(8,128)(2,1)S(1)}, bf16[256,768]{1,0:T(8,128)(2,1)S(1)}, u32[]{:S(2)}, u32[]{:S(2)}) collective-permute-start(bf16[256,768]{1,0:T(8,128)(2,1)S(1)} %get-tuple-element.173.refs_0_), channel_id=1, source_target_pairs={{0,8},{8,0},{16,24},{24,16},{1,9},{9,1},{17,25},{25,17},{2,10},{10... | collective-permute-start | bytes 1179656 | tf_op jit(solution)/shard_map/ppermute | solution.py:525
  97.9 15.4 %collective-permute-start.29 = (bf16[256,768]{1,0:T(8,128)(2,1)S(1)}, bf16[256,768]{1,0:T(8,128)(2,1)S(1)}, u32[]{:S(2)}, u32[]{:S(2)}) collective-permute-start(bf16[256,768]{1,0:T(8,128)(2,1)S(1)} %get-tuple-element.173.refs_0_), channel_id=1, source_target_pairs={{0,16},{8,24},{16,0},{24,8},{1,17},{9,25},{17,1},{25,9},{2,18},{10... | collective-permute-start | bytes 1179656 | tf_op jit(solution)/shard_map/ppermute | solution.py:528
  99.4 11.5 %collective-permute-start.24 = (bf16[128,768]{1,0:T(8,128)(2,1)S(1)}, bf16[128,768]{1,0:T(8,128)(2,1)S(1)}, u32[]{:S(2)}, u32[]{:S(2)}) collective-permute-start(bf16[128,768]{1,0:T(8,128)(2,1)S(1)} %get-tuple-element.169), channel_id=1, source_target_pairs={{0,4},{1,5},{2,6},{3,7},{4,0},{5,1},{6,2},{7,3},{8,12},{9,13},{10,... | collective-permute-start | bytes 589832 | tf_op jit(solution)/shard_map/ppermute | solution.py:531
  125.3 12.0 %collective-permute-start.32 = (bf16[640,768]{1,0:T(8,128)(2,1)S(1)}, bf16[640,768]{1,0:T(8,128)(2,1)S(1)}, u32[]{:S(2)}, u32[]{:S(2)}) collective-permute-start(bf16[640,768]{1,0:T(8,128)(2,1)S(1)} %get-tuple-element.178.vo_ref.refs_1_), channel_id=1, source_target_pairs={{0,1},{1,0},{2,3},{3,2},{4,5},{5,4},{6,7},{7,6},{8,9},{9,8},{10,11... | collective-permute-start | bytes 2949128 | tf_op jit(solution)/shard_map/ppermute | solution.py:522
  125.5 11.4 %collective-permute-start.34 = (bf16[256,768]{1,0:T(8,128)(2,1)S(1)}, bf16[256,768]{1,0:T(8,128)(2,1)S(1)}, u32[]{:S(2)}, u32[]{:S(2)}) collective-permute-start(bf16[256,768]{1,0:T(8,128)(2,1)S(1)} %collective-permute-done.30.refs_3_), channel_id=1, source_target_pairs={{0,8},{8,0},{16,24},{24,16},{1,9},{9,1},{17,25},{25,17},{2,10},{10... | collective-permute-start | bytes 1179656 | tf_op jit(solution)/shard_map/ppermute | solution.py:525
  126.2 11.2 %collective-permute-start.33 = (bf16[256,768]{1,0:T(8,128)(2,1)S(1)}, bf16[256,768]{1,0:T(8,128)(2,1)S(1)}, u32[]{:S(2)}, u32[]{:S(2)}) collective-permute-start(bf16[256,768]{1,0:T(8,128)(2,1)S(1)} %collective-permute-done.28.refs_2_), channel_id=1, source_target_pairs={{0,16},{8,24},{16,0},{24,8},{1,17},{9,25},{17,1},{25,9},{2,18},{10... | collective-permute-start | bytes 1179656 | tf_op jit(solution)/shard_map/ppermute | solution.py:528
  141.1 25.0 %collective-permute-start.36 = (bf16[192,1536]{1,0:T(8,128)(2,1)S(1)}, bf16[192,1536]{1,0:T(8,128)(2,1)S(1)}, u32[]{:S(2)}, u32[]{:S(2)}) collective-permute-start(bf16[192,1536]{1,0:T(8,128)(2,1)S(1)} %get-tuple-element.188), channel_id=1, source_target_pairs={{0,16},{8,24},{16,0},{24,8},{1,17},{9,25},{17,1},{25,9},{2,18},{10... | collective-permute-start | bytes 1769480 | tf_op jit(solution)/shard_map/ppermute | solution.py:528
  142.6 23.5 %collective-permute-start.38 = (bf16[192,1536]{1,0:T(8,128)(2,1)S(1)}, bf16[192,1536]{1,0:T(8,128)(2,1)S(1)}, u32[]{:S(2)}, u32[]{:S(2)}) collective-permute-start(bf16[192,1536]{1,0:T(8,128)(2,1)S(1)} %get-tuple-element.189), channel_id=1, source_target_pairs={{0,8},{8,0},{16,24},{24,16},{1,9},{9,1},{17,25},{25,17},{2,10},{10... | collective-permute-start | bytes 1769480 | tf_op jit(solution)/shard_map/ppermute | solution.py:525
  143.9 22.2 %collective-permute-start.37 = (bf16[128,768]{1,0:T(8,128)(2,1)S(1)}, bf16[128,768]{1,0:T(8,128)(2,1)S(1)}, u32[]{:S(2)}, u32[]{:S(2)}) collective-permute-start(bf16[128,768]{1,0:T(8,128)(2,1)S(1)} %get-tuple-element.193), channel_id=1, source_target_pairs={{0,4},{1,5},{2,6},{3,7},{4,0},{5,1},{6,2},{7,3},{8,12},{9,13},{10,... | collective-permute-start | bytes 589832 | tf_op jit(solution)/shard_map/ppermute | solution.py:531
  150.1 16.1 %collective-permute-start.40 = (f32[16,768]{1,0:T(8,128)S(1)}, f32[16,768]{1,0:T(8,128)S(1)}, u32[]{:S(2)}, u32[]{:S(2)}) collective-permute-start(f32[16,768]{1,0:T(8,128)S(1)} %add.88.small_ref), channel_id=1, source_target_pairs={{0,16},{8,24},{16,0},{24,8},{1,17},{9,25},{17,1},{25,9},{2,18},{10... | collective-permute-start | bytes 147464 | tf_op jit(solution)/shard_map/ppermute | solution.py:528
  166.4 14.0 %collective-permute-start.41 = (bf16[128,768]{1,0:T(8,128)(2,1)S(1)}, bf16[128,768]{1,0:T(8,128)(2,1)S(1)}, u32[]{:S(2)}, u32[]{:S(2)}) collective-permute-start(bf16[128,768]{1,0:T(8,128)(2,1)S(1)} %get-tuple-element.205), channel_id=1, source_target_pairs={{0,2},{1,3},{2,0},{3,1},{4,6},{5,7},{6,4},{7,5},{8,10},{9,11},{10,... | collective-permute-start | bytes 589832 | tf_op jit(solution)/shard_map/ppermute | solution.py:531
  167.3 13.3 %collective-permute-start.43 = (bf16[112,1536]{1,0:T(8,128)(2,1)S(1)}, bf16[112,1536]{1,0:T(8,128)(2,1)S(1)}, u32[]{:S(2)}, u32[]{:S(2)}) collective-permute-start(bf16[112,1536]{1,0:T(8,128)(2,1)S(1)} %get-tuple-element.203.a_low_ref), channel_id=1, source_target_pairs={{0,8},{8,0},{16,24},{24,16},{1,9},{9,1},{17,25},{25,17},{2,10},{10... | collective-permute-start | bytes 1032200 | tf_op jit(solution)/shard_map/ppermute | solution.py:525
  168.1 12.5 %collective-permute-start.44 = (bf16[96,1536]{1,0:T(8,128)(2,1)S(1)}, bf16[96,1536]{1,0:T(8,128)(2,1)S(1)}, u32[]{:S(2)}, u32[]{:S(2)}) collective-permute-start(bf16[96,1536]{1,0:T(8,128)(2,1)S(1)} %get-tuple-element.204), channel_id=1, source_target_pairs={{0,16},{8,24},{16,0},{24,8},{1,17},{9,25},{17,1},{25,9},{2,18},{10... | collective-permute-start | bytes 884744 | tf_op jit(solution)/shard_map/ppermute | solution.py:528
  169.5 11.0 %collective-permute-start.42 = (bf16[128,768]{1,0:T(8,128)(2,1)S(1)}, bf16[128,768]{1,0:T(8,128)(2,1)S(1)}, u32[]{:S(2)}, u32[]{:S(2)}) collective-permute-start(bf16[128,768]{1,0:T(8,128)(2,1)S(1)} %get-tuple-element.206), channel_id=1, source_target_pairs={{0,6},{1,7},{2,4},{3,5},{4,2},{5,3},{6,0},{7,1},{8,14},{9,15},{10,... | collective-permute-start | bytes 589832 | tf_op jit(solution)/shard_map/ppermute | solution.py:531
  181.5 15.6 %collective-permute-start.47 = (bf16[112,768]{1,0:T(8,128)(2,1)S(1)}, bf16[112,768]{1,0:T(8,128)(2,1)S(1)}, u32[]{:S(2)}, u32[]{:S(2)}) collective-permute-start(bf16[112,768]{1,0:T(8,128)(2,1)S(1)} %get-tuple-element.218), channel_id=1, source_target_pairs={{0,4},{1,5},{2,6},{3,7},{4,0},{5,1},{6,2},{7,3},{8,12},{9,13},{10,... | collective-permute-start | bytes 516104 | tf_op jit(solution)/shard_map/ppermute | solution.py:531
  184.2 12.9 %collective-permute-start.48 = (bf16[112,768]{1,0:T(8,128)(2,1)S(1)}, bf16[112,768]{1,0:T(8,128)(2,1)S(1)}, u32[]{:S(2)}, u32[]{:S(2)}) collective-permute-start(bf16[112,768]{1,0:T(8,128)(2,1)S(1)} %get-tuple-element.219), channel_id=1, source_target_pairs={{0,6},{1,7},{2,4},{3,5},{4,2},{5,3},{6,0},{7,1},{8,14},{9,15},{10,... | collective-permute-start | bytes 516104 | tf_op jit(solution)/shard_map/ppermute | solution.py:531
  (60 other events, 638.0 us)

commit v3 on v2

--- a/solution.py
+++ b/solution.py
@@ -11,7 +11,6 @@
 EPSILON = 1e-06
 BF = jnp.bfloat16
 F32 = jnp.float32
-VMEM_BYTES = 20 * 1024 * 1024
 GROUP = 256
 FAR_FIRST = (2, 3, 1)
 
@@ -40,8 +39,8 @@
     return jax.ShapeDtypeStruct(shape, dtype)
 
 
-def params():
-    return pltpu.CompilerParams(vmem_limit_bytes=VMEM_BYTES)
+def params(megabytes=20):
+    return pltpu.CompilerParams(vmem_limit_bytes=megabytes * 1024 * 1024)
 
 
 def cost(flops, nbytes):
@@ -81,7 +80,7 @@
     for ref in refs[:-2]:
         out_ref[:, base : base + ref.shape[1]] = ref[...]
         base += ref.shape[1]
-    router = refs[-2][...]
+    router = refs[-2][...].astype(F32).T.astype(BF)
     out_ref[:, base:] = jnp.concatenate(
         [router, jnp.zeros((router.shape[0], out_ref.shape[1] - base - router.shape[1]), router.dtype)], axis=1
     )
@@ -264,48 +263,55 @@
         base += size
 
 
-def expert_kernel(pieces, extra, own_ref, *refs):
+def load_kernel(after_ref, w1_ref, w2_ref, w1_out, w2_out, token_ref, sems):
+    copies = []
+    for ref, out_ref in ((w1_ref, w1_out), (w2_ref, w2_out)):
+        rows = ref.shape[1] // 4
+        for part in range(4):
+            at = pl.ds(part * rows, rows)
+            copies.append(pltpu.make_async_copy(ref.at[0, at], out_ref.at[at], sems.at[len(copies)]))
+    for copy in copies:
+        copy.start()
+    token_ref[...] = jnp.zeros_like(token_ref)
+    for copy in copies:
+        copy.wait()
+
+
+def hidden_grad_kernel(first_ref, second_ref, w2_ref, first_out, second_out):
+    rows = first_ref.shape[0]
+    dy = jnp.concatenate([first_ref[...], second_ref[...]], axis=0)
+    width = first_out.shape[1] // 3
+    for part in range(3):
+        at = slice(part * width, (part + 1) * width)
+        both = mm_nt(dy, w2_ref[at, :])
+        first_out[:, at] = both[:rows]
+        second_out[:, at] = both[rows:]
+
+
+def expert_kernel(pieces, own_ref, *refs):
     rows_refs, dy = refs[:pieces], refs[pieces]
-    router_ref, w1_ref, w2_ref = refs[pieces + 1 : pieces + 4]
-    refs = refs[pieces + 4 :]
-    extra_refs, refs = refs[: sum(extra)], refs[sum(extra) :]
+    router_ref, w1_ref, w2_ref, hidden_grad_ref = refs[pieces + 1 : pieces + 5]
+    refs = refs[pieces + 5 :]
     back_refs, result_refs = refs[:pieces], refs[pieces : 2 * pieces]
-    router_grad_ref, rows = refs[2 * pieces : 2 * pieces + 2]
-    extra_out, refs = refs[2 * pieces + 2 : 2 * pieces + 2 + len(extra)], refs[2 * pieces + 2 + len(extra) :]
-    branch, probs_ref, gate_ref, result, back = refs
-    step = pl.program_id(0)
+    router_grad_ref, rows = refs[2 * pieces :]
     own = own_ref[0]
-
-    @pl.when(step == 0)
-    def _():
-        join(rows_refs, rows)
-        base = 0
-        for count, out_ref in zip(extra, extra_out, strict=True):
-            join(extra_refs[base : base + count], out_ref)
-            base += count
-        router_probs, gate = gate_of(rows[...], router_ref[...], one_lane(probs_ref.shape, own))
-        probs_ref[...] = router_probs
-        gate_ref[...] = gate
-        branch[...] = (dy[...].astype(F32) * gate).astype(BF)
-        result[...] = jnp.zeros_like(result)
-        back[...] = jnp.zeros_like(back)
-
-    w1, w2 = w1_ref[0], w2_ref[0]
-    hidden, slope = gelu_parts(mm(rows[...], w1))
-    result[...] += mm(hidden.astype(BF), w2)
-    pre_grad = (mm_nt(branch[...], w2) * slope).astype(BF)
-    back[...] += mm_nt(pre_grad, w1)
-
-    @pl.when(step == pl.num_programs(0) - 1)
-    def _():
-        returned = result[...].astype(BF)
-        part_out(returned, result_refs)
-        gate_grad = jnp.sum(dy[...].astype(F32) * returned.astype(F32), axis=-1, keepdims=True)
-        router_probs, gate = probs_ref[...], gate_ref[...]
-        picked = one_lane(router_probs.shape, own)
-        logit_grad = (router_probs * (picked - gate) * gate_grad).astype(BF)
-        router_grad_ref[...] = mm_tn(logit_grad, rows[...])
-        part_out((back[...] + mm_nt(logit_grad, router_ref[...])).astype(BF), back_refs)
+    join(rows_refs, rows)
+    picked = one_lane((rows.shape[0], router_ref.shape[1]), own)
+    router_probs, gate = gate_of(rows[...], router_ref[...], picked)
+    result, back = 0.0, 0.0
+    width = w1_ref.shape[1] // 2
+    for part in range(2):
+        at = slice(part * width, (part + 1) * width)
+        hidden, slope = gelu_parts(mm(rows[...], w1_ref[:, at]))
+        result += mm(hidden.astype(BF), w2_ref[at, :])
+        pre_grad = (hidden_grad_ref[:, at] * gate * slope).astype(BF)
+        back += mm_nt(pre_grad, w1_ref[:, at])
+    returned = result.astype(BF)
+    part_out(returned, result_refs)
+    gate_grad = jnp.sum(dy[...].astype(F32) * returned.astype(F32), axis=-1, keepdims=True)
+    logit_grad = (router_probs * (picked - gate) * gate_grad).astype(BF)
+    router_grad_ref[...] = mm_tn(logit_grad, rows[...])
+    part_out((back + mm_nt(logit_grad, router_ref[...])).astype(BF), back_refs)
 
 
 def expert_grad_kernel(pieces, more, place_ref, *refs):
@@ -659,7 +665,7 @@
         device_of[..., None] * shard + jnp.arange(shard, dtype=jnp.int32)
     ).reshape(1, model).astype(jnp.int32)
 
-    shards = (query_weight, value_weight, key_weight, out_weight, router_weight)
+    shards = (query_weight, value_weight, key_weight, out_weight, router_weight.T)
     packed = pl.pallas_call(
         pack_kernel,
         out_shape=shape_of((shard, 4 * model + 128), BF),
@@ -725,6 +731,15 @@
         name="bias",
     )(after(bucket_line, qv, ko), rel_table)
     qv_far, ko_far = at.gather_far(*all_after([qv_near, ko_near], bias))
+    w_first, w_second, loaded = pl.pallas_call(
+        load_kernel,
+        out_shape=(pltpu.VMEM((model, hidden), BF), pltpu.VMEM((hidden, model), BF), shape_of((8, 128), F32)),
+        in_specs=[pl.BlockSpec(memory_space=pltpu.VMEM)] + [pl.BlockSpec(memory_space=pl.ANY)] * 2,
+        out_specs=(pl.BlockSpec(memory_space=pltpu.VMEM),) * 3,
+        scratch_shapes=[pltpu.SemaphoreType.DMA((8,))],
+        compiler_params=params(),
+        name="load",
+    )(bias[0, :8, :128], expert_in, expert_out)
     both_side = at.core(both_near)
     dy_two = at.send_more(dy_blocks, 2, (qv_near, dy_one))
     qv_far, ko_far, dy_two = all_after([qv_far, ko_far, dy_two], both_side)
@@ -789,7 +804,7 @@
         compiler_params=params(),
         cost_estimate=cost(8 * rows * model * model, 12 * model * model),
         name="attend",
-    )(normed, bias, perm, *in_hbm(tokens), gain_ffn, *in_hbm(slots_map), picked, *qv_pieces, *qv_pieces, *ko_pieces, *ko_pieces)
+    )(normed, bias, perm, *in_hbm(tokens), after(gain_ffn, loaded), *in_hbm(slots_map), picked, *qv_pieces, *qv_pieces, *ko_pieces, *ko_pieces)
 
     got = at.core(after(send, dy_three))
     first, second = at.to_owners(keep, got, (dy_ax, dy_ay))
@@ -797,49 +812,38 @@
         dy_b = jnp.concatenate([dy_one, dy_three], axis=0)
     dy_b_later = after(dy_b, got, dy_ax, dy_ay)
     dy_by, dy_bx = at.y(dy_b_later), at.x(dy_b_later)
-    part = 1024
-
-    def expert(rows_list, dy_rows, router_in, extra=()):
+    in_vmem = pl.BlockSpec(memory_space=pltpu.VMEM)
+    hidden_grads = pl.pallas_call(
+        hidden_grad_kernel,
+        out_shape=(shape_of((half, hidden), F32),) * 2,
+        in_specs=[in_vmem] * 3,
+        out_specs=(in_vmem,) * 2,
+        compiler_params=params(),
+        name="hidden_grads",
+    )(dy_a, dy_b, w_second)
+
+    def expert(rows_list, dy_rows, hidden_grad, router_in):
         sizes = [v.shape[0] for v in rows_list]
         count = sum(sizes)
-        flat = [v for group in extra for v in group]
-        joined = [sum(v.shape[0] for v in group) for group in extra]
+        shapes = [((n, model), BF) for n in sizes * 2] + [((experts, model), F32), ((count, model), BF)]
         outs = pl.pallas_call(
-            functools.partial(expert_kernel, len(sizes), tuple(len(group) for group in extra)),
-            grid=(hidden // part,),
-            out_shape=tuple(shape_of((n, model), BF) for n in sizes * 2)
-            + (shape_of((experts, model), F32),)
-            + tuple(shape_of((n, model), BF) for n in [count, *joined]),
-            in_specs=[smem]
-            + [full((n, model)) for n in [*sizes, count]]
-            + [
-                full((model, experts)),
-                pl.BlockSpec((1, model, part), lambda f: (0, 0, f)),
-                pl.BlockSpec((1, part, model), lambda f: (0, f, 0)),
-            ]
-            + [full(v.shape) for v in flat],
-            out_specs=tuple(full((n, model)) for n in sizes * 2)
-            + (full((experts, model)),)
-            + tuple(full((n, model)) for n in [count, *joined]),
-            scratch_shapes=[
-                pltpu.VMEM((count, model), BF),
-                pltpu.VMEM((count, experts), F32),
-                pltpu.VMEM((count, 1), F32),
-                pltpu.VMEM((count, model), F32),
-                pltpu.VMEM((count, model), F32),
-            ],
+            functools.partial(expert_kernel, len(sizes)),
+            out_shape=tuple(shape_of(*v) for v in shapes),
+            in_specs=[smem] + [in_vmem] * (len(sizes) + 5),
+            out_specs=(in_vmem,) * len(shapes),
             compiler_params=params(),
-            cost_estimate=cost(8 * count * model * hidden, 4 * model * hidden),
             name="expert",
-        )(own, *rows_list, dy_rows, router_in, expert_in, expert_out, *flat)
+        )(own, *rows_list, dy_rows, router_in, w_first, w_second, hidden_grad)
         n = len(sizes)
-        return list(outs[:n]), list(outs[n : 2 * n]), outs[2 * n], outs[2 * n + 1 :]
-
-    dy_ax_later, dy_by_later = all_after([dy_ax, dy_by], first[-1], dy_bx)
+        return list(outs[:n]), list(outs[n : 2 * n]), outs[2 * n], outs[2 * n + 1]
+
+    dy_ax_later, dy_by_later = all_after([dy_ax, dy_by], first[-1], dy_bx, hidden_grads[1])
     dy_axy, dy_byx = at.y(dy_ax_later), at.x(dy_by_later)
-    back_a, returned_a, router_grad_a, (rows_a,) = expert(first, dy_a, after(router, dy_by, dy_bx))
+    back_a, returned_a, router_grad_a, rows_a = expert(first, dy_a, hidden_grads[0], after(router, dy_by, dy_bx))
     rows_ax, rows_ay = at.x(rows_a), at.y(rows_a)
-    back_b, returned_b, router_grad_b, (rows_b,) = expert(second, dy_b, after(router, router_grad_a, dy_axy, dy_byx))
+    back_b, returned_b, router_grad_b, rows_b = expert(
+        second, dy_b, hidden_grads[1], after(router, router_grad_a, dy_axy, dy_byx)
+    )
     rows_b_later = after(rows_b, rows_ax, rows_ay)
     rows_by, rows_bx = at.y(rows_b_later), at.x(rows_b_later)
     back_keep, back_send = at.to_senders(back_a, back_b)
@@ -876,7 +880,7 @@
             compiler_params=params(),
             cost_estimate=cost(8 * count * model * slice_width, 20 * model * slice_width),
             name="expert_grads",
-        )(place, *in_hbm(*rows_list, *dy_list), own, router_in, expert_in, expert_out, *before)
+        )(place, *in_hbm(*rows_list, *dy_list), own, router_in, expert_in, expert_out, *in_hbm(*before))
 
     rows_axy, rows_byx = at.y(after(rows_ax, rows_by, rows_bx, back_send)), at.x(after(rows_by, rows_bx, back_send))
 
@@ -973,7 +977,7 @@
         "weight_grads",
         [((quarter_rows, pair), F32), ((quarter_rows, pair), BF)] * 2,
         normed,
-        normed_side,
+        after(normed_side, small),
         mixed,
         vo_grads,
         vo_side,
@@ -988,8 +992,8 @@
     else:
         home_two = at.apart(jnp.concatenate([*returned_a, *returned_b], axis=0).reshape(nz, -1, model))
     near_sums = expert_grads(
-        [rows_a, rows_b, rows_ax, rows_by, rows_ay, rows_bx],
-        [dy_a, dy_b, dy_ax, dy_by, dy_ay, dy_bx],
+        [rows_a, rows_b, rows_ax, rows_by],
+        [dy_a, dy_b, dy_ax, dy_by],
         after(router, a_low, b_low),
         (),
     )
@@ -1006,12 +1010,7 @@
         small_got,
     )
     a_got, b_got = at.x(a_low), at.y(b_low)
-    far_sums = expert_grads(
-        [rows_axy, rows_byx],
-        [dy_axy, dy_byx],
-        after(router, a_low, b_low),
-        near_sums,
-    )
+    mid_sums = expert_grads([rows_ay, rows_bx], [dy_ay, dy_bx], after(router, a_low, b_low), near_sums)
     if at.near:
         home = [at.far(v, k) for v, k in zip(all_after([returned_b[1], returned_b[0]], a_low, b_low), (3, 1))]
         home_blocks = [returned_a[0], home[1], home_two, home[0]]
@@ -1029,7 +1028,7 @@
             [((4 * shard, model), F32)] + [((small_rows + 4 * shard, model), BF)] * 3,
             a,
             a_low,
-            after(a_got, far_sums[0], *home),
+            after(a_got, mid_sums[0], *home),
             b,
             b_got,
         )
@@ -1044,7 +1043,7 @@
         grad_value, grad_query, grad_proj, grad_key = [sums[:, n * model : (n + 1) * model] for n in range(4)]
         summed = lax.psum(summed, "expert", axis_index_groups=at.columns)
     returned_send = at.core(after(returned_other, hold))
-    grad_in, grad_out_w = far_sums
+    grad_in, grad_out_w = expert_grads([rows_axy, rows_byx], [dy_axy, dy_byx], after(router, hold), mid_sums)
     keep_rows = half // len(returned_keep)
     expert_result = mm(
         slots_t,
@@ -1056,7 +1055,7 @@
             fold_last_kernel,
             "fold_last",
             [((shard, model), F32)] * 4 + [((small_rows, model), F32)],
-            after(keep_sum, output),
+            after(keep_sum, output, grad_in),
             low[0],
             *[got_z[k] for k in (1, 2, 3)],
         )

time: 201 us -> 191 us (0.950)
  starting transfers between devices: 51.8 us -> 45.4 us
  local copies, waits for them, and re-layouts: 15.1 us -> 9.91 us
  Pallas kernels: 70.2 us -> 75.2 us
  waiting for transfers between devices: 56.8 us -> 53.3 us
    pallas_call x2 -> x3, Pallas kernels: 22.1 us -> 28.1 us  [expert_grads(): pl.pallas_call(functools.partial(expert_grad_kernel, len(sizes), bool(bef...]
    ppermute x18, starting transfers between devices: 28.6 us -> 23.1 us  [far(): lax.ppermute(v, 'expert', [(i, i ^ 2 * k) for i in range(self.experts)])]
    ppermute x18, waiting for transfers between devices: 43.5 us -> 38.3 us  [far(): lax.ppermute(v, 'expert', [(i, i ^ 2 * k) for i in range(self.experts)])]
    unnamed x89 -> x82, local copies, waits for them, and re-layouts: 9.4 us -> 5.21 us
    ppermute x11, waiting for transfers between devices: 4.93 us -> 9.01 us  [y(): return lax.ppermute(v, 'dp', [(i, i ^ 2) for i in range(self.dp)])]
    pallas_call x2 -> x4, Pallas kernels: 18.5 us -> 17.6 us  [the longest x2 10.6 us: expert(): pl.pallas_call(functools.partial(expert_kernel, len(sizes)), out_shape=tu...]
  transfers between devices with their start and end apart: 49 -> 49, of which waited for: 20 -> 22; matrix products, arithmetic and copies ran while one was open for 4% -> 4% of each run, Pallas kernels for 31% -> 35%
where the time goes in v3:
time: 191 us; the launch traced here: 190 us
  Pallas kernels  75.2 us (39%)
  waiting for transfers between devices  53.3 us (28%)
  starting transfers between devices  45.4 us (24%)
  local copies, waits for them, and re-layouts  9.91 us (5%)
  other arithmetic  4.01 us (2%)
    ppermute x18, waiting for transfers between devices, far(): lax.ppermute(v, 'expert', [(i, i ^ 2 * k) for i in range(self.experts)])  38.3 us
    pallas_call x3, Pallas kernels, expert_grads(): pl.pallas_call(functools.partial(expert_grad_kernel, len(sizes), bool(bef...  28.1 us
    ppermute x18, starting transfers between devices, far(): lax.ppermute(v, 'expert', [(i, i ^ 2 * k) for i in range(self.experts)])  23.1 us
    ppermute x11, starting transfers between devices, y(): return lax.ppermute(v, 'dp', [(i, i ^ 2) for i in range(self.dp)])  11.7 us
    pallas_call x2, Pallas kernels, expert(): pl.pallas_call(functools.partial(expert_kernel, len(sizes)), out_shape=tu...  10.6 us
    ppermute x10, starting transfers between devices, x(): return lax.ppermute(v, 'dp', [(i, i ^ 1) for i in range(self.dp)])  9.76 us
    ppermute x11, waiting for transfers between devices, y(): return lax.ppermute(v, 'dp', [(i, i ^ 2) for i in range(self.dp)])  9.01 us
    pallas_call x1, Pallas kernels, per_device(): pl.pallas_call(functools.partial(attend_kernel, head), grid=(groups,), ou...  8.91 us
  transfers between devices with their start and end apart: 49, of which 22 were waited for; matrix products, arithmetic and copies ran while one was open for 4% of the time, Pallas kernels for 35%

profile of v3, /device:TPU:0, one launch (start us, length us, event | category | flops | bytes accessed | tf_op | source)
XLA Modules:
  0.0 190.3 jit_solution(20500661762634121)
XLA Ops:
  0.6 1.6 pack.1
  2.2 5.0 %collective-permute-start.2 = (bf16[24,3200]{1,0:T(8,128)(2,1)}, bf16[24,3200]{1,0:T(8,128)(2,1)S(1)}, u32[]{:S(2)}, u32[]{:S(2)}) collective-permute-start(bf16[24,3200]{1,0:T(8,128)(2,1)} %pack.1), channel_id=1, source_target_pairs={{0,6},{1,7},{2,4},{3,5},{4,2},{5,3},{6,0},{7,1},{8,14},{9,15},{10,... | collective-permute-start | bytes 460808 | tf_op jit(solution)/shard_map/ppermute | solution.py:537
  12.3 1.6 route.1
  14.7 5.8 %collective-permute-done.1 = bf16[24,3200]{1,0:T(8,128)(2,1)S(1)} collective-permute-done((bf16[24,3200]{1,0:T(8,128)(2,1)}, bf16[24,3200]{1,0:T(8,128)(2,1)S(1)}, u32[]{:S(2)}, u32[]{:S(2)}) %collective-permute-start.1) | collective-permute-done | bytes 153632 | tf_op jit(solution)/shard_map/ppermute | solution.py:537
  27.1 5.7 %collective-permute-done.4 = bf16[128,768]{1,0:T(8,128)(2,1)S(1)} collective-permute-done((bf16[128,768]{1,0:T(8,128)(2,1)S(1)}, bf16[128,768]{1,0:T(8,128)(2,1)S(1)}, u32[]{:S(2)}, u32[]{:S(2)}) %collective-permute-start.4) | collective-permute-done | bytes 196640 | tf_op jit(solution)/shard_map/ppermute | solution.py:537
  38.6 11.5 %collective-permute-done.9 = bf16[128,768]{1,0:T(8,128)(2,1)S(1)} collective-permute-done((bf16[128,768]{1,0:T(8,128)(2,1)S(1)}, bf16[128,768]{1,0:T(8,128)(2,1)S(1)}, u32[]{:S(2)}, u32[]{:S(2)}) %collective-permute-start.9) | collective-permute-done | bytes 196640 | tf_op jit(solution)/shard_map/ppermute | solution.py:537
  50.1 2.4 %collective-permute-done.7.refs_8_.refs_12_ = bf16[192,1536]{1,0:T(8,128)(2,1)S(1)} collective-permute-done((bf16[192,1536]{1,0:T(8,128)(2,1)S(1)}, bf16[192,1536]{1,0:T(8,128)(2,1)S(1)}, u32[]{:S(2)}, u32[]{:S(2)}) %collective-permute-start.7) | collective-permute-done | bytes 589856 | tf_op jit(solution)/shard_map/ppermute | solution.py:534
  53.8 2.3 %collective-permute-start.13 = (bf16[128,768]{1,0:T(8,128)(2,1)S(1)}, bf16[128,768]{1,0:T(8,128)(2,1)S(1)}, u32[]{:S(2)}, u32[]{:S(2)}) collective-permute-start(bf16[128,768]{1,0:T(8,128)(2,1)S(1)} %copy-done.34), channel_id=1, source_target_pairs={{0,6},{1,7},{2,4},{3,5},{4,2},{5,3},{6,0},{7,1},{8,14},{9,15},{10,... | collective-permute-start | bytes 589832 | tf_op jit(solution)/shard_map/ppermute | solution.py:537
  56.1 1.6 collective-permute-start.16
  58.5 8.9 %attend.1 = (bf16[256,768]{1,0:T(8,128)(2,1)S(1)}, bf16[256,768]{1,0:T(8,128)(2,1)S(1)}, bf16[256,768]{1,0:T(8,128)(2,1)S(1)}, f32[12,256,256]{2,1,0:T(8,128)S(1...) custom-call(bf16[256,768]{1,0:T(8,128)(2,1)S(1)} %copy-done.11, ...), custom_call_target="tpu_custom_call" | custom-call | flops 1024 | bytes 1024 | tf_op jit(solution)/shard_map/attend/pallas_call | solution.py:764
  71.2 4.4 %load.1 = (bf16[768,3072]{1,0:T(8,128)(2,1)S(1)}, bf16[3072,768]{1,0:T(8,128)(2,1)S(1)}, f32[8,128]{1,0:T(8,128)}) custom-call(f32[8,128]{1,0:T(8,128)S(1)} %slice_bitcast_fusion.after_ref, bf16[1,768,3072]{2,1,0:T(8,128)(2,1)} %refs_6_.5, bf16[1,3072,768]{2,1,0:T(8,128)(2,1)} %refs_7_.3), custom_call_target="tpu_custom_call" | custom-call | tf_op jit(solution)/shard_map/load/pallas_call | solution.py:734
  75.6 2.6 %hidden_grads.1 = (f32[256,3072]{1,0:T(8,128)S(1)}, f32[256,3072]{1,0:T(8,128)S(1)}) custom-call(bf16[256,768]{1,0:T(8,128)(2,1)S(1)} %pad_maximum_fusion.first_ref.refs_2_.refs_4_, bf16[256,768]{1,0:T(8,128)(2,1)S(1)} %constant_dynamic-update-slice_fusion.second_ref.refs_2_.refs_5_, bf16[3072,768]{1,0:T(8,128)(2,1)S(1)} %get-tuple-element.164.w2_ref.refs_5_), custom_call_target="tpu_custom_call" | custom-call | tf_op jit(solution)/shard_map/hidden_grads/pallas_call | solution.py:816
  78.2 3.3 %collective-permute-done.17.refs_1_ = bf16[128,768]{1,0:T(8,128)(2,1)S(1)} collective-permute-done((bf16[128,768]{1,0:T(8,128)(2,1)S(1)}, bf16[128,768]{1,0:T(8,128)(2,1)S(1)}, u32[]{:S(2)}, u32[]{:S(2)}) %collective-permute-start.17) | collective-permute-done | bytes 196640 | tf_op jit(solution)/shard_map/ppermute | solution.py:537
  81.6 1.6 collective-permute-start.22
  83.9 2.3 %collective-permute-start.21 = (bf16[128,768]{1,0:T(8,128)(2,1)S(1)}, bf16[128,768]{1,0:T(8,128)(2,1)S(1)}, u32[]{:S(2)}, u32[]{:S(2)}) collective-permute-start(bf16[128,768]{1,0:T(8,128)(2,1)S(1)} %get-tuple-element.169), channel_id=1, source_target_pairs={{0,6},{1,7},{2,4},{3,5},{4,2},{5,3},{6,0},{7,1},{8,14},{9,15},{10,... | collective-permute-start | bytes 589832 | tf_op jit(solution)/shard_map/ppermute | solution.py:537
  86.2 5.2 %expert.2 = (bf16[128,768]{1,0:T(8,128)(2,1)S(1)}, bf16[128,768]{1,0:T(8,128)(2,1)S(1)}, bf16[128,768]{1,0:T(8,128)(2,1)S(1)}, bf16[128,768]{1,0:T(8,128)(2,1)S(...) custom-call(s32[1]{0:T(128)} %bitcast.11.own_ref.refs_8_.refs_4_, ...), custom_call_target="tpu_custom_call" | custom-call | tf_op jit(solution)/shard_map/expert/pallas_call | solution.py:829
  95.0 5.4 %expert.3 = (bf16[128,768]{1,0:T(8,128)(2,1)S(1)}, bf16[128,768]{1,0:T(8,128)(2,1)S(1)}, bf16[128,768]{1,0:T(8,128)(2,1)S(1)}, bf16[128,768]{1,0:T(8,128)(2,1)S(...) custom-call(s32[1]{0:T(128)} %bitcast.11.own_ref.refs_8_.refs_4_, ...), custom_call_target="tpu_custom_call" | custom-call | tf_op jit(solution)/shard_map/expert/pallas_call | solution.py:829
  100.4 3.9 %collective-permute-done.24.refs_2_ = bf16[128,768]{1,0:T(8,128)(2,1)S(1)} collective-permute-done((bf16[128,768]{1,0:T(8,128)(2,1)S(1)}, bf16[128,768]{1,0:T(8,128)(2,1)S(1)}, u32[]{:S(2)}, u32[]{:S(2)}) %collective-permute-start.24) | collective-permute-done | bytes 196640 | tf_op jit(solution)/shard_map/ppermute | solution.py:537
  104.3 4.0 %collective-permute-start.26 = (bf16[128,768]{1,0:T(8,128)(2,1)S(1)}, bf16[128,768]{1,0:T(8,128)(2,1)S(1)}, u32[]{:S(2)}, u32[]{:S(2)}) collective-permute-start(bf16[128,768]{1,0:T(8,128)(2,1)S(1)} %get-tuple-element.182), channel_id=1, source_target_pairs={{0,6},{1,7},{2,4},{3,5},{4,2},{5,3},{6,0},{7,1},{8,14},{9,15},{10,... | collective-permute-start | bytes 589832 | tf_op jit(solution)/shard_map/ppermute | solution.py:537
  108.4 2.0 %collective-permute-start.31 = (bf16[256,768]{1,0:T(8,128)(2,1)S(1)}, bf16[256,768]{1,0:T(8,128)(2,1)S(1)}, u32[]{:S(2)}, u32[]{:S(2)}) collective-permute-start(bf16[256,768]{1,0:T(8,128)(2,1)S(1)} %get-tuple-element.185.refs_1_), channel_id=1, source_target_pairs={{0,8},{8,0},{16,24},{24,16},{1,9},{9,1},{17,25},{25,17},{2,10},{10... | collective-permute-start | bytes 1179656 | tf_op jit(solution)/shard_map/ppermute | solution.py:531
  110.3 2.7 %collective-permute-done.25.refs_1_ = bf16[128,768]{1,0:T(8,128)(2,1)S(1)} collective-permute-done((bf16[128,768]{1,0:T(8,128)(2,1)S(1)}, bf16[128,768]{1,0:T(8,128)(2,1)S(1)}, u32[]{:S(2)}, u32[]{:S(2)}) %collective-permute-start.25) | collective-permute-done | bytes 196640 | tf_op jit(solution)/shard_map/ppermute | solution.py:537
  113.1 2.5 %collective-permute-done.26.refs_3_ = bf16[128,768]{1,0:T(8,128)(2,1)S(1)} collective-permute-done((bf16[128,768]{1,0:T(8,128)(2,1)S(1)}, bf16[128,768]{1,0:T(8,128)(2,1)S(1)}, u32[]{:S(2)}, u32[]{:S(2)}) %collective-permute-start.26) | collective-permute-done | bytes 196640 | tf_op jit(solution)/shard_map/ppermute | solution.py:537
  118.1 2.9 %middle.1 = (f32[256,768]{1,0:T(8,128)S(1)}, f32[1,768]{1,0:T(1,128)S(1)}, bf16[256,768]{1,0:T(8,128)(2,1)S(1)}, bf16[640,768]{1,0:T(8,128)(2,1)S(1)}) custom-call(bf16[128,768]{1,0:T(8,128)(2,1)S(1)} %get-tuple-element.177.refs_0_, bf16[128,768]{1,0:T(8,128)(2,1)S(1)} %collective-permute-done.25.refs_1_, ...), custom_call_target="tpu_custom_call" | custom-call | flops 1024 | bytes 1024 | tf_op jit(solution)/shard_map/middle/pallas_call | solution.py:887
  122.5 5.6 %score_grads.1 = (bf16[512,768]{1,0:T(8,128)(2,1)S(1)}, f32[12,1,512]{2,1,0:T(1,128)S(1)}) custom-call(bf16[256,768]{1,0:T(8,128)(2,1)S(1)} %get-tuple-element.189.mixed_grad_ref, bf16[256,768]{1,0:T(8,128)(2,1)S(1)} %get-tuple-element.190.v_ref, bf16[256,768]{1,0:T(8,128)(2,1)S(1)} %get-tuple-element.191.q_ref, ...), custom_call_target="tpu_custom_call" | custom-call | flops 1024 | bytes 1024 | tf_op jit(solution)/shard_map/score_grads/pallas_call | solution.py:920
  128.1 4.6 %collective-permute-done.33.refs_0_ = bf16[256,768]{1,0:T(8,128)(2,1)S(1)} collective-permute-done((bf16[256,768]{1,0:T(8,128)(2,1)S(1)}, bf16[256,768]{1,0:T(8,128)(2,1)S(1)}, u32[]{:S(2)}, u32[]{:S(2)}) %collective-permute-start.33) | collective-permute-done | bytes 393248 | tf_op jit(solution)/shard_map/ppermute | solution.py:534
  134.1 3.9 %inputs.1 = (f32[256,768]{1,0:T(8,128)}, f32[16,768]{1,0:T(8,128)S(1)}) custom-call(bf16[512,768]{1,0:T(8,128)(2,1)S(1)} %get-tuple-element.205.refs_0_.qk_ref, bf16[640,768]{1,0:T(8,128)(2,1)S(1)} %get-tuple-element.194.refs_1_.vo_ref, bf16[256,768]{1,0:T(8,128)(2,1)S(1)} %copy-done.5, f32[1,768]{1,0:T(1,128)S(1)} %get-tuple-element.195.refs_3_, ...), custom_call_target="tpu_custom_call" | custom-call | flops 1024 | bytes 1024 | tf_op jit(solution)/shard_map/inputs/pallas_call | solution.py:932
  144.1 1.5 collective-permute-start.40
  145.6 10.6 %expert_grads.3 = (f32[1,768,768]{2,1,0:T(8,128)}, f32[1,768,768]{2,1,0:T(8,128)}) custom-call(s32[1]{0:T(128)} %bitcast.19.place_ref, bf16[256,768]{1,0:T(8,128)(2,1)} %copy-done.12, bf16[256,768]{1,0:T(8,128)(2,1)} %copy-done.13, bf16[256,768]{1,0:T(8,128)(2,1)} %copy-done.24, bf16[256,768]{1,0:T(8,128)(2,1)} %copy-done.25, bf16[256,768]{1,0:T(8,128)(2,1)} %copy-done, ...), custom_call_target="tpu_custom_call" | custom-call | flops 1024 | bytes 1024 | tf_op jit(solution)/shard_map/expert_grads/pallas_call | solution.py:863
  159.7 2.0 %collective-permute-start.42 = (bf16[128,768]{1,0:T(8,128)(2,1)S(1)}, bf16[128,768]{1,0:T(8,128)(2,1)S(1)}, u32[]{:S(2)}, u32[]{:S(2)}) collective-permute-start(bf16[128,768]{1,0:T(8,128)(2,1)S(1)} %get-tuple-element.219), channel_id=1, source_target_pairs={{0,6},{1,7},{2,4},{3,5},{4,2},{5,3},{6,0},{7,1},{8,14},{9,15},{10,... | collective-permute-start | bytes 589832 | tf_op jit(solution)/shard_map/ppermute | solution.py:537
  161.7 8.8 %expert_grads.4 = (f32[1,768,768]{2,1,0:T(8,128)}, f32[1,768,768]{2,1,0:T(8,128)}) custom-call(s32[1]{0:T(128)} %bitcast.19.place_ref, bf16[256,768]{1,0:T(8,128)(2,1)} %copy-done.30, bf16[256,768]{1,0:T(8,128)(2,1)} %copy-done.33, bf16[256,768]{1,0:T(8,128)(2,1)} %copy-done.28, bf16[256,768]{1,0:T(8,128)(2,1)} %copy-done.29, ...), custom_call_target="tpu_custom_call" | custom-call | flops 1024 | bytes 1024 | tf_op jit(solution)/shard_map/expert_grads/pallas_call | solution.py:863
  172.1 2.0 %collective-permute-start.48 = (bf16[112,768]{1,0:T(8,128)(2,1)S(1)}, bf16[112,768]{1,0:T(8,128)(2,1)S(1)}, u32[]{:S(2)}, u32[]{:S(2)}) collective-permute-start(bf16[112,768]{1,0:T(8,128)(2,1)S(1)} %get-tuple-element.235), channel_id=1, source_target_pairs={{0,6},{1,7},{2,4},{3,5},{4,2},{5,3},{6,0},{7,1},{8,14},{9,15},{10,... | collective-permute-start | bytes 516104 | tf_op jit(solution)/shard_map/ppermute | solution.py:537
  175.2 8.8 %expert_grads.5 = (f32[1,768,768]{2,1,0:T(8,128)}, f32[1,768,768]{2,1,0:T(8,128)}) custom-call(s32[1]{0:T(128)} %bitcast.19.place_ref, bf16[256,768]{1,0:T(8,128)(2,1)} %copy-done.31, bf16[256,768]{1,0:T(8,128)(2,1)} %copy-done.32, bf16[256,768]{1,0:T(8,128)(2,1)} %copy-done.26, bf16[256,768]{1,0:T(8,128)(2,1)} %copy-done.27, ...), custom_call_target="tpu_custom_call" | custom-call | flops 1024 | bytes 1024 | tf_op jit(solution)/shard_map/expert_grads/pallas_call | solution.py:863
  (205 shorter events, 52.1 us)
Async XLA Ops:
  2.2 12.4 %collective-permute-start.2 = (bf16[24,3200]{1,0:T(8,128)(2,1)}, bf16[24,3200]{1,0:T(8,128)(2,1)S(1)}, u32[]{:S(2)}, u32[]{:S(2)}) collective-permute-start(bf16[24,3200]{1,0:T(8,128)(2,1)} %pack.1), channel_id=1, source_target_pairs={{0,6},{1,7},{2,4},{3,5},{4,2},{5,3},{6,0},{7,1},{8,14},{9,15},{10,... | collective-permute-start | bytes 460808 | tf_op jit(solution)/shard_map/ppermute | solution.py:537
  7.3 13.2 %collective-permute-start.1 = (bf16[24,3200]{1,0:T(8,128)(2,1)}, bf16[24,3200]{1,0:T(8,128)(2,1)S(1)}, u32[]{:S(2)}, u32[]{:S(2)}) collective-permute-start(bf16[24,3200]{1,0:T(8,128)(2,1)} %pack.1), channel_id=1, source_target_pairs={{0,4},{1,5},{2,6},{3,7},{4,0},{5,1},{6,2},{7,3},{8,12},{9,13},{10,... | collective-permute-start | bytes 460808 | tf_op jit(solution)/shard_map/ppermute | solution.py:537
  7.3 13.2 %collective-permute-start = (bf16[24,3200]{1,0:T(8,128)(2,1)}, bf16[24,3200]{1,0:T(8,128)(2,1)S(1)}, u32[]{:S(2)}, u32[]{:S(2)}) collective-permute-start(bf16[24,3200]{1,0:T(8,128)(2,1)} %pack.1), channel_id=1, source_target_pairs={{0,2},{1,3},{2,0},{3,1},{4,6},{5,7},{6,4},{7,5},{8,10},{9,11},{10,... | collective-permute-start | bytes 460808 | tf_op jit(solution)/shard_map/ppermute | solution.py:537
  35.0 18.3 %collective-permute-start.10 = (bf16[192,3200]{1,0:T(8,128)(2,1)}, bf16[192,3200]{1,0:T(8,128)(2,1)S(1)}, u32[]{:S(2)}, u32[]{:S(2)}) collective-permute-start(bf16[192,3200]{1,0:T(8,128)(2,1)} %get-tuple-element.146), channel_id=1, source_target_pairs={{0,1},{1,0},{2,3},{3,2},{4,5},{5,4},{6,7},{7,6},{8,9},{9,8},{10,11... | collective-permute-start | bytes 3686408 | tf_op jit(solution)/shard_map/ppermute | solution.py:528
  36.4 16.9 %collective-permute-start.8 = (bf16[192,1664]{1,0:T(8,128)(2,1)S(1)}, bf16[192,1664]{1,0:T(8,128)(2,1)S(1)}, u32[]{:S(2)}, u32[]{:S(2)}) collective-permute-start(bf16[192,1664]{1,0:T(8,128)(2,1)S(1)} %get-tuple-element.144.refs_15_.refs_19_.refs_12_), channel_id=1, source_target_pairs={{0,8},{8,0},{16,24},{24,16},{1,9},{9,1},{17,25},{25,17},{2,10},{10... | collective-permute-start | bytes 1916936 | tf_op jit(solution)/shard_map/ppermute | solution.py:531
  37.0 15.4 %collective-permute-start.7 = (bf16[192,1536]{1,0:T(8,128)(2,1)S(1)}, bf16[192,1536]{1,0:T(8,128)(2,1)S(1)}, u32[]{:S(2)}, u32[]{:S(2)}) collective-permute-start(bf16[192,1536]{1,0:T(8,128)(2,1)S(1)} %copy-done.2), channel_id=1, source_target_pairs={{0,16},{8,24},{16,0},{24,8},{1,17},{9,25},{17,1},{25,9},{2,18},{10... | collective-permute-start | bytes 1769480 | tf_op jit(solution)/shard_map/ppermute | solution.py:534
  38.6 11.5 %collective-permute-start.9 = (bf16[128,768]{1,0:T(8,128)(2,1)S(1)}, bf16[128,768]{1,0:T(8,128)(2,1)S(1)}, u32[]{:S(2)}, u32[]{:S(2)}) collective-permute-start(bf16[128,768]{1,0:T(8,128)(2,1)S(1)} %copy-done.35), channel_id=1, source_target_pairs={{0,4},{1,5},{2,6},{3,7},{4,0},{5,1},{6,2},{7,3},{8,12},{9,13},{10,... | collective-permute-start | bytes 589832 | tf_op jit(solution)/shard_map/ppermute | solution.py:537
  53.8 13.6 %collective-permute-start.13 = (bf16[128,768]{1,0:T(8,128)(2,1)S(1)}, bf16[128,768]{1,0:T(8,128)(2,1)S(1)}, u32[]{:S(2)}, u32[]{:S(2)}) collective-permute-start(bf16[128,768]{1,0:T(8,128)(2,1)S(1)} %copy-done.34), channel_id=1, source_target_pairs={{0,6},{1,7},{2,4},{3,5},{4,2},{5,3},{6,0},{7,1},{8,14},{9,15},{10,... | collective-permute-start | bytes 589832 | tf_op jit(solution)/shard_map/ppermute | solution.py:537
  56.1 11.4 %collective-permute-start.16 = (bf16[256,768]{1,0:T(8,128)(2,1)S(1)}, bf16[256,768]{1,0:T(8,128)(2,1)S(1)}, u32[]{:S(2)}, u32[]{:S(2)}) collective-permute-start(bf16[256,768]{1,0:T(8,128)(2,1)S(1)} %pad_maximum_fusion.first_ref.refs_2_.refs_4_), channel_id=1, source_target_pairs={{0,16},{8,24},{16,0},{24,8},{1,17},{9,25},{17,1},{25,9},{2,18},{10... | collective-permute-start | bytes 1179656 | tf_op jit(solution)/shard_map/ppermute | solution.py:534
  69.2 12.4 %collective-permute-start.19 = (bf16[256,768]{1,0:T(8,128)(2,1)S(1)}, bf16[256,768]{1,0:T(8,128)(2,1)S(1)}, u32[]{:S(2)}, u32[]{:S(2)}) collective-permute-start(bf16[256,768]{1,0:T(8,128)(2,1)S(1)} %constant_dynamic-update-slice_fusion.second_ref.refs_2_.refs_5_), channel_id=1, source_target_pairs={{0,8},{8,0},{16,24},{24,16},{1,9},{9,1},{17,25},{25,17},{2,10},{10... | collective-permute-start | bytes 1179656 | tf_op jit(solution)/shard_map/ppermute | solution.py:531
  70.5 11.0 %collective-permute-start.18 = (bf16[256,768]{1,0:T(8,128)(2,1)S(1)}, bf16[256,768]{1,0:T(8,128)(2,1)S(1)}, u32[]{:S(2)}, u32[]{:S(2)}) collective-permute-start(bf16[256,768]{1,0:T(8,128)(2,1)S(1)} %constant_dynamic-update-slice_fusion.second_ref.refs_2_.refs_5_), channel_id=1, source_target_pairs={{0,16},{8,24},{16,0},{24,8},{1,17},{9,25},{17,1},{25,9},{2,18},{10... | collective-permute-start | bytes 1179656 | tf_op jit(solution)/shard_map/ppermute | solution.py:534
  81.6 11.1 %collective-permute-start.22 = (bf16[256,768]{1,0:T(8,128)(2,1)S(1)}, bf16[256,768]{1,0:T(8,128)(2,1)S(1)}, u32[]{:S(2)}, u32[]{:S(2)}) collective-permute-start(bf16[256,768]{1,0:T(8,128)(2,1)S(1)} %collective-permute-done.15.refs_6_), channel_id=1, source_target_pairs={{0,16},{8,24},{16,0},{24,8},{1,17},{9,25},{17,1},{25,9},{2,18},{10... | collective-permute-start | bytes 1179656 | tf_op jit(solution)/shard_map/ppermute | solution.py:534
  83.2 10.8 %collective-permute-start.23 = (bf16[256,768]{1,0:T(8,128)(2,1)S(1)}, bf16[256,768]{1,0:T(8,128)(2,1)S(1)}, u32[]{:S(2)}, u32[]{:S(2)}) collective-permute-start(bf16[256,768]{1,0:T(8,128)(2,1)S(1)} %collective-permute-done.18.refs_7_), channel_id=1, source_target_pairs={{0,8},{8,0},{16,24},{24,16},{1,9},{9,1},{17,25},{25,17},{2,10},{10... | collective-permute-start | bytes 1179656 | tf_op jit(solution)/shard_map/ppermute | solution.py:531
  83.9 11.1 %collective-permute-start.21 = (bf16[128,768]{1,0:T(8,128)(2,1)S(1)}, bf16[128,768]{1,0:T(8,128)(2,1)S(1)}, u32[]{:S(2)}, u32[]{:S(2)}) collective-permute-start(bf16[128,768]{1,0:T(8,128)(2,1)S(1)} %get-tuple-element.169), channel_id=1, source_target_pairs={{0,6},{1,7},{2,4},{3,5},{4,2},{5,3},{6,0},{7,1},{8,14},{9,15},{10,... | collective-permute-start | bytes 589832 | tf_op jit(solution)/shard_map/ppermute | solution.py:537
  91.4 16.9 %collective-permute-start.29 = (bf16[256,768]{1,0:T(8,128)(2,1)S(1)}, bf16[256,768]{1,0:T(8,128)(2,1)S(1)}, u32[]{:S(2)}, u32[]{:S(2)}) collective-permute-start(bf16[256,768]{1,0:T(8,128)(2,1)S(1)} %get-tuple-element.184.refs_0_), channel_id=1, source_target_pairs={{0,16},{8,24},{16,0},{24,8},{1,17},{9,25},{17,1},{25,9},{2,18},{10... | collective-permute-start | bytes 1179656 | tf_op jit(solution)/shard_map/ppermute | solution.py:534
  92.7 15.7 %collective-permute-start.28 = (bf16[256,768]{1,0:T(8,128)(2,1)S(1)}, bf16[256,768]{1,0:T(8,128)(2,1)S(1)}, u32[]{:S(2)}, u32[]{:S(2)}) collective-permute-start(bf16[256,768]{1,0:T(8,128)(2,1)S(1)} %get-tuple-element.184.refs_0_), channel_id=1, source_target_pairs={{0,8},{8,0},{16,24},{24,16},{1,9},{9,1},{17,25},{25,17},{2,10},{10... | collective-permute-start | bytes 1179656 | tf_op jit(solution)/shard_map/ppermute | solution.py:531
  104.3 11.2 %collective-permute-start.26 = (bf16[128,768]{1,0:T(8,128)(2,1)S(1)}, bf16[128,768]{1,0:T(8,128)(2,1)S(1)}, u32[]{:S(2)}, u32[]{:S(2)}) collective-permute-start(bf16[128,768]{1,0:T(8,128)(2,1)S(1)} %get-tuple-element.182), channel_id=1, source_target_pairs={{0,6},{1,7},{2,4},{3,5},{4,2},{5,3},{6,0},{7,1},{8,14},{9,15},{10,... | collective-permute-start | bytes 589832 | tf_op jit(solution)/shard_map/ppermute | solution.py:537
  121.0 12.0 %collective-permute-start.32 = (bf16[640,768]{1,0:T(8,128)(2,1)S(1)}, bf16[640,768]{1,0:T(8,128)(2,1)S(1)}, u32[]{:S(2)}, u32[]{:S(2)}) collective-permute-start(bf16[640,768]{1,0:T(8,128)(2,1)S(1)} %get-tuple-element.194.refs_1_.vo_ref), channel_id=1, source_target_pairs={{0,1},{1,0},{2,3},{3,2},{4,5},{5,4},{6,7},{7,6},{8,9},{9,8},{10,11... | collective-permute-start | bytes 2949128 | tf_op jit(solution)/shard_map/ppermute | solution.py:528
  121.1 11.5 %collective-permute-start.33 = (bf16[256,768]{1,0:T(8,128)(2,1)S(1)}, bf16[256,768]{1,0:T(8,128)(2,1)S(1)}, u32[]{:S(2)}, u32[]{:S(2)}) collective-permute-start(bf16[256,768]{1,0:T(8,128)(2,1)S(1)} %collective-permute-done.28.refs_2_), channel_id=1, source_target_pairs={{0,16},{8,24},{16,0},{24,8},{1,17},{9,25},{17,1},{25,9},{2,18},{10... | collective-permute-start | bytes 1179656 | tf_op jit(solution)/shard_map/ppermute | solution.py:534
  121.8 11.2 %collective-permute-start.34 = (bf16[256,768]{1,0:T(8,128)(2,1)S(1)}, bf16[256,768]{1,0:T(8,128)(2,1)S(1)}, u32[]{:S(2)}, u32[]{:S(2)}) collective-permute-start(bf16[256,768]{1,0:T(8,128)(2,1)S(1)} %collective-permute-done.30.refs_3_), channel_id=1, source_target_pairs={{0,8},{8,0},{16,24},{24,16},{1,9},{9,1},{17,25},{25,17},{2,10},{10... | collective-permute-start | bytes 1179656 | tf_op jit(solution)/shard_map/ppermute | solution.py:531
  139.5 16.7 %collective-permute-start.36 = (bf16[192,1536]{1,0:T(8,128)(2,1)S(1)}, bf16[192,1536]{1,0:T(8,128)(2,1)S(1)}, u32[]{:S(2)}, u32[]{:S(2)}) collective-permute-start(bf16[192,1536]{1,0:T(8,128)(2,1)S(1)} %get-tuple-element.207), channel_id=1, source_target_pairs={{0,16},{8,24},{16,0},{24,8},{1,17},{9,25},{17,1},{25,9},{2,18},{10... | collective-permute-start | bytes 1769480 | tf_op jit(solution)/shard_map/ppermute | solution.py:534
  141.0 15.3 %collective-permute-start.38 = (bf16[192,1536]{1,0:T(8,128)(2,1)S(1)}, bf16[192,1536]{1,0:T(8,128)(2,1)S(1)}, u32[]{:S(2)}, u32[]{:S(2)}) collective-permute-start(bf16[192,1536]{1,0:T(8,128)(2,1)S(1)} %get-tuple-element.208), channel_id=1, source_target_pairs={{0,8},{8,0},{16,24},{24,16},{1,9},{9,1},{17,25},{25,17},{2,10},{10... | collective-permute-start | bytes 1769480 | tf_op jit(solution)/shard_map/ppermute | solution.py:531
  141.6 14.6 %collective-permute-start.37 = (bf16[128,768]{1,0:T(8,128)(2,1)S(1)}, bf16[128,768]{1,0:T(8,128)(2,1)S(1)}, u32[]{:S(2)}, u32[]{:S(2)}) collective-permute-start(bf16[128,768]{1,0:T(8,128)(2,1)S(1)} %get-tuple-element.212), channel_id=1, source_target_pairs={{0,4},{1,5},{2,6},{3,7},{4,0},{5,1},{6,2},{7,3},{8,12},{9,13},{10,... | collective-permute-start | bytes 589832 | tf_op jit(solution)/shard_map/ppermute | solution.py:537
  144.1 12.1 %collective-permute-start.40 = (f32[16,768]{1,0:T(8,128)S(1)}, f32[16,768]{1,0:T(8,128)S(1)}, u32[]{:S(2)}, u32[]{:S(2)}) collective-permute-start(f32[16,768]{1,0:T(8,128)S(1)} %add.88.small_ref), channel_id=1, source_target_pairs={{0,16},{8,24},{16,0},{24,8},{1,17},{9,25},{17,1},{25,9},{2,18},{10... | collective-permute-start | bytes 147464 | tf_op jit(solution)/shard_map/ppermute | solution.py:534
  156.5 14.0 %collective-permute-start.41 = (bf16[128,768]{1,0:T(8,128)(2,1)S(1)}, bf16[128,768]{1,0:T(8,128)(2,1)S(1)}, u32[]{:S(2)}, u32[]{:S(2)}) collective-permute-start(bf16[128,768]{1,0:T(8,128)(2,1)S(1)} %get-tuple-element.218), channel_id=1, source_target_pairs={{0,2},{1,3},{2,0},{3,1},{4,6},{5,7},{6,4},{7,5},{8,10},{9,11},{10,... | collective-permute-start | bytes 589832 | tf_op jit(solution)/shard_map/ppermute | solution.py:537
  157.9 13.3 %collective-permute-start.44 = (bf16[96,1536]{1,0:T(8,128)(2,1)S(1)}, bf16[96,1536]{1,0:T(8,128)(2,1)S(1)}, u32[]{:S(2)}, u32[]{:S(2)}) collective-permute-start(bf16[96,1536]{1,0:T(8,128)(2,1)S(1)} %get-tuple-element.217), channel_id=1, source_target_pairs={{0,16},{8,24},{16,0},{24,8},{1,17},{9,25},{17,1},{25,9},{2,18},{10... | collective-permute-start | bytes 884744 | tf_op jit(solution)/shard_map/ppermute | solution.py:534
  158.7 12.6 %collective-permute-start.43 = (bf16[112,1536]{1,0:T(8,128)(2,1)S(1)}, bf16[112,1536]{1,0:T(8,128)(2,1)S(1)}, u32[]{:S(2)}, u32[]{:S(2)}) collective-permute-start(bf16[112,1536]{1,0:T(8,128)(2,1)S(1)} %get-tuple-element.216.a_low_ref), channel_id=1, source_target_pairs={{0,8},{8,0},{16,24},{24,16},{1,9},{9,1},{17,25},{25,17},{2,10},{10... | collective-permute-start | bytes 1032200 | tf_op jit(solution)/shard_map/ppermute | solution.py:531
  159.7 10.8 %collective-permute-start.42 = (bf16[128,768]{1,0:T(8,128)(2,1)S(1)}, bf16[128,768]{1,0:T(8,128)(2,1)S(1)}, u32[]{:S(2)}, u32[]{:S(2)}) collective-permute-start(bf16[128,768]{1,0:T(8,128)(2,1)S(1)} %get-tuple-element.219), channel_id=1, source_target_pairs={{0,6},{1,7},{2,4},{3,5},{4,2},{5,3},{6,0},{7,1},{8,14},{9,15},{10,... | collective-permute-start | bytes 589832 | tf_op jit(solution)/shard_map/ppermute | solution.py:537
  171.4 12.5 %collective-permute-start.45 = (bf16[256,768]{1,0:T(8,128)(2,1)}, bf16[256,768]{1,0:T(8,128)(2,1)S(1)}, u32[]{:S(2)}, u32[]{:S(2)}) collective-permute-start(bf16[256,768]{1,0:T(8,128)(2,1)} %pad_maximum_fusion.2), channel_id=1, source_target_pairs={{0,1},{1,0},{2,3},{3,2},{4,5},{5,4},{6,7},{7,6},{8,9},{9,8},{10,11... | collective-permute-start | bytes 1179656 | tf_op jit(solution)/shard_map/ppermute | solution.py:528
  171.6 14.7 %collective-permute-start.47 = (bf16[112,768]{1,0:T(8,128)(2,1)S(1)}, bf16[112,768]{1,0:T(8,128)(2,1)S(1)}, u32[]{:S(2)}, u32[]{:S(2)}) collective-permute-start(bf16[112,768]{1,0:T(8,128)(2,1)S(1)} %get-tuple-element.234), channel_id=1, source_target_pairs={{0,4},{1,5},{2,6},{3,7},{4,0},{5,1},{6,2},{7,3},{8,12},{9,13},{10,... | collective-permute-start | bytes 516104 | tf_op jit(solution)/shard_map/ppermute | solution.py:537
  172.1 14.2 %collective-permute-start.48 = (bf16[112,768]{1,0:T(8,128)(2,1)S(1)}, bf16[112,768]{1,0:T(8,128)(2,1)S(1)}, u32[]{:S(2)}, u32[]{:S(2)}) collective-permute-start(bf16[112,768]{1,0:T(8,128)(2,1)S(1)} %get-tuple-element.235), channel_id=1, source_target_pairs={{0,6},{1,7},{2,4},{3,5},{4,2},{5,3},{6,0},{7,1},{8,14},{9,15},{10,... | collective-permute-start | bytes 516104 | tf_op jit(solution)/shard_map/ppermute | solution.py:537
  174.1 13.5 %collective-permute-start.46 = (bf16[112,768]{1,0:T(8,128)(2,1)S(1)}, bf16[112,768]{1,0:T(8,128)(2,1)S(1)}, u32[]{:S(2)}, u32[]{:S(2)}) collective-permute-start(bf16[112,768]{1,0:T(8,128)(2,1)S(1)} %get-tuple-element.233.own_ref), channel_id=1, source_target_pairs={{0,2},{1,3},{2,0},{3,1},{4,6},{5,7},{6,4},{7,5},{8,10},{9,11},{10,... | collective-permute-start | bytes 516104 | tf_op jit(solution)/shard_map/ppermute | solution.py:537
  (57 other events, 574.9 us)

commit v4 on v3

--- a/solution.py
+++ b/solution.py
@@ -169,7 +169,7 @@
 def fill_x_first(pieces, out_ref):
     half = pieces[0].shape[0]
     for number, piece in enumerate(pieces):
-        out_ref[number * half : (number + 1) * half, :] = piece[...]
+        out_ref[number * half : (number + 1) * half, :] = piece[:, : out_ref.shape[1]]
 
 
 def fill_y_first(pieces, out_ref, starts=(0, 0, 0, 0)):
@@ -186,65 +186,63 @@
         out_ref[base + half + part : base + 2 * half, :] = other[part:, at_other]
 
 
-def near_kernel(qv_ref, qv_x_ref, ko_ref, ko_y_ref, qv_near_ref, ko_near_ref, both_ref):
+def near_kernel(qv_ref, qv_x_ref, ko_ref, ko_y_ref, qv_near_ref, ko_near_ref, both_ref, qv_kept_ref, ko_kept_ref):
     part, width = qv_ref.shape
     for number, (left, right) in enumerate(((qv_ref, ko_ref), (qv_x_ref, ko_y_ref))):
         at = slice(number * part, (number + 1) * part)
         qv_near_ref[at, :] = left[...]
         ko_near_ref[at, :] = right[...]
+        qv_kept_ref[at, :] = left[...]
+        ko_kept_ref[at, :] = right[...]
         both_ref[at, :width] = left[...]
         both_ref[at, width:] = right[...]
 
 
 def attend_kernel(head, *refs):
     normed_ref, bias_ref, perm_ref, x_ref, gain_ref, slots_ref, picked_ref = refs[:7]
-    wq_refs, wv_refs, wk_refs, ko_refs = refs[7:11], refs[11:15], refs[15:19], refs[19:23]
-    q_ref, k_ref, v_ref, probs_ref, mixed_ref, mixed_other_ref = refs[23:29]
-    middle_ref, router_ref, gate_ref, keep_ref, send_ref = refs[29:34]
-    wq, wk, wv, wo, mixed = refs[34:]
-    step = pl.program_id(0)
+    qv_refs, ko_refs = refs[7:11], refs[11:15]
+    q_ref, k_ref, v_ref, probs_ref, mixed_ref, mixed_other_ref = refs[15:21]
+    middle_ref, router_ref, gate_ref, keep_ref, send_ref = refs[21:26]
+    wqv, wk, wo = refs[26:]
     experts = router_ref.shape[1]
     model = x_ref.shape[1]
 
-    fill_x_first(wq_refs, wq)
-    fill_y_first(wk_refs, wk)
-    fill_x_first(wv_refs, wv)
+    fill_x_first(qv_refs, wqv)
+    fill_y_first(ko_refs, wk, (0, 0, 2 * model, 0))
+    fill_y_first(ko_refs, wo, (model, model, 3 * model, model))
     normed = normed_ref[...]
-    q = mm(normed, wq[...]).astype(BF)
-    k = mm(normed, wk[...]).astype(BF)
-    v = mm(normed, wv[...]).astype(BF)
-    q_ref[...] = q
-    k_ref[...] = k
-    v_ref[...] = v
-    rows = []
-    for h in range(q.shape[1] // head):
-        part = slice(h * head, (h + 1) * head)
-        scores = mm_nt(q[:, part], k[:, part]) + bias_ref[h]
-        exponent = jnp.exp(scores - jnp.max(scores, axis=-1, keepdims=True))
-        probs = exponent / jnp.sum(exponent, axis=-1, keepdims=True)
-        probs_ref[h] = probs
-        rows.append(mm(probs.astype(BF), v[:, part]))
-    mixed[step] = jnp.concatenate(rows, axis=1).astype(BF)
-
-    @pl.when(step == pl.num_programs(0) - 1)
-    def _():
-        fill_y_first(ko_refs, wo, (model, model, 3 * model, model))
-        perm = perm_ref[...]
-        every = jnp.concatenate([mixed[g] for g in range(mixed.shape[0])], axis=1)
-        mixed_in_order = mm(every, perm).astype(BF)
-        mixed_ref[...] = mixed_in_order[:, : model // 2]
-        mixed_other_ref[...] = mixed_in_order[:, model // 2 :]
-        middle = x_ref[...].astype(F32) + mm(mixed_in_order, wo[:, :model])
-        middle_ref[...] = middle
-        scale = lax.rsqrt(jnp.mean(middle * middle, axis=-1, keepdims=True) + EPSILON)
-        ffn_in = (middle * scale * gain_ref[...]).astype(BF)
-        router = mm(perm, wo[:, model:]).astype(BF)[:, :experts]
-        router_ref[...] = router
-        rows = mm(slots_ref[...], ffn_in).astype(BF)
-        gate_ref[...] = gate_of(ffn_in, router, picked_ref[...])[1]
-        half = rows.shape[0] // 2
-        keep_ref[...] = rows[:half]
-        send_ref[...] = rows[half:]
+    mixed = []
+    for group in range(model // GROUP):
+        at = slice(group * GROUP, (group + 1) * GROUP)
+        q = mm(normed, wqv[:, at]).astype(BF)
+        k = mm(normed, wk[:, at]).astype(BF)
+        v = mm(normed, wqv[:, model + group * GROUP : model + (group + 1) * GROUP]).astype(BF)
+        q_ref[:, at] = q
+        k_ref[:, at] = k
+        v_ref[:, at] = v
+        for h in range(GROUP // head):
+            part = slice(h * head, (h + 1) * head)
+            number = group * (GROUP // head) + h
+            scores = mm_nt(q[:, part], k[:, part]) + bias_ref[number]
+            exponent = jnp.exp(scores - jnp.max(scores, axis=-1, keepdims=True))
+            probs = exponent / jnp.sum(exponent, axis=-1, keepdims=True)
+            probs_ref[number] = probs
+            mixed.append(mm(probs.astype(BF), v[:, part]))
+    perm = perm_ref[...]
+    mixed_in_order = mm(jnp.concatenate(mixed, axis=1).astype(BF), perm).astype(BF)
+    mixed_ref[...] = mixed_in_order[:, : model // 2]
+    mixed_other_ref[...] = mixed_in_order[:, model // 2 :]
+    middle = x_ref[...].astype(F32) + mm(mixed_in_order, wo[:, :model])
+    middle_ref[...] = middle
+    scale = lax.rsqrt(jnp.mean(middle * middle, axis=-1, keepdims=True) + EPSILON)
+    ffn_in = (middle * scale * gain_ref[...]).astype(BF)
+    router = mm(perm, wo[:, model:]).astype(BF)[:, :experts]
+    router_ref[...] = router
+    rows = mm(slots_ref[...], ffn_in).astype(BF)
+    gate_ref[...] = gate_of(ffn_in, router, picked_ref[...])[1]
+    half = rows.shape[0] // 2
+    keep_ref[...] = rows[:half]
+    send_ref[...] = rows[half:]
 
 
 def join(refs, out_ref):
@@ -314,6 +312,48 @@
     part_out((back + mm_nt(logit_grad, router_ref[...])).astype(BF), back_refs)
 
 
+def expert_grad_rows(pieces, refs, own_ref, router_ref, rows_all, branch_all):
+    join(refs[:pieces], rows_all)
+    join(refs[pieces:], branch_all)
+    picked = one_lane((rows_all.shape[0], router_ref.shape[1]), own_ref[0])
+    gate = gate_of(rows_all[...], router_ref[...], picked)[1]
+    branch_all[...] = (branch_all[...].astype(F32) * gate).astype(BF)
+
+
+def expert_grad_part(rows, branch, w1, w2):
+    hidden, slope = gelu_parts(mm(rows, w1))
+    pre_grad = (mm_nt(branch, w2) * slope).astype(BF)
+    return mm_tn(rows, pre_grad), mm_tn(hidden.astype(BF), branch)
+
+
+def first_expert_grad_kernel(pieces, own_ref, place_ref, *refs):
+    router_ref, w1_ref, w2_ref, g1_ref, g2_ref, rows_all, branch_all = refs[2 * pieces :]
+    expert_grad_rows(pieces, refs[: 2 * pieces], own_ref, router_ref, rows_all, branch_all)
+    width = g1_ref.shape[1]
+    for part in range(width // GROUP):
+        at = pl.ds(pl.multiple_of(place_ref[0] * width + part * GROUP, GROUP), GROUP)
+        here = slice(part * GROUP, (part + 1) * GROUP)
+        g1, g2 = expert_grad_part(rows_all[...], branch_all[...], w1_ref[:, at], w2_ref[at, :])
+        g1_ref[:, here] = g1
+        g2_ref[here, :] = g2
+
+
+def next_expert_grad_kernel(pieces, own_ref, place_ref, *refs):
+    router_ref, w1_ref, w2_ref, before1_ref, before2_ref, g1_ref, g2_ref, rows_all, branch_all = refs[2 * pieces :]
+    step = pl.program_id(0)
+
+    @pl.when(step == 0)
+    def _():
+        expert_grad_rows(pieces, refs[: 2 * pieces], own_ref, router_ref, rows_all, branch_all)
+
+    width = before1_ref.shape[1]
+    at = pl.ds(pl.multiple_of(place_ref[0] * width + step * GROUP, GROUP), GROUP)
+    here = pl.ds(pl.multiple_of(step * GROUP, GROUP), GROUP)
+    g1, g2 = expert_grad_part(rows_all[...], branch_all[...], w1_ref[:, at], w2_ref[at, :])
+    g1_ref[0] = g1 + before1_ref[:, here]
+    g2_ref[0] = g2 + before2_ref[here, :]
+
+
 def expert_grad_kernel(pieces, more, place_ref, *refs):
     del place_ref
     rows_refs, dy_refs, refs = refs[:pieces], refs[pieces : 2 * pieces], refs[2 * pieces :]
@@ -439,14 +479,25 @@
             keep_ref[...] = jnp.concatenate(blocks, axis=0)
 
 
-def fold_last_kernel(keep_ref, own_ref, *refs):
+def fold_last_kernel(heads, device_ref, keep_ref, own_ref, *refs):
     got, outs = [ref[...].astype(F32) for ref in refs[:3]], refs[3:]
     shard = outs[0].shape[0]
-    first = outs[4].shape[0]
+    experts = outs[7].shape[0]
+    first = got[0].shape[0] - 4 * shard
     total = keep_ref[...] + ((got[0][first:] + got[1][first:]) + got[2][first:])
     for number in range(4):
         outs[number][...] = total[number * shard : (number + 1) * shard]
-    outs[4][...] = (own_ref[...][:first].astype(F32) + got[0][:first]) + (got[1][:first] + got[2][:first])
+    small = (own_ref[...][:first].astype(F32) + got[0][:first]) + (got[1][:first] + got[2][:first])
+    outs[4][...] = small[experts : experts + 1]
+    outs[5][...] = small[experts + 1 : experts + 2]
+    every = outs[6].shape[1]
+    line = small[experts + 2 : experts + 3]
+    outs[6][...] = jnp.concatenate([line[:, h * every : (h + 1) * every] for h in range(heads)], axis=0)
+    spots = (small.shape[1], shard)
+    mine = lax.broadcasted_iota(jnp.int32, spots, 0) == lax.broadcasted_iota(jnp.int32, spots, 1) + device_ref[0] * shard
+    outs[7][...] = lax.dot_general(
+        small[:experts], mine.astype(F32), (((1,), (0,)), ((), ())), precision=PRECISE, preferred_element_type=F32
+    )
 
 
 def score_grad_kernel(head, mixed_grad_ref, v_ref, q_ref, k_ref, probs_ref, grads_ref, along_ref):
@@ -706,19 +757,11 @@
     normed_side = dy_got[half:]
     dy_got = dy_got[:half]
     qv, ko = line[:, : 2 * model], line[:, 2 * model :]
-    qv, ko = all_after([qv, ko], dy_got)
+    qv, ko = all_after([qv, ko], slots_t)
     dy_keep, dy_got = all_after([dy_keep, dy_got], qv, ko)
     part_rows = qv.shape[0]
     dy_blocks = at.by_z(dy_keep, dy_got)
     dy_one = at.send_more(dy_blocks, 1, (dy_blocks,))
-    qv_near, ko_near, both_near = pl.pallas_call(
-        near_kernel,
-        out_shape=tuple(shape_of((2 * part_rows, width), BF) for width in (2 * model, 2 * model + 128, 4 * model + 128)),
-        in_specs=[pl.BlockSpec(memory_space=pltpu.VMEM)] * 4,
-        out_specs=(pl.BlockSpec(memory_space=pltpu.VMEM),) * 3,
-        compiler_params=params(),
-        name="near",
-    )(after(qv, dy_one), at.x(qv), ko, at.y(ko))
     bias = pl.pallas_call(
         bias_kernel,
         grid=(groups,),
@@ -729,8 +772,18 @@
         compiler_params=params(),
         cost_estimate=cost(1 << 20, 4 * head_count * rows * rows),
         name="bias",
-    )(after(bucket_line, qv, ko), rel_table)
-    qv_far, ko_far = at.gather_far(*all_after([qv_near, ko_near], bias))
+    )(after(bucket_line, slots_t), rel_table)
+    qv_near, ko_near, both_near, qv_kept, ko_kept = pl.pallas_call(
+        near_kernel,
+        out_shape=tuple(pltpu.HBM((2 * part_rows, width), BF) for width in (2 * model, 2 * model + 128, 4 * model + 128))
+        + tuple(shape_of((2 * part_rows, width), BF) for width in (2 * model, 2 * model + 128)),
+        in_specs=[pl.BlockSpec(memory_space=pltpu.VMEM)] * 4,
+        out_specs=tuple(pl.BlockSpec((2 * part_rows, width), lambda: (0, 0)) for width in (2 * model, 2 * model + 128, 4 * model + 128))
+        + (pl.BlockSpec(memory_space=pltpu.VMEM),) * 2,
+        compiler_params=params(),
+        name="near",
+    )(after(qv, dy_one, bias), at.x(qv), ko, at.y(ko))
+    qv_far, ko_far = at.gather_far(qv_near, ko_near)
     w_first, w_second, loaded = pl.pallas_call(
         load_kernel,
         out_shape=(pltpu.VMEM((model, hidden), BF), pltpu.VMEM((hidden, model), BF), shape_of((8, 128), F32)),
@@ -744,8 +797,8 @@
     dy_two = at.send_more(dy_blocks, 2, (qv_near, dy_one))
     qv_far, ko_far, dy_two = all_after([qv_far, ko_far, dy_two], both_side)
     dy_three = at.send_more(dy_blocks, 3, (qv_far, ko_far, dy_two))
-    qv_pieces = (qv_near, qv_far, both_side, at.core(qv_far))
-    ko_pieces = (ko_near, ko_far, both_side, at.core(ko_far))
+    qv_pieces = (qv_kept, qv_far, both_side, at.core(qv_far))
+    ko_pieces = (ko_kept, ko_far, both_side, at.core(ko_far))
     if at.near:
         dy_a = jnp.concatenate([dy_blocks[0], dy_two], axis=0)
     else:
@@ -757,54 +810,43 @@
     wide = ko_near.shape[1]
     side_wide = both_side.shape[1]
     head_block = pl.BlockSpec((per_group, rows, rows), lambda g: (g, 0, 0))
-    later = pl.BlockSpec((quarter, GROUP), lambda g: (0, groups + g))
-    side_k = pl.BlockSpec((quarter, GROUP), lambda g: (0, 2 * groups + g))
-    first_k = cols(quarter, GROUP)
+    in_vmem = pl.BlockSpec(memory_space=pltpu.VMEM)
     ko_full = [full((quarter, wide)), full((quarter, wide)), full((quarter, side_wide)), full((quarter, wide))]
+    attend_shapes = [((rows, model), BF)] * 3 + [
+        ((head_count, rows, rows), F32),
+        ((rows, model // 2), BF),
+        ((rows, model // 2), BF),
+        ((rows, model), F32),
+        ((model, experts), BF),
+        ((rows, 1), F32),
+        ((half, model), BF),
+        ((half, model), BF),
+    ]
     q, k, v, probs, mixed, mixed_other, middle, router, gate, keep, send = pl.pallas_call(
         functools.partial(attend_kernel, head),
-        grid=(groups,),
-        out_shape=(shape_of((rows, model), BF),) * 3
-        + (
-            shape_of((head_count, rows, rows), F32),
-            shape_of((rows, model // 2), BF),
-            shape_of((rows, model // 2), BF),
-            shape_of((rows, model), F32),
-            shape_of((model, experts), BF),
-            shape_of((rows, 1), F32),
-            shape_of((half, model), BF),
-            shape_of((half, model), BF),
-        ),
-        in_specs=[
-            full((rows, model)),
-            head_block,
-            full((model, model)),
-            full((rows, model)),
-            full((1, model)),
-            full((slots, rows)),
-            full((rows, experts)),
-        ]
-        + [cols(quarter, GROUP)] * 4
-        + [later] * 4
-        + [first_k, first_k, side_k, first_k]
-        + ko_full,
-        out_specs=(cols(rows, GROUP),) * 3
-        + (
-            head_block,
-            full((rows, model // 2)),
-            full((rows, model // 2)),
-            full((rows, model)),
-            full((model, experts)),
-            full((rows, 1)),
-            full((half, model)),
-            full((half, model)),
-        ),
-        scratch_shapes=[pltpu.VMEM((model, GROUP), BF)] * 3
-        + [pltpu.VMEM((model, wide - model), BF), pltpu.VMEM((groups, rows, GROUP), BF)],
+        out_shape=tuple(pltpu.HBM(*v) if v[0] == (rows, 1) else shape_of(*v) for v in attend_shapes),
+        in_specs=[in_vmem] * 3
+        + [pl.BlockSpec((rows, model), lambda: (0, 0)), in_vmem]
+        + [pl.BlockSpec((slots, rows), lambda: (0, 0)), pl.BlockSpec((rows, experts), lambda: (0, 0))]
+        + [in_vmem] * 8,
+        out_specs=(in_vmem,) * 8 + (pl.BlockSpec((rows, 1), lambda: (0, 0)),) + (in_vmem,) * 2,
+        scratch_shapes=[
+            pltpu.VMEM((model, 2 * model), BF),
+            pltpu.VMEM((model, model), BF),
+            pltpu.VMEM((model, wide - model), BF),
+        ],
         compiler_params=params(),
-        cost_estimate=cost(8 * rows * model * model, 12 * model * model),
         name="attend",
-    )(normed, bias, perm, *in_hbm(tokens), after(gain_ffn, loaded), *in_hbm(slots_map), picked, *qv_pieces, *qv_pieces, *ko_pieces, *ko_pieces)
+    )(
+        normed,
+        bias,
+        perm,
+        *in_hbm(tokens),
+        after(gain_ffn, loaded),
+        *in_hbm(slots_map, picked),
+        *qv_pieces,
+        *ko_pieces,
+    )
 
     got = at.core(after(send, dy_three))
     first, second = at.to_owners(keep, got, (dy_ax, dy_ay))
@@ -812,7 +854,6 @@
         dy_b = jnp.concatenate([dy_one, dy_three], axis=0)
     dy_b_later = after(dy_b, got, dy_ax, dy_ay)
     dy_by, dy_bx = at.y(dy_b_later), at.x(dy_b_later)
-    in_vmem = pl.BlockSpec(memory_space=pltpu.VMEM)
     hidden_grads = pl.pallas_call(
         hidden_grad_kernel,
         out_shape=(shape_of((half, hidden), F32),) * 2,
@@ -881,6 +922,38 @@
             cost_estimate=cost(8 * count * model * slice_width, 20 * model * slice_width),
             name="expert_grads",
         )(place, *in_hbm(*rows_list, *dy_list), own, router_in, expert_in, expert_out, *in_hbm(*before))
+
+    whole_vmem = pl.BlockSpec(memory_space=pltpu.VMEM)
+
+    def first_expert_grads(rows_list, dy_list, router_in):
+        count = sum(v.shape[0] for v in rows_list)
+        ins = [*rows_list, *dy_list, router_in, w_first, w_second]
+        return pl.pallas_call(
+            functools.partial(first_expert_grad_kernel, len(rows_list)),
+            out_shape=(shape_of((model, slice_width), F32), shape_of((slice_width, model), F32)),
+            in_specs=[smem] * 2 + [whole_vmem] * len(ins),
+            out_specs=(whole_vmem,) * 2,
+            scratch_shapes=[pltpu.VMEM((count, model), BF)] * 2,
+            compiler_params=params(24),
+            name="expert_grads",
+        )(own, place, *ins)
+
+    def next_expert_grads(rows_list, dy_list, router_in, before):
+        count = sum(v.shape[0] for v in rows_list)
+        pieces = [*rows_list, *dy_list]
+        return pl.pallas_call(
+            functools.partial(next_expert_grad_kernel, len(rows_list)),
+            grid=(slice_width // GROUP,),
+            out_shape=(pltpu.HBM((1, model, slice_width), F32), pltpu.HBM((1, slice_width, model), F32)),
+            in_specs=[smem] * 2 + [full(v.shape) for v in pieces] + [whole_vmem] * 5,
+            out_specs=(
+                pl.BlockSpec((1, model, GROUP), lambda g: (0, 0, g)),
+                pl.BlockSpec((1, GROUP, model), lambda g: (0, g, 0)),
+            ),
+            scratch_shapes=[pltpu.VMEM((count, model), BF)] * 2,
+            compiler_params=params(24),
+            name="expert_grads",
+        )(own, place, *in_hbm(*pieces), router_in, w_first, w_second, *before)
 
     rows_axy, rows_byx = at.y(after(rows_ax, rows_by, rows_bx, back_send)), at.x(after(rows_by, rows_bx, back_send))
 
@@ -977,7 +1050,7 @@
         "weight_grads",
         [((quarter_rows, pair), F32), ((quarter_rows, pair), BF)] * 2,
         normed,
-        after(normed_side, small),
+        normed_side,
         mixed,
         vo_grads,
         vo_side,
@@ -991,11 +1064,8 @@
         home_two = at.far(after(returned_a[1], a_low, b_low), 2)
     else:
         home_two = at.apart(jnp.concatenate([*returned_a, *returned_b], axis=0).reshape(nz, -1, model))
-    near_sums = expert_grads(
-        [rows_a, rows_b, rows_ax, rows_by],
-        [dy_a, dy_b, dy_ax, dy_by],
-        after(router, a_low, b_low),
-        (),
+    near_sums = first_expert_grads(
+        [rows_a, rows_b, rows_ax, rows_by], [dy_a, dy_b, dy_ax, dy_by], after(router, a_low, b_low)
     )
     eighth = quarter_rows // 2
     a, a_low, b, b_low = vmem_call(
@@ -1010,7 +1080,7 @@
         small_got,
     )
     a_got, b_got = at.x(a_low), at.y(b_low)
-    mid_sums = expert_grads([rows_ay, rows_bx], [dy_ay, dy_bx], after(router, a_low, b_low), near_sums)
+    mid_sums = next_expert_grads([rows_ay, rows_bx], [dy_ay, dy_bx], after(router, a_low, b_low), near_sums)
     if at.near:
         home = [at.far(v, k) for v, k in zip(all_after([returned_b[1], returned_b[0]], a_low, b_low), (3, 1))]
         home_blocks = [returned_a[0], home[1], home_two, home[0]]
@@ -1050,28 +1120,33 @@
         jnp.concatenate([v[:keep_rows] for v in returned_keep] + [returned_send], axis=0),
     )
     output = (middle + gate * expert_result).astype(BF)
+    device = (at.row * at.experts + lax.axis_index("expert")).astype(jnp.int32)
     if at.near:
-        grad_value, grad_query, grad_proj, grad_key, summed = vmem_call(
-            fold_last_kernel,
-            "fold_last",
-            [((shard, model), F32)] * 4 + [((small_rows, model), F32)],
-            after(keep_sum, output, grad_in),
-            low[0],
-            *[got_z[k] for k in (1, 2, 3)],
-        )
-    device = at.row * at.experts + lax.axis_index("expert")
-    grad_router = lax.dynamic_slice_in_dim(summed[:experts], device * shard, shard, axis=1).T
+        last_ins = [after(keep_sum, output, grad_in), low[0], *[got_z[k] for k in (1, 2, 3)]]
+        last_shapes = [(shard, model)] * 4 + [(1, model)] * 2 + [(head_count, bucket_count), (experts, shard)]
+        grad_value, grad_query, grad_proj, grad_key, gain_1, gain_2, table, router_t = pl.pallas_call(
+            functools.partial(fold_last_kernel, head_count),
+            out_shape=tuple(shape_of(v, F32) for v in last_shapes),
+            in_specs=[smem] + [pl.BlockSpec(v.shape, lambda: (0, 0)) for v in last_ins],
+            out_specs=tuple(pl.BlockSpec(v, lambda: (0, 0)) for v in last_shapes),
+            compiler_params=params(),
+            name="fold_last",
+        )(device.reshape(1), *last_ins)
+    else:
+        gain_1, gain_2 = summed[experts], summed[experts + 1]
+        table = summed[experts + 2, : head_count * bucket_count].reshape(head_count, bucket_count)
+        router_t = lax.dynamic_slice_in_dim(summed[:experts], device * shard, shard, axis=1)
     return (
         output,
         input_grad,
-        summed[experts],
-        summed[experts + 1],
-        summed[experts + 2, : head_count * bucket_count].reshape(head_count, bucket_count).T,
+        gain_1.reshape(model),
+        gain_2.reshape(model),
+        table.T,
         grad_query,
         grad_key,
         grad_value,
         grad_proj,
-        grad_router,
+        router_t.T,
         grad_in,
         grad_out_w,
     )

time: 191 us -> 185 us (0.969); the launches traced: 190 us -> 182 us
  Pallas kernels: 75.2 us -> 69.2 us
  waiting for transfers between devices: 53.3 us -> 50.4 us
    pallas_call x3 -> x1, Pallas kernels: 28.1 us -> 8.72 us  [expert_grads(): pl.pallas_call(functools.partial(expert_grad_kernel, len(sizes), bool(bef...]
    pallas_call x2 -> x5, Pallas kernels: 10.1 us -> 24.5 us  [the longest x1 7.62 us: per_device(): pl.pallas_call(functools.partial(attend_kernel, head), out_shape=tuple((p...]
    ppermute x18, waiting for transfers between devices: 38.3 us -> 35.3 us  [far(): lax.ppermute(v, 'expert', [(i, i ^ 2 * k) for i in range(self.experts)])]
    ppermute x11, starting transfers between devices: 11.7 us -> 14.1 us  [y(): return lax.ppermute(v, 'dp', [(i, i ^ 2) for i in range(self.dp)])]
    unnamed x82 -> x42, local copies, waits for them, and re-layouts: 5.21 us -> 5.22 us
  transfers between devices with their start and end apart: 49 -> 49, of which waited for: 22 -> 20; matrix products, arithmetic and copies ran while one was open for 4% -> 5% of each run, Pallas kernels for 35% -> 33%
where the time goes in v4:
time: 185 us; the launch traced here: 182 us
  Pallas kernels  69.2 us (37%)
  waiting for transfers between devices  50.4 us (27%)
  starting transfers between devices  46.5 us (25%)
  local copies, waits for them, and re-layouts  8.85 us (5%)
  other arithmetic  4.39 us (2%)
    ppermute x18, waiting for transfers between devices, far(): lax.ppermute(v, 'expert', [(i, i ^ 2 * k) for i in range(self.experts)])  35.3 us
    ppermute x18, starting transfers between devices, far(): lax.ppermute(v, 'expert', [(i, i ^ 2 * k) for i in range(self.experts)])  22.3 us
    ppermute x11, starting transfers between devices, y(): return lax.ppermute(v, 'dp', [(i, i ^ 2) for i in range(self.dp)])  14.1 us
    pallas_call x2, Pallas kernels, expert(): pl.pallas_call(functools.partial(expert_kernel, len(sizes)), out_shape=tu...  9.93 us
    ppermute x11, waiting for transfers between devices, y(): return lax.ppermute(v, 'dp', [(i, i ^ 2) for i in range(self.dp)])  9.83 us
    ppermute x10, starting transfers between devices, x(): return lax.ppermute(v, 'dp', [(i, i ^ 1) for i in range(self.dp)])  9.28 us
    pallas_call x1, Pallas kernels, expert_grads(): pl.pallas_call(functools.partial(expert_grad_kernel, len(sizes), bool(bef...  8.72 us
    pallas_call x1, Pallas kernels, per_device(): pl.pallas_call(functools.partial(attend_kernel, head), out_shape=tuple((p...  7.62 us
  transfers between devices with their start and end apart: 49, of which 20 were waited for; matrix products, arithmetic and copies ran while one was open for 5% of the time, Pallas kernels for 33%

profile of v4, /device:TPU:0, one launch (start us, length us, event | category | flops | bytes accessed | tf_op | source)
XLA Modules:
  0.0 181.9 jit_solution(16737144009223012344)
XLA Ops:
  0.6 1.6 pack.1
  2.2 5.0 %collective-permute-start.2 = (bf16[24,3200]{1,0:T(8,128)(2,1)}, bf16[24,3200]{1,0:T(8,128)(2,1)S(1)}, u32[]{:S(2)}, u32[]{:S(2)}) collective-permute-start(bf16[24,3200]{1,0:T(8,128)(2,1)} %pack.1), channel_id=1, source_target_pairs={{0,6},{1,7},{2,4},{3,5},{4,2},{5,3},{6,0},{7,1},{8,14},{9,15},{10,... | collective-permute-start | bytes 460808 | tf_op jit(solution)/shard_map/ppermute | solution.py:588
  12.3 1.6 route.1
  14.0 6.4 %collective-permute-done.1 = bf16[24,3200]{1,0:T(8,128)(2,1)S(1)} collective-permute-done((bf16[24,3200]{1,0:T(8,128)(2,1)}, bf16[24,3200]{1,0:T(8,128)(2,1)S(1)}, u32[]{:S(2)}, u32[]{:S(2)}) %collective-permute-start.1) | collective-permute-done | bytes 153632 | tf_op jit(solution)/shard_map/ppermute | solution.py:588
  22.3 1.6 collective-permute-start.5
  27.1 1.8 bias.1.refs_1_
  29.0 4.0 %collective-permute-done.4 = bf16[128,768]{1,0:T(8,128)(2,1)} collective-permute-done((bf16[128,768]{1,0:T(8,128)(2,1)}, bf16[128,768]{1,0:T(8,128)(2,1)}, u32[]{:S(2)}, u32[]{:S(2)}) %collective-permute-start.4) | collective-permute-done | bytes 196640 | tf_op jit(solution)/shard_map/ppermute | solution.py:588
  33.0 1.6 near.1
  36.7 10.7 %collective-permute-done.9 = bf16[128,768]{1,0:T(8,128)(2,1)S(1)} collective-permute-done((bf16[128,768]{1,0:T(8,128)(2,1)S(1)}, bf16[128,768]{1,0:T(8,128)(2,1)S(1)}, u32[]{:S(2)}, u32[]{:S(2)}) %collective-permute-start.9) | collective-permute-done | bytes 196640 | tf_op jit(solution)/shard_map/ppermute | solution.py:588
  47.4 3.5 %collective-permute-done.7.refs_8_.refs_12_ = bf16[192,1536]{1,0:T(8,128)(2,1)S(1)} collective-permute-done((bf16[192,1536]{1,0:T(8,128)(2,1)}, bf16[192,1536]{1,0:T(8,128)(2,1)S(1)}, u32[]{:S(2)}, u32[]{:S(2)}) %collective-permute-start.7) | collective-permute-done | bytes 589856 | tf_op jit(solution)/shard_map/ppermute | solution.py:585
  52.1 2.5 %collective-permute-start.13 = (bf16[128,768]{1,0:T(8,128)(2,1)S(1)}, bf16[128,768]{1,0:T(8,128)(2,1)S(1)}, u32[]{:S(2)}, u32[]{:S(2)}) collective-permute-start(bf16[128,768]{1,0:T(8,128)(2,1)S(1)} %get-tuple-element.157), channel_id=1, source_target_pairs={{0,6},{1,7},{2,4},{3,5},{4,2},{5,3},{6,0},{7,1},{8,14},{9,15},{10,... | collective-permute-start | bytes 589832 | tf_op jit(solution)/shard_map/ppermute | solution.py:588
  55.9 7.6 %attend.1 = (bf16[256,768]{1,0:T(8,128)(2,1)S(1)}, bf16[256,768]{1,0:T(8,128)(2,1)S(1)}, bf16[256,768]{1,0:T(8,128)(2,1)S(1)}, f32[12,256,256]{2,1,0:T(8,128)S(1...) custom-call(bf16[256,768]{1,0:T(8,128)(2,1)S(1)} %get-tuple-element., ...), custom_call_target="tpu_custom_call" | custom-call | tf_op jit(solution)/shard_map/attend/pallas_call | solution.py:825
  68.3 4.4 %load.1 = (bf16[768,3072]{1,0:T(8,128)(2,1)S(1)}, bf16[3072,768]{1,0:T(8,128)(2,1)S(1)}, f32[8,128]{1,0:T(8,128)}) custom-call(f32[8,128]{1,0:T(8,128)S(1)} %slice_bitcast_fusion.after_ref, bf16[1,768,3072]{2,1,0:T(8,128)(2,1)} %refs_6_.3, bf16[1,3072,768]{2,1,0:T(8,128)(2,1)} %refs_7_.1), custom_call_target="tpu_custom_call" | custom-call | tf_op jit(solution)/shard_map/load/pallas_call | solution.py:787
  72.7 2.6 %hidden_grads.1 = (f32[256,3072]{1,0:T(8,128)S(1)}, f32[256,3072]{1,0:T(8,128)S(1)}) custom-call(bf16[256,768]{1,0:T(8,128)(2,1)S(1)} %pad_maximum_fusion.first_ref.refs_2_.refs_4_, bf16[256,768]{1,0:T(8,128)(2,1)S(1)} %constant_dynamic-update-slice_fusion.second_ref.refs_2_.refs_5_, bf16[3072,768]{1,0:T(8,128)(2,1)S(1)} %get-tuple-element.166.w2_ref.refs_5_.refs_10_.refs_6_), custom_call_target="tpu_custom_call" | custom-call | tf_op jit(solution)/shard_map/hidden_grads/pallas_call | solution.py:857
  75.3 3.1 %collective-permute-done.17.refs_1_ = bf16[128,768]{1,0:T(8,128)(2,1)S(1)} collective-permute-done((bf16[128,768]{1,0:T(8,128)(2,1)S(1)}, bf16[128,768]{1,0:T(8,128)(2,1)S(1)}, u32[]{:S(2)}, u32[]{:S(2)}) %collective-permute-start.17) | collective-permute-done | bytes 196640 | tf_op jit(solution)/shard_map/ppermute | solution.py:588
  80.1 2.5 %collective-permute-start.21 = (bf16[128,768]{1,0:T(8,128)(2,1)S(1)}, bf16[128,768]{1,0:T(8,128)(2,1)S(1)}, u32[]{:S(2)}, u32[]{:S(2)}) collective-permute-start(bf16[128,768]{1,0:T(8,128)(2,1)S(1)} %get-tuple-element.171), channel_id=1, source_target_pairs={{0,6},{1,7},{2,4},{3,5},{4,2},{5,3},{6,0},{7,1},{8,14},{9,15},{10,... | collective-permute-start | bytes 589832 | tf_op jit(solution)/shard_map/ppermute | solution.py:588
  82.6 5.1 %expert.2 = (bf16[128,768]{1,0:T(8,128)(2,1)S(1)}, bf16[128,768]{1,0:T(8,128)(2,1)S(1)}, bf16[128,768]{1,0:T(8,128)(2,1)S(1)}, bf16[128,768]{1,0:T(8,128)(2,1)S(...) custom-call(s32[1]{0:T(128)} %bitcast.11.own_ref.refs_4_, bf16[128,768]{1,0:T(8,128)(2,1)S(1)} %get-tuple-element.160.refs_0_, ...), custom_call_target="tpu_custom_call" | custom-call | tf_op jit(solution)/shard_map/expert/pallas_call | solution.py:870
  91.4 4.9 %expert.3 = (bf16[128,768]{1,0:T(8,128)(2,1)S(1)}, bf16[128,768]{1,0:T(8,128)(2,1)S(1)}, bf16[128,768]{1,0:T(8,128)(2,1)S(1)}, bf16[128,768]{1,0:T(8,128)(2,1)S(...) custom-call(s32[1]{0:T(128)} %bitcast.11.own_ref.refs_4_, bf16[128,768]{1,0:T(8,128)(2,1)S(1)} %collective-permute-done.20.refs_0_, ...), custom_call_target="tpu_custom_call" | custom-call | tf_op jit(solution)/shard_map/expert/pallas_call | solution.py:870
  96.3 4.8 %collective-permute-done.24.refs_2_ = bf16[128,768]{1,0:T(8,128)(2,1)S(1)} collective-permute-done((bf16[128,768]{1,0:T(8,128)(2,1)S(1)}, bf16[128,768]{1,0:T(8,128)(2,1)S(1)}, u32[]{:S(2)}, u32[]{:S(2)}) %collective-permute-start.24) | collective-permute-done | bytes 196640 | tf_op jit(solution)/shard_map/ppermute | solution.py:588
  101.0 1.6 collective-permute-start.26
  103.7 3.5 %collective-permute-start.30 = (bf16[256,768]{1,0:T(8,128)(2,1)S(1)}, bf16[256,768]{1,0:T(8,128)(2,1)S(1)}, u32[]{:S(2)}, u32[]{:S(2)}) collective-permute-start(bf16[256,768]{1,0:T(8,128)(2,1)S(1)} %get-tuple-element.188.refs_1_), channel_id=1, source_target_pairs={{0,16},{8,24},{16,0},{24,8},{1,17},{9,25},{17,1},{25,9},{2,18},{10... | collective-permute-start | bytes 1179656 | tf_op jit(solution)/shard_map/ppermute | solution.py:585
  107.3 4.8 %collective-permute-done.25.refs_1_ = bf16[128,768]{1,0:T(8,128)(2,1)S(1)} collective-permute-done((bf16[128,768]{1,0:T(8,128)(2,1)S(1)}, bf16[128,768]{1,0:T(8,128)(2,1)S(1)}, u32[]{:S(2)}, u32[]{:S(2)}) %collective-permute-start.25) | collective-permute-done | bytes 196640 | tf_op jit(solution)/shard_map/ppermute | solution.py:588
  114.3 2.8 %middle.1 = (f32[256,768]{1,0:T(8,128)S(1)}, f32[1,768]{1,0:T(1,128)S(1)}, bf16[256,768]{1,0:T(8,128)(2,1)S(1)}, bf16[640,768]{1,0:T(8,128)(2,1)S(1)}) custom-call(bf16[128,768]{1,0:T(8,128)(2,1)S(1)} %get-tuple-element.180.refs_0_, bf16[128,768]{1,0:T(8,128)(2,1)S(1)} %collective-permute-done.25.refs_1_, ...), custom_call_target="tpu_custom_call" | custom-call | flops 1024 | bytes 1024 | tf_op jit(solution)/shard_map/middle/pallas_call | solution.py:960
  119.1 5.8 %score_grads.1 = (bf16[512,768]{1,0:T(8,128)(2,1)S(1)}, f32[12,1,512]{2,1,0:T(1,128)S(1)}) custom-call(bf16[256,768]{1,0:T(8,128)(2,1)S(1)} %get-tuple-element.193.mixed_grad_ref, bf16[256,768]{1,0:T(8,128)(2,1)S(1)} %get-tuple-element.194.v_ref, bf16[256,768]{1,0:T(8,128)(2,1)S(1)} %get-tuple-element.195.q_ref, ...), custom_call_target="tpu_custom_call" | custom-call | flops 1024 | bytes 1024 | tf_op jit(solution)/shard_map/score_grads/pallas_call | solution.py:993
  124.9 3.8 %collective-permute-done.33.refs_0_ = bf16[256,768]{1,0:T(8,128)(2,1)S(1)} collective-permute-done((bf16[256,768]{1,0:T(8,128)(2,1)S(1)}, bf16[256,768]{1,0:T(8,128)(2,1)S(1)}, u32[]{:S(2)}, u32[]{:S(2)}) %collective-permute-start.33) | collective-permute-done | bytes 393248 | tf_op jit(solution)/shard_map/ppermute | solution.py:585
  135.1 1.8 collective-permute-start.37
  136.9 3.9 %inputs.1 = (f32[256,768]{1,0:T(8,128)}, f32[16,768]{1,0:T(8,128)S(1)}) custom-call(bf16[512,768]{1,0:T(8,128)(2,1)S(1)} %get-tuple-element.200.qk_ref.refs_0_, bf16[640,768]{1,0:T(8,128)(2,1)S(1)} %get-tuple-element.192.vo_ref.refs_1_, bf16[256,768]{1,0:T(8,128)(2,1)S(1)} %copy-done.1, f32[1,768]{1,0:T(1,128)S(1)} %get-tuple-element.210.refs_3_, ...), custom_call_target="tpu_custom_call" | custom-call | flops 1024 | bytes 1024 | tf_op jit(solution)/shard_map/inputs/pallas_call | solution.py:1005
  143.0 6.9 %expert_grads.3 = (f32[768,768]{1,0:T(8,128)S(1)}, f32[768,768]{1,0:T(8,128)S(1)}) custom-call(s32[1]{0:T(128)} %bitcast.11.own_ref.refs_4_, s32[1]{0:T(128)} %bitcast.19.place_ref, bf16[256,768]{1,0:T(8,128)(2,1)S(1)} %get-tuple-element.187.refs_0_, bf16[256,768]{1,0:T(8,128)(2,1)S(1)} %get-tuple-element.188.refs_1_, ...), custom_call_target="tpu_custom_call" | custom-call | tf_op jit(solution)/shard_map/expert_grads/pallas_call | solution.py:931
  155.2 7.3 %expert_grads.4 = (f32[1,768,768]{2,1,0:T(8,128)}, f32[1,768,768]{2,1,0:T(8,128)}) custom-call(s32[1]{0:T(128)} %bitcast.11.own_ref.refs_4_, s32[1]{0:T(128)} %bitcast.19.place_ref, bf16[256,768]{1,0:T(8,128)(2,1)} %copy-done.12, bf16[256,768]{1,0:T(8,128)(2,1)} %copy-done.15, bf16[256,768]{1,0:T(8,128)(2,1)} %copy-done.8, bf16[256,768]{1,0:T(8,128)(2,1)} %copy-done.11, ...), custom_call_target="tpu_custom_call" | custom-call | tf_op jit(solution)/shard_map/expert_grads/pallas_call | solution.py:944
  163.6 2.0 %collective-permute-start.47 = (bf16[112,768]{1,0:T(8,128)(2,1)S(1)}, bf16[112,768]{1,0:T(8,128)(2,1)S(1)}, u32[]{:S(2)}, u32[]{:S(2)}) collective-permute-start(bf16[112,768]{1,0:T(8,128)(2,1)S(1)} %get-tuple-element.235), channel_id=1, source_target_pairs={{0,4},{1,5},{2,6},{3,7},{4,0},{5,1},{6,2},{7,3},{8,12},{9,13},{10,... | collective-permute-start | bytes 516104 | tf_op jit(solution)/shard_map/ppermute | solution.py:588
  165.6 1.8 collective-permute-start.48
  167.4 8.7 %expert_grads.5 = (f32[1,768,768]{2,1,0:T(8,128)}, f32[1,768,768]{2,1,0:T(8,128)}) custom-call(s32[1]{0:T(128)} %bitcast.19.place_ref, bf16[256,768]{1,0:T(8,128)(2,1)} %copy-done.13, bf16[256,768]{1,0:T(8,128)(2,1)} %copy-done.14, bf16[256,768]{1,0:T(8,128)(2,1)} %copy-done.9, bf16[256,768]{1,0:T(8,128)(2,1)} %copy-done.10, s32[1]{0:T(128)} %bitcast.11.own_ref.refs_4_, ...), custom_call_target="tpu_custom_call" | custom-call | flops 1024 | bytes 1024 | tf_op jit(solution)/shard_map/expert_grads/pallas_call | solution.py:904
  (162 shorter events, 50.6 us)
Async XLA Ops:
  2.2 11.8 %collective-permute-start.2 = (bf16[24,3200]{1,0:T(8,128)(2,1)}, bf16[24,3200]{1,0:T(8,128)(2,1)S(1)}, u32[]{:S(2)}, u32[]{:S(2)}) collective-permute-start(bf16[24,3200]{1,0:T(8,128)(2,1)} %pack.1), channel_id=1, source_target_pairs={{0,6},{1,7},{2,4},{3,5},{4,2},{5,3},{6,0},{7,1},{8,14},{9,15},{10,... | collective-permute-start | bytes 460808 | tf_op jit(solution)/shard_map/ppermute | solution.py:588
  7.3 13.2 %collective-permute-start.1 = (bf16[24,3200]{1,0:T(8,128)(2,1)}, bf16[24,3200]{1,0:T(8,128)(2,1)S(1)}, u32[]{:S(2)}, u32[]{:S(2)}) collective-permute-start(bf16[24,3200]{1,0:T(8,128)(2,1)} %pack.1), channel_id=1, source_target_pairs={{0,4},{1,5},{2,6},{3,7},{4,0},{5,1},{6,2},{7,3},{8,12},{9,13},{10,... | collective-permute-start | bytes 460808 | tf_op jit(solution)/shard_map/ppermute | solution.py:588
  7.3 13.2 %collective-permute-start = (bf16[24,3200]{1,0:T(8,128)(2,1)}, bf16[24,3200]{1,0:T(8,128)(2,1)S(1)}, u32[]{:S(2)}, u32[]{:S(2)}) collective-permute-start(bf16[24,3200]{1,0:T(8,128)(2,1)} %pack.1), channel_id=1, source_target_pairs={{0,2},{1,3},{2,0},{3,1},{4,6},{5,7},{6,4},{7,5},{8,10},{9,11},{10,... | collective-permute-start | bytes 460808 | tf_op jit(solution)/shard_map/ppermute | solution.py:588
  13.9 11.5 %collective-permute-start.3 = (bf16[384,768]{1,0:T(8,128)(2,1)S(1)}, bf16[384,768]{1,0:T(8,128)(2,1)S(1)}, u32[]{:S(2)}, u32[]{:S(2)}) collective-permute-start(bf16[384,768]{1,0:T(8,128)(2,1)S(1)} %get-tuple-element.138), channel_id=1, source_target_pairs={{0,1},{1,0},{2,3},{3,2},{4,5},{5,4},{6,7},{7,6},{8,9},{9,8},{10,11... | collective-permute-start | bytes 1769480 | tf_op jit(solution)/shard_map/ppermute | solution.py:579
  34.6 17.0 %collective-permute-start.10 = (bf16[192,3200]{1,0:T(8,128)(2,1)}, bf16[192,3200]{1,0:T(8,128)(2,1)S(1)}, u32[]{:S(2)}, u32[]{:S(2)}) collective-permute-start(bf16[192,3200]{1,0:T(8,128)(2,1)} %get-tuple-element.148), channel_id=1, source_target_pairs={{0,1},{1,0},{2,3},{3,2},{4,5},{5,4},{6,7},{7,6},{8,9},{9,8},{10,11... | collective-permute-start | bytes 3686408 | tf_op jit(solution)/shard_map/ppermute | solution.py:579
  34.6 17.0 %collective-permute-start.8 = (bf16[192,1664]{1,0:T(8,128)(2,1)}, bf16[192,1664]{1,0:T(8,128)(2,1)S(1)}, u32[]{:S(2)}, u32[]{:S(2)}) collective-permute-start(bf16[192,1664]{1,0:T(8,128)(2,1)} %get-tuple-element.146), channel_id=1, source_target_pairs={{0,8},{8,0},{16,24},{24,16},{1,9},{9,1},{17,25},{25,17},{2,10},{10... | collective-permute-start | bytes 1916936 | tf_op jit(solution)/shard_map/ppermute | solution.py:582
  35.2 15.7 %collective-permute-start.7 = (bf16[192,1536]{1,0:T(8,128)(2,1)}, bf16[192,1536]{1,0:T(8,128)(2,1)S(1)}, u32[]{:S(2)}, u32[]{:S(2)}) collective-permute-start(bf16[192,1536]{1,0:T(8,128)(2,1)} %get-tuple-element.145), channel_id=1, source_target_pairs={{0,16},{8,24},{16,0},{24,8},{1,17},{9,25},{17,1},{25,9},{2,18},{10... | collective-permute-start | bytes 1769480 | tf_op jit(solution)/shard_map/ppermute | solution.py:585
  35.8 11.5 %collective-permute-start.9 = (bf16[128,768]{1,0:T(8,128)(2,1)S(1)}, bf16[128,768]{1,0:T(8,128)(2,1)S(1)}, u32[]{:S(2)}, u32[]{:S(2)}) collective-permute-start(bf16[128,768]{1,0:T(8,128)(2,1)S(1)} %copy-done.16), channel_id=1, source_target_pairs={{0,4},{1,5},{2,6},{3,7},{4,0},{5,1},{6,2},{7,3},{8,12},{9,13},{10,... | collective-permute-start | bytes 589832 | tf_op jit(solution)/shard_map/ppermute | solution.py:588
  52.1 11.4 %collective-permute-start.13 = (bf16[128,768]{1,0:T(8,128)(2,1)S(1)}, bf16[128,768]{1,0:T(8,128)(2,1)S(1)}, u32[]{:S(2)}, u32[]{:S(2)}) collective-permute-start(bf16[128,768]{1,0:T(8,128)(2,1)S(1)} %get-tuple-element.157), channel_id=1, source_target_pairs={{0,6},{1,7},{2,4},{3,5},{4,2},{5,3},{6,0},{7,1},{8,14},{9,15},{10,... | collective-permute-start | bytes 589832 | tf_op jit(solution)/shard_map/ppermute | solution.py:588
  54.6 10.8 %collective-permute-start.16 = (bf16[256,768]{1,0:T(8,128)(2,1)S(1)}, bf16[256,768]{1,0:T(8,128)(2,1)S(1)}, u32[]{:S(2)}, u32[]{:S(2)}) collective-permute-start(bf16[256,768]{1,0:T(8,128)(2,1)S(1)} %pad_maximum_fusion.first_ref.refs_2_.refs_4_), channel_id=1, source_target_pairs={{0,16},{8,24},{16,0},{24,8},{1,17},{9,25},{17,1},{25,9},{2,18},{10... | collective-permute-start | bytes 1179656 | tf_op jit(solution)/shard_map/ppermute | solution.py:585
  65.7 12.8 %collective-permute-start.19 = (bf16[256,768]{1,0:T(8,128)(2,1)S(1)}, bf16[256,768]{1,0:T(8,128)(2,1)S(1)}, u32[]{:S(2)}, u32[]{:S(2)}) collective-permute-start(bf16[256,768]{1,0:T(8,128)(2,1)S(1)} %constant_dynamic-update-slice_fusion.second_ref.refs_2_.refs_5_), channel_id=1, source_target_pairs={{0,8},{8,0},{16,24},{24,16},{1,9},{9,1},{17,25},{25,17},{2,10},{10... | collective-permute-start | bytes 1179656 | tf_op jit(solution)/shard_map/ppermute | solution.py:582
  66.6 11.9 %collective-permute-start.18 = (bf16[256,768]{1,0:T(8,128)(2,1)S(1)}, bf16[256,768]{1,0:T(8,128)(2,1)S(1)}, u32[]{:S(2)}, u32[]{:S(2)}) collective-permute-start(bf16[256,768]{1,0:T(8,128)(2,1)S(1)} %constant_dynamic-update-slice_fusion.second_ref.refs_2_.refs_5_), channel_id=1, source_target_pairs={{0,16},{8,24},{16,0},{24,8},{1,17},{9,25},{17,1},{25,9},{2,18},{10... | collective-permute-start | bytes 1179656 | tf_op jit(solution)/shard_map/ppermute | solution.py:585
  78.5 11.1 %collective-permute-start.22 = (bf16[256,768]{1,0:T(8,128)(2,1)S(1)}, bf16[256,768]{1,0:T(8,128)(2,1)S(1)}, u32[]{:S(2)}, u32[]{:S(2)}) collective-permute-start(bf16[256,768]{1,0:T(8,128)(2,1)S(1)} %collective-permute-done.15.refs_6_), channel_id=1, source_target_pairs={{0,16},{8,24},{16,0},{24,8},{1,17},{9,25},{17,1},{25,9},{2,18},{10... | collective-permute-start | bytes 1179656 | tf_op jit(solution)/shard_map/ppermute | solution.py:585
  79.2 11.1 %collective-permute-start.23 = (bf16[256,768]{1,0:T(8,128)(2,1)S(1)}, bf16[256,768]{1,0:T(8,128)(2,1)S(1)}, u32[]{:S(2)}, u32[]{:S(2)}) collective-permute-start(bf16[256,768]{1,0:T(8,128)(2,1)S(1)} %collective-permute-done.18.refs_7_), channel_id=1, source_target_pairs={{0,8},{8,0},{16,24},{24,16},{1,9},{9,1},{17,25},{25,17},{2,10},{10... | collective-permute-start | bytes 1179656 | tf_op jit(solution)/shard_map/ppermute | solution.py:582
  80.1 11.1 %collective-permute-start.20 = (bf16[128,768]{1,0:T(8,128)(2,1)S(1)}, bf16[128,768]{1,0:T(8,128)(2,1)S(1)}, u32[]{:S(2)}, u32[]{:S(2)}) collective-permute-start(bf16[128,768]{1,0:T(8,128)(2,1)S(1)} %get-tuple-element.169), channel_id=1, source_target_pairs={{0,2},{1,3},{2,0},{3,1},{4,6},{5,7},{6,4},{7,5},{8,10},{9,11},{10,... | collective-permute-start | bytes 589832 | tf_op jit(solution)/shard_map/ppermute | solution.py:588
  80.1 11.3 %collective-permute-start.21 = (bf16[128,768]{1,0:T(8,128)(2,1)S(1)}, bf16[128,768]{1,0:T(8,128)(2,1)S(1)}, u32[]{:S(2)}, u32[]{:S(2)}) collective-permute-start(bf16[128,768]{1,0:T(8,128)(2,1)S(1)} %get-tuple-element.171), channel_id=1, source_target_pairs={{0,6},{1,7},{2,4},{3,5},{4,2},{5,3},{6,0},{7,1},{8,14},{9,15},{10,... | collective-permute-start | bytes 589832 | tf_op jit(solution)/shard_map/ppermute | solution.py:588
  87.6 15.0 %collective-permute-start.29 = (bf16[256,768]{1,0:T(8,128)(2,1)S(1)}, bf16[256,768]{1,0:T(8,128)(2,1)S(1)}, u32[]{:S(2)}, u32[]{:S(2)}) collective-permute-start(bf16[256,768]{1,0:T(8,128)(2,1)S(1)} %get-tuple-element.187.refs_0_), channel_id=1, source_target_pairs={{0,16},{8,24},{16,0},{24,8},{1,17},{9,25},{17,1},{25,9},{2,18},{10... | collective-permute-start | bytes 1179656 | tf_op jit(solution)/shard_map/ppermute | solution.py:585
  89.6 13.1 %collective-permute-start.28 = (bf16[256,768]{1,0:T(8,128)(2,1)S(1)}, bf16[256,768]{1,0:T(8,128)(2,1)S(1)}, u32[]{:S(2)}, u32[]{:S(2)}) collective-permute-start(bf16[256,768]{1,0:T(8,128)(2,1)S(1)} %get-tuple-element.187.refs_0_), channel_id=1, source_target_pairs={{0,8},{8,0},{16,24},{24,16},{1,9},{9,1},{17,25},{25,17},{2,10},{10... | collective-permute-start | bytes 1179656 | tf_op jit(solution)/shard_map/ppermute | solution.py:582
  101.0 11.0 %collective-permute-start.25 = (bf16[128,768]{1,0:T(8,128)(2,1)S(1)}, bf16[128,768]{1,0:T(8,128)(2,1)S(1)}, u32[]{:S(2)}, u32[]{:S(2)}) collective-permute-start(bf16[128,768]{1,0:T(8,128)(2,1)S(1)} %get-tuple-element.184), channel_id=1, source_target_pairs={{0,2},{1,3},{2,0},{3,1},{4,6},{5,7},{6,4},{7,5},{8,10},{9,11},{10,... | collective-permute-start | bytes 589832 | tf_op jit(solution)/shard_map/ppermute | solution.py:588
  101.0 11.0 %collective-permute-start.26 = (bf16[128,768]{1,0:T(8,128)(2,1)S(1)}, bf16[128,768]{1,0:T(8,128)(2,1)S(1)}, u32[]{:S(2)}, u32[]{:S(2)}) collective-permute-start(bf16[128,768]{1,0:T(8,128)(2,1)S(1)} %get-tuple-element.185), channel_id=1, source_target_pairs={{0,6},{1,7},{2,4},{3,5},{4,2},{5,3},{6,0},{7,1},{8,14},{9,15},{10,... | collective-permute-start | bytes 589832 | tf_op jit(solution)/shard_map/ppermute | solution.py:588
  117.0 12.2 %collective-permute-start.32 = (bf16[640,768]{1,0:T(8,128)(2,1)S(1)}, bf16[640,768]{1,0:T(8,128)(2,1)S(1)}, u32[]{:S(2)}, u32[]{:S(2)}) collective-permute-start(bf16[640,768]{1,0:T(8,128)(2,1)S(1)} %get-tuple-element.192.vo_ref.refs_1_), channel_id=1, source_target_pairs={{0,1},{1,0},{2,3},{3,2},{4,5},{5,4},{6,7},{7,6},{8,9},{9,8},{10,11... | collective-permute-start | bytes 2949128 | tf_op jit(solution)/shard_map/ppermute | solution.py:579
  117.1 11.5 %collective-permute-start.33 = (bf16[256,768]{1,0:T(8,128)(2,1)S(1)}, bf16[256,768]{1,0:T(8,128)(2,1)S(1)}, u32[]{:S(2)}, u32[]{:S(2)}) collective-permute-start(bf16[256,768]{1,0:T(8,128)(2,1)S(1)} %collective-permute-done.28.refs_2_), channel_id=1, source_target_pairs={{0,16},{8,24},{16,0},{24,8},{1,17},{9,25},{17,1},{25,9},{2,18},{10... | collective-permute-start | bytes 1179656 | tf_op jit(solution)/shard_map/ppermute | solution.py:585
  118.1 11.2 %collective-permute-start.34 = (bf16[256,768]{1,0:T(8,128)(2,1)S(1)}, bf16[256,768]{1,0:T(8,128)(2,1)S(1)}, u32[]{:S(2)}, u32[]{:S(2)}) collective-permute-start(bf16[256,768]{1,0:T(8,128)(2,1)S(1)} %collective-permute-done.30.refs_3_), channel_id=1, source_target_pairs={{0,8},{8,0},{16,24},{24,16},{1,9},{9,1},{17,25},{25,17},{2,10},{10... | collective-permute-start | bytes 1179656 | tf_op jit(solution)/shard_map/ppermute | solution.py:582
  133.1 16.8 %collective-permute-start.36 = (bf16[192,1536]{1,0:T(8,128)(2,1)S(1)}, bf16[192,1536]{1,0:T(8,128)(2,1)S(1)}, u32[]{:S(2)}, u32[]{:S(2)}) collective-permute-start(bf16[192,1536]{1,0:T(8,128)(2,1)S(1)} %get-tuple-element.202), channel_id=1, source_target_pairs={{0,16},{8,24},{16,0},{24,8},{1,17},{9,25},{17,1},{25,9},{2,18},{10... | collective-permute-start | bytes 1769480 | tf_op jit(solution)/shard_map/ppermute | solution.py:585
  134.3 15.7 %collective-permute-start.38 = (bf16[192,1536]{1,0:T(8,128)(2,1)S(1)}, bf16[192,1536]{1,0:T(8,128)(2,1)S(1)}, u32[]{:S(2)}, u32[]{:S(2)}) collective-permute-start(bf16[192,1536]{1,0:T(8,128)(2,1)S(1)} %get-tuple-element.203), channel_id=1, source_target_pairs={{0,8},{8,0},{16,24},{24,16},{1,9},{9,1},{17,25},{25,17},{2,10},{10... | collective-permute-start | bytes 1769480 | tf_op jit(solution)/shard_map/ppermute | solution.py:582
  135.1 14.8 %collective-permute-start.37 = (bf16[128,768]{1,0:T(8,128)(2,1)S(1)}, bf16[128,768]{1,0:T(8,128)(2,1)S(1)}, u32[]{:S(2)}, u32[]{:S(2)}) collective-permute-start(bf16[128,768]{1,0:T(8,128)(2,1)S(1)} %get-tuple-element.207), channel_id=1, source_target_pairs={{0,4},{1,5},{2,6},{3,7},{4,0},{5,1},{6,2},{7,3},{8,12},{9,13},{10,... | collective-permute-start | bytes 589832 | tf_op jit(solution)/shard_map/ppermute | solution.py:588
  150.2 12.4 %collective-permute-start.41 = (bf16[128,768]{1,0:T(8,128)(2,1)S(1)}, bf16[128,768]{1,0:T(8,128)(2,1)S(1)}, u32[]{:S(2)}, u32[]{:S(2)}) collective-permute-start(bf16[128,768]{1,0:T(8,128)(2,1)S(1)} %get-tuple-element.219), channel_id=1, source_target_pairs={{0,2},{1,3},{2,0},{3,1},{4,6},{5,7},{6,4},{7,5},{8,10},{9,11},{10,... | collective-permute-start | bytes 589832 | tf_op jit(solution)/shard_map/ppermute | solution.py:588
  151.4 11.3 %collective-permute-start.44 = (bf16[96,1536]{1,0:T(8,128)(2,1)S(1)}, bf16[96,1536]{1,0:T(8,128)(2,1)S(1)}, u32[]{:S(2)}, u32[]{:S(2)}) collective-permute-start(bf16[96,1536]{1,0:T(8,128)(2,1)S(1)} %get-tuple-element.218), channel_id=1, source_target_pairs={{0,16},{8,24},{16,0},{24,8},{1,17},{9,25},{17,1},{25,9},{2,18},{10... | collective-permute-start | bytes 884744 | tf_op jit(solution)/shard_map/ppermute | solution.py:585
  162.8 13.3 %collective-permute-start.45 = (bf16[256,768]{1,0:T(8,128)(2,1)S(1)}, bf16[256,768]{1,0:T(8,128)(2,1)}, u32[]{:S(2)}, u32[]{:S(2)}) collective-permute-start(bf16[256,768]{1,0:T(8,128)(2,1)S(1)} %pad_maximum_fusion.2), channel_id=1, source_target_pairs={{0,1},{1,0},{2,3},{3,2},{4,5},{5,4},{6,7},{7,6},{8,9},{9,8},{10,11... | collective-permute-start | bytes 1179656 | tf_op jit(solution)/shard_map/ppermute | solution.py:579
  163.6 15.6 %collective-permute-start.47 = (bf16[112,768]{1,0:T(8,128)(2,1)S(1)}, bf16[112,768]{1,0:T(8,128)(2,1)S(1)}, u32[]{:S(2)}, u32[]{:S(2)}) collective-permute-start(bf16[112,768]{1,0:T(8,128)(2,1)S(1)} %get-tuple-element.235), channel_id=1, source_target_pairs={{0,4},{1,5},{2,6},{3,7},{4,0},{5,1},{6,2},{7,3},{8,12},{9,13},{10,... | collective-permute-start | bytes 516104 | tf_op jit(solution)/shard_map/ppermute | solution.py:588
  165.6 13.6 %collective-permute-start.48 = (bf16[112,768]{1,0:T(8,128)(2,1)S(1)}, bf16[112,768]{1,0:T(8,128)(2,1)S(1)}, u32[]{:S(2)}, u32[]{:S(2)}) collective-permute-start(bf16[112,768]{1,0:T(8,128)(2,1)S(1)} %get-tuple-element.236), channel_id=1, source_target_pairs={{0,6},{1,7},{2,4},{3,5},{4,2},{5,3},{6,0},{7,1},{8,14},{9,15},{10,... | collective-permute-start | bytes 516104 | tf_op jit(solution)/shard_map/ppermute | solution.py:588
  167.4 12.1 %collective-permute-start.46 = (bf16[112,768]{1,0:T(8,128)(2,1)S(1)}, bf16[112,768]{1,0:T(8,128)(2,1)S(1)}, u32[]{:S(2)}, u32[]{:S(2)}) collective-permute-start(bf16[112,768]{1,0:T(8,128)(2,1)S(1)} %get-tuple-element.234.own_ref), channel_id=1, source_target_pairs={{0,2},{1,3},{2,0},{3,1},{4,6},{5,7},{6,4},{7,5},{8,10},{9,11},{10,... | collective-permute-start | bytes 516104 | tf_op jit(solution)/shard_map/ppermute | solution.py:588
  (37 other events, 262.7 us)

commit v5 on v4

--- a/solution.py
+++ b/solution.py
@@ -488,8 +488,8 @@
     for number in range(4):
         outs[number][...] = total[number * shard : (number + 1) * shard]
     small = (own_ref[...][:first].astype(F32) + got[0][:first]) + (got[1][:first] + got[2][:first])
-    outs[4][...] = small[experts : experts + 1]
-    outs[5][...] = small[experts + 1 : experts + 2]
+    outs[4][...] = small[experts]
+    outs[5][...] = small[experts + 1]
     every = outs[6].shape[1]
     line = small[experts + 2 : experts + 3]
     outs[6][...] = jnp.concatenate([line[:, h * every : (h + 1) * every] for h in range(heads)], axis=0)
@@ -1123,12 +1123,12 @@
     device = (at.row * at.experts + lax.axis_index("expert")).astype(jnp.int32)
     if at.near:
         last_ins = [after(keep_sum, output, grad_in), low[0], *[got_z[k] for k in (1, 2, 3)]]
-        last_shapes = [(shard, model)] * 4 + [(1, model)] * 2 + [(head_count, bucket_count), (experts, shard)]
+        last_shapes = [(shard, model)] * 4 + [(model,)] * 2 + [(head_count, bucket_count), (experts, shard)]
         grad_value, grad_query, grad_proj, grad_key, gain_1, gain_2, table, router_t = pl.pallas_call(
             functools.partial(fold_last_kernel, head_count),
             out_shape=tuple(shape_of(v, F32) for v in last_shapes),
             in_specs=[smem] + [pl.BlockSpec(v.shape, lambda: (0, 0)) for v in last_ins],
-            out_specs=tuple(pl.BlockSpec(v, lambda: (0, 0)) for v in last_shapes),
+            out_specs=tuple(pl.BlockSpec(v, (lambda: (0, 0)) if len(v) > 1 else (lambda: (0,))) for v in last_shapes),
             compiler_params=params(),
             name="fold_last",
         )(device.reshape(1), *last_ins)

time: 185 us -> 184 us (level)
  transfers between devices with their start and end apart: 49 -> 49, of which waited for: 20 -> 20; matrix products, arithmetic and copies ran while one was open for 5% -> 5% of each run, Pallas kernels for 33% -> 34%
where the time goes in v5:
time: 184 us; the launch traced here: 181 us
  Pallas kernels  69.2 us (38%)
  waiting for transfers between devices  50.4 us (27%)
  starting transfers between devices  46.5 us (25%)
  local copies, waits for them, and re-layouts  8.91 us (5%)
  other arithmetic  3.17 us (2%)
    ppermute x18, waiting for transfers between devices, far(): lax.ppermute(v, 'expert', [(i, i ^ 2 * k) for i in range(self.experts)])  35.3 us
    ppermute x18, starting transfers between devices, far(): lax.ppermute(v, 'expert', [(i, i ^ 2 * k) for i in range(self.experts)])  22.4 us
    ppermute x11, starting transfers between devices, y(): return lax.ppermute(v, 'dp', [(i, i ^ 2) for i in range(self.dp)])  14 us
    ppermute x11, waiting for transfers between devices, y(): return lax.ppermute(v, 'dp', [(i, i ^ 2) for i in range(self.dp)])  9.99 us
    pallas_call x2, Pallas kernels, expert(): pl.pallas_call(functools.partial(expert_kernel, len(sizes)), out_shape=tu...  9.94 us
    ppermute x10, starting transfers between devices, x(): return lax.ppermute(v, 'dp', [(i, i ^ 1) for i in range(self.dp)])  9.24 us
    pallas_call x1, Pallas kernels, expert_grads(): pl.pallas_call(functools.partial(expert_grad_kernel, len(sizes), bool(bef...  8.71 us
    pallas_call x1, Pallas kernels, per_device(): pl.pallas_call(functools.partial(attend_kernel, head), out_shape=tuple((p...  7.63 us
  transfers between devices with their start and end apart: 49, of which 20 were waited for; matrix products, arithmetic and copies ran while one was open for 5% of the time, Pallas kernels for 34%

profile of v5, /device:TPU:0, one launch (start us, length us, event | category | flops | bytes accessed | tf_op | source)
XLA Modules:
  0.0 180.7 jit_solution(4885106275561205582)
XLA Ops:
  0.6 1.6 pack.1
  2.2 5.0 %collective-permute-start.2 = (bf16[24,3200]{1,0:T(8,128)(2,1)}, bf16[24,3200]{1,0:T(8,128)(2,1)S(1)}, u32[]{:S(2)}, u32[]{:S(2)}) collective-permute-start(bf16[24,3200]{1,0:T(8,128)(2,1)} %pack.1), channel_id=1, source_target_pairs={{0,6},{1,7},{2,4},{3,5},{4,2},{5,3},{6,0},{7,1},{8,14},{9,15},{10,... | collective-permute-start | bytes 460808 | tf_op jit(solution)/shard_map/ppermute | solution.py:588
  12.3 1.6 route.1
  14.0 6.4 %collective-permute-done.1 = bf16[24,3200]{1,0:T(8,128)(2,1)S(1)} collective-permute-done((bf16[24,3200]{1,0:T(8,128)(2,1)}, bf16[24,3200]{1,0:T(8,128)(2,1)S(1)}, u32[]{:S(2)}, u32[]{:S(2)}) %collective-permute-start.1) | collective-permute-done | bytes 153632 | tf_op jit(solution)/shard_map/ppermute | solution.py:588
  22.3 1.6 collective-permute-start.5
  27.2 1.8 %bias.1.refs_1_ = f32[12,256,256]{2,1,0:T(8,128)S(1)} custom-call(s32[1,512]{1,0:T(1,128)S(1)} %bitcast.36, f32[32,12]{1,0:T(8,128)S(1)} %copy.27.table_ref), custom_call_target="tpu_custom_call" | custom-call | flops 1024 | bytes 1024 | tf_op jit(solution)/shard_map/bias/pallas_call | solution.py:765
  29.0 4.0 %collective-permute-done.4 = bf16[128,768]{1,0:T(8,128)(2,1)} collective-permute-done((bf16[128,768]{1,0:T(8,128)(2,1)}, bf16[128,768]{1,0:T(8,128)(2,1)}, u32[]{:S(2)}, u32[]{:S(2)}) %collective-permute-start.4) | collective-permute-done | bytes 196640 | tf_op jit(solution)/shard_map/ppermute | solution.py:588
  33.0 1.6 near.1
  36.7 10.7 %collective-permute-done.9 = bf16[128,768]{1,0:T(8,128)(2,1)S(1)} collective-permute-done((bf16[128,768]{1,0:T(8,128)(2,1)S(1)}, bf16[128,768]{1,0:T(8,128)(2,1)S(1)}, u32[]{:S(2)}, u32[]{:S(2)}) %collective-permute-start.9) | collective-permute-done | bytes 196640 | tf_op jit(solution)/shard_map/ppermute | solution.py:588
  47.4 3.5 %collective-permute-done.7.refs_8_.refs_12_ = bf16[192,1536]{1,0:T(8,128)(2,1)S(1)} collective-permute-done((bf16[192,1536]{1,0:T(8,128)(2,1)}, bf16[192,1536]{1,0:T(8,128)(2,1)S(1)}, u32[]{:S(2)}, u32[]{:S(2)}) %collective-permute-start.7) | collective-permute-done | bytes 589856 | tf_op jit(solution)/shard_map/ppermute | solution.py:585
  52.2 2.5 %collective-permute-start.13 = (bf16[128,768]{1,0:T(8,128)(2,1)S(1)}, bf16[128,768]{1,0:T(8,128)(2,1)S(1)}, u32[]{:S(2)}, u32[]{:S(2)}) collective-permute-start(bf16[128,768]{1,0:T(8,128)(2,1)S(1)} %get-tuple-element.157), channel_id=1, source_target_pairs={{0,6},{1,7},{2,4},{3,5},{4,2},{5,3},{6,0},{7,1},{8,14},{9,15},{10,... | collective-permute-start | bytes 589832 | tf_op jit(solution)/shard_map/ppermute | solution.py:588
  55.9 7.6 %attend.1 = (bf16[256,768]{1,0:T(8,128)(2,1)S(1)}, bf16[256,768]{1,0:T(8,128)(2,1)S(1)}, bf16[256,768]{1,0:T(8,128)(2,1)S(1)}, f32[12,256,256]{2,1,0:T(8,128)S(1...) custom-call(bf16[256,768]{1,0:T(8,128)(2,1)S(1)} %get-tuple-element., ...), custom_call_target="tpu_custom_call" | custom-call | tf_op jit(solution)/shard_map/attend/pallas_call | solution.py:825
  68.3 4.4 %load.1 = (bf16[768,3072]{1,0:T(8,128)(2,1)S(1)}, bf16[3072,768]{1,0:T(8,128)(2,1)S(1)}, f32[8,128]{1,0:T(8,128)}) custom-call(f32[8,128]{1,0:T(8,128)S(1)} %slice_bitcast_fusion.after_ref, bf16[1,768,3072]{2,1,0:T(8,128)(2,1)} %refs_6_.3, bf16[1,3072,768]{2,1,0:T(8,128)(2,1)} %refs_7_.1), custom_call_target="tpu_custom_call" | custom-call | tf_op jit(solution)/shard_map/load/pallas_call | solution.py:787
  72.7 2.6 %hidden_grads.1 = (f32[256,3072]{1,0:T(8,128)S(1)}, f32[256,3072]{1,0:T(8,128)S(1)}) custom-call(bf16[256,768]{1,0:T(8,128)(2,1)S(1)} %pad_maximum_fusion.first_ref.refs_2_.refs_4_, bf16[256,768]{1,0:T(8,128)(2,1)S(1)} %constant_dynamic-update-slice_fusion.second_ref.refs_2_.refs_5_, bf16[3072,768]{1,0:T(8,128)(2,1)S(1)} %get-tuple-element.166.w2_ref.refs_5_.refs_10_.refs_6_), custom_call_target="tpu_custom_call" | custom-call | tf_op jit(solution)/shard_map/hidden_grads/pallas_call | solution.py:857
  75.3 3.1 %collective-permute-done.17.refs_1_ = bf16[128,768]{1,0:T(8,128)(2,1)S(1)} collective-permute-done((bf16[128,768]{1,0:T(8,128)(2,1)S(1)}, bf16[128,768]{1,0:T(8,128)(2,1)S(1)}, u32[]{:S(2)}, u32[]{:S(2)}) %collective-permute-start.17) | collective-permute-done | bytes 196640 | tf_op jit(solution)/shard_map/ppermute | solution.py:588
  80.1 2.4 %collective-permute-start.21 = (bf16[128,768]{1,0:T(8,128)(2,1)S(1)}, bf16[128,768]{1,0:T(8,128)(2,1)S(1)}, u32[]{:S(2)}, u32[]{:S(2)}) collective-permute-start(bf16[128,768]{1,0:T(8,128)(2,1)S(1)} %get-tuple-element.171), channel_id=1, source_target_pairs={{0,6},{1,7},{2,4},{3,5},{4,2},{5,3},{6,0},{7,1},{8,14},{9,15},{10,... | collective-permute-start | bytes 589832 | tf_op jit(solution)/shard_map/ppermute | solution.py:588
  82.6 5.1 %expert.2 = (bf16[128,768]{1,0:T(8,128)(2,1)S(1)}, bf16[128,768]{1,0:T(8,128)(2,1)S(1)}, bf16[128,768]{1,0:T(8,128)(2,1)S(1)}, bf16[128,768]{1,0:T(8,128)(2,1)S(...) custom-call(s32[1]{0:T(128)} %bitcast.11.own_ref.refs_4_, bf16[128,768]{1,0:T(8,128)(2,1)S(1)} %get-tuple-element.160.refs_0_, ...), custom_call_target="tpu_custom_call" | custom-call | tf_op jit(solution)/shard_map/expert/pallas_call | solution.py:870
  91.4 4.9 %expert.3 = (bf16[128,768]{1,0:T(8,128)(2,1)S(1)}, bf16[128,768]{1,0:T(8,128)(2,1)S(1)}, bf16[128,768]{1,0:T(8,128)(2,1)S(1)}, bf16[128,768]{1,0:T(8,128)(2,1)S(...) custom-call(s32[1]{0:T(128)} %bitcast.11.own_ref.refs_4_, bf16[128,768]{1,0:T(8,128)(2,1)S(1)} %collective-permute-done.20.refs_0_, ...), custom_call_target="tpu_custom_call" | custom-call | tf_op jit(solution)/shard_map/expert/pallas_call | solution.py:870
  96.2 4.8 %collective-permute-done.24.refs_2_ = bf16[128,768]{1,0:T(8,128)(2,1)S(1)} collective-permute-done((bf16[128,768]{1,0:T(8,128)(2,1)S(1)}, bf16[128,768]{1,0:T(8,128)(2,1)S(1)}, u32[]{:S(2)}, u32[]{:S(2)}) %collective-permute-start.24) | collective-permute-done | bytes 196640 | tf_op jit(solution)/shard_map/ppermute | solution.py:588
  101.0 1.6 collective-permute-start.26
  103.8 3.6 %collective-permute-start.30 = (bf16[256,768]{1,0:T(8,128)(2,1)S(1)}, bf16[256,768]{1,0:T(8,128)(2,1)S(1)}, u32[]{:S(2)}, u32[]{:S(2)}) collective-permute-start(bf16[256,768]{1,0:T(8,128)(2,1)S(1)} %get-tuple-element.188.refs_1_), channel_id=1, source_target_pairs={{0,16},{8,24},{16,0},{24,8},{1,17},{9,25},{17,1},{25,9},{2,18},{10... | collective-permute-start | bytes 1179656 | tf_op jit(solution)/shard_map/ppermute | solution.py:585
  107.3 4.8 %collective-permute-done.25.refs_1_ = bf16[128,768]{1,0:T(8,128)(2,1)S(1)} collective-permute-done((bf16[128,768]{1,0:T(8,128)(2,1)S(1)}, bf16[128,768]{1,0:T(8,128)(2,1)S(1)}, u32[]{:S(2)}, u32[]{:S(2)}) %collective-permute-start.25) | collective-permute-done | bytes 196640 | tf_op jit(solution)/shard_map/ppermute | solution.py:588
  114.3 2.7 %middle.1 = (f32[256,768]{1,0:T(8,128)S(1)}, f32[1,768]{1,0:T(1,128)S(1)}, bf16[256,768]{1,0:T(8,128)(2,1)S(1)}, bf16[640,768]{1,0:T(8,128)(2,1)S(1)}) custom-call(bf16[128,768]{1,0:T(8,128)(2,1)S(1)} %get-tuple-element.180.refs_0_, bf16[128,768]{1,0:T(8,128)(2,1)S(1)} %collective-permute-done.25.refs_1_, ...), custom_call_target="tpu_custom_call" | custom-call | flops 1024 | bytes 1024 | tf_op jit(solution)/shard_map/middle/pallas_call | solution.py:960
  119.1 5.8 %score_grads.1 = (bf16[512,768]{1,0:T(8,128)(2,1)S(1)}, f32[12,1,512]{2,1,0:T(1,128)S(1)}) custom-call(bf16[256,768]{1,0:T(8,128)(2,1)S(1)} %get-tuple-element.193.mixed_grad_ref, bf16[256,768]{1,0:T(8,128)(2,1)S(1)} %get-tuple-element.194.v_ref, bf16[256,768]{1,0:T(8,128)(2,1)S(1)} %get-tuple-element.195.q_ref, ...), custom_call_target="tpu_custom_call" | custom-call | flops 1024 | bytes 1024 | tf_op jit(solution)/shard_map/score_grads/pallas_call | solution.py:993
  124.9 3.8 %collective-permute-done.33.refs_0_ = bf16[256,768]{1,0:T(8,128)(2,1)S(1)} collective-permute-done((bf16[256,768]{1,0:T(8,128)(2,1)S(1)}, bf16[256,768]{1,0:T(8,128)(2,1)S(1)}, u32[]{:S(2)}, u32[]{:S(2)}) %collective-permute-start.33) | collective-permute-done | bytes 393248 | tf_op jit(solution)/shard_map/ppermute | solution.py:585
  135.1 1.8 collective-permute-start.37
  136.9 3.9 %inputs.1 = (f32[256,768]{1,0:T(8,128)}, f32[16,768]{1,0:T(8,128)S(1)}) custom-call(bf16[512,768]{1,0:T(8,128)(2,1)S(1)} %get-tuple-element.200.qk_ref.refs_0_, bf16[640,768]{1,0:T(8,128)(2,1)S(1)} %get-tuple-element.192.vo_ref.refs_1_, bf16[256,768]{1,0:T(8,128)(2,1)S(1)} %copy-done.1, f32[1,768]{1,0:T(1,128)S(1)} %get-tuple-element.210.refs_3_, ...), custom_call_target="tpu_custom_call" | custom-call | flops 1024 | bytes 1024 | tf_op jit(solution)/shard_map/inputs/pallas_call | solution.py:1005
  143.0 6.9 %expert_grads.3 = (f32[768,768]{1,0:T(8,128)S(1)}, f32[768,768]{1,0:T(8,128)S(1)}) custom-call(s32[1]{0:T(128)} %bitcast.11.own_ref.refs_4_, s32[1]{0:T(128)} %bitcast.19.place_ref, bf16[256,768]{1,0:T(8,128)(2,1)S(1)} %get-tuple-element.187.refs_0_, bf16[256,768]{1,0:T(8,128)(2,1)S(1)} %get-tuple-element.188.refs_1_, ...), custom_call_target="tpu_custom_call" | custom-call | tf_op jit(solution)/shard_map/expert_grads/pallas_call | solution.py:931
  155.2 7.3 %expert_grads.4 = (f32[1,768,768]{2,1,0:T(8,128)}, f32[1,768,768]{2,1,0:T(8,128)}) custom-call(s32[1]{0:T(128)} %bitcast.11.own_ref.refs_4_, s32[1]{0:T(128)} %bitcast.19.place_ref, bf16[256,768]{1,0:T(8,128)(2,1)} %copy-done.12, bf16[256,768]{1,0:T(8,128)(2,1)} %copy-done.15, bf16[256,768]{1,0:T(8,128)(2,1)} %copy-done.8, bf16[256,768]{1,0:T(8,128)(2,1)} %copy-done.11, ...), custom_call_target="tpu_custom_call" | custom-call | tf_op jit(solution)/shard_map/expert_grads/pallas_call | solution.py:944
  163.6 2.0 %collective-permute-start.47 = (bf16[112,768]{1,0:T(8,128)(2,1)S(1)}, bf16[112,768]{1,0:T(8,128)(2,1)S(1)}, u32[]{:S(2)}, u32[]{:S(2)}) collective-permute-start(bf16[112,768]{1,0:T(8,128)(2,1)S(1)} %get-tuple-element.235), channel_id=1, source_target_pairs={{0,4},{1,5},{2,6},{3,7},{4,0},{5,1},{6,2},{7,3},{8,12},{9,13},{10,... | collective-permute-start | bytes 516104 | tf_op jit(solution)/shard_map/ppermute | solution.py:588
  165.6 1.8 collective-permute-start.48
  167.4 8.7 %expert_grads.5 = (f32[1,768,768]{2,1,0:T(8,128)}, f32[1,768,768]{2,1,0:T(8,128)}) custom-call(s32[1]{0:T(128)} %bitcast.19.place_ref, bf16[256,768]{1,0:T(8,128)(2,1)} %copy-done.13, bf16[256,768]{1,0:T(8,128)(2,1)} %copy-done.14, bf16[256,768]{1,0:T(8,128)(2,1)} %copy-done.9, bf16[256,768]{1,0:T(8,128)(2,1)} %copy-done.10, s32[1]{0:T(128)} %bitcast.11.own_ref.refs_4_, ...), custom_call_target="tpu_custom_call" | custom-call | flops 1024 | bytes 1024 | tf_op jit(solution)/shard_map/expert_grads/pallas_call | solution.py:904
  (160 shorter events, 49.4 us)
Async XLA Ops:
  2.2 11.8 %collective-permute-start.2 = (bf16[24,3200]{1,0:T(8,128)(2,1)}, bf16[24,3200]{1,0:T(8,128)(2,1)S(1)}, u32[]{:S(2)}, u32[]{:S(2)}) collective-permute-start(bf16[24,3200]{1,0:T(8,128)(2,1)} %pack.1), channel_id=1, source_target_pairs={{0,6},{1,7},{2,4},{3,5},{4,2},{5,3},{6,0},{7,1},{8,14},{9,15},{10,... | collective-permute-start | bytes 460808 | tf_op jit(solution)/shard_map/ppermute | solution.py:588
  7.3 13.2 %collective-permute-start.1 = (bf16[24,3200]{1,0:T(8,128)(2,1)}, bf16[24,3200]{1,0:T(8,128)(2,1)S(1)}, u32[]{:S(2)}, u32[]{:S(2)}) collective-permute-start(bf16[24,3200]{1,0:T(8,128)(2,1)} %pack.1), channel_id=1, source_target_pairs={{0,4},{1,5},{2,6},{3,7},{4,0},{5,1},{6,2},{7,3},{8,12},{9,13},{10,... | collective-permute-start | bytes 460808 | tf_op jit(solution)/shard_map/ppermute | solution.py:588
  7.3 13.2 %collective-permute-start = (bf16[24,3200]{1,0:T(8,128)(2,1)}, bf16[24,3200]{1,0:T(8,128)(2,1)S(1)}, u32[]{:S(2)}, u32[]{:S(2)}) collective-permute-start(bf16[24,3200]{1,0:T(8,128)(2,1)} %pack.1), channel_id=1, source_target_pairs={{0,2},{1,3},{2,0},{3,1},{4,6},{5,7},{6,4},{7,5},{8,10},{9,11},{10,... | collective-permute-start | bytes 460808 | tf_op jit(solution)/shard_map/ppermute | solution.py:588
  13.9 11.5 %collective-permute-start.3 = (bf16[384,768]{1,0:T(8,128)(2,1)S(1)}, bf16[384,768]{1,0:T(8,128)(2,1)S(1)}, u32[]{:S(2)}, u32[]{:S(2)}) collective-permute-start(bf16[384,768]{1,0:T(8,128)(2,1)S(1)} %get-tuple-element.138), channel_id=1, source_target_pairs={{0,1},{1,0},{2,3},{3,2},{4,5},{5,4},{6,7},{7,6},{8,9},{9,8},{10,11... | collective-permute-start | bytes 1769480 | tf_op jit(solution)/shard_map/ppermute | solution.py:579
  34.6 17.0 %collective-permute-start.10 = (bf16[192,3200]{1,0:T(8,128)(2,1)}, bf16[192,3200]{1,0:T(8,128)(2,1)S(1)}, u32[]{:S(2)}, u32[]{:S(2)}) collective-permute-start(bf16[192,3200]{1,0:T(8,128)(2,1)} %get-tuple-element.148), channel_id=1, source_target_pairs={{0,1},{1,0},{2,3},{3,2},{4,5},{5,4},{6,7},{7,6},{8,9},{9,8},{10,11... | collective-permute-start | bytes 3686408 | tf_op jit(solution)/shard_map/ppermute | solution.py:579
  34.6 17.0 %collective-permute-start.8 = (bf16[192,1664]{1,0:T(8,128)(2,1)}, bf16[192,1664]{1,0:T(8,128)(2,1)S(1)}, u32[]{:S(2)}, u32[]{:S(2)}) collective-permute-start(bf16[192,1664]{1,0:T(8,128)(2,1)} %get-tuple-element.146), channel_id=1, source_target_pairs={{0,8},{8,0},{16,24},{24,16},{1,9},{9,1},{17,25},{25,17},{2,10},{10... | collective-permute-start | bytes 1916936 | tf_op jit(solution)/shard_map/ppermute | solution.py:582
  35.2 15.7 %collective-permute-start.7 = (bf16[192,1536]{1,0:T(8,128)(2,1)}, bf16[192,1536]{1,0:T(8,128)(2,1)S(1)}, u32[]{:S(2)}, u32[]{:S(2)}) collective-permute-start(bf16[192,1536]{1,0:T(8,128)(2,1)} %get-tuple-element.145), channel_id=1, source_target_pairs={{0,16},{8,24},{16,0},{24,8},{1,17},{9,25},{17,1},{25,9},{2,18},{10... | collective-permute-start | bytes 1769480 | tf_op jit(solution)/shard_map/ppermute | solution.py:585
  35.8 11.6 %collective-permute-start.9 = (bf16[128,768]{1,0:T(8,128)(2,1)S(1)}, bf16[128,768]{1,0:T(8,128)(2,1)S(1)}, u32[]{:S(2)}, u32[]{:S(2)}) collective-permute-start(bf16[128,768]{1,0:T(8,128)(2,1)S(1)} %copy-done.16), channel_id=1, source_target_pairs={{0,4},{1,5},{2,6},{3,7},{4,0},{5,1},{6,2},{7,3},{8,12},{9,13},{10,... | collective-permute-start | bytes 589832 | tf_op jit(solution)/shard_map/ppermute | solution.py:588
  52.2 11.4 %collective-permute-start.13 = (bf16[128,768]{1,0:T(8,128)(2,1)S(1)}, bf16[128,768]{1,0:T(8,128)(2,1)S(1)}, u32[]{:S(2)}, u32[]{:S(2)}) collective-permute-start(bf16[128,768]{1,0:T(8,128)(2,1)S(1)} %get-tuple-element.157), channel_id=1, source_target_pairs={{0,6},{1,7},{2,4},{3,5},{4,2},{5,3},{6,0},{7,1},{8,14},{9,15},{10,... | collective-permute-start | bytes 589832 | tf_op jit(solution)/shard_map/ppermute | solution.py:588
  54.7 10.8 %collective-permute-start.16 = (bf16[256,768]{1,0:T(8,128)(2,1)S(1)}, bf16[256,768]{1,0:T(8,128)(2,1)S(1)}, u32[]{:S(2)}, u32[]{:S(2)}) collective-permute-start(bf16[256,768]{1,0:T(8,128)(2,1)S(1)} %pad_maximum_fusion.first_ref.refs_2_.refs_4_), channel_id=1, source_target_pairs={{0,16},{8,24},{16,0},{24,8},{1,17},{9,25},{17,1},{25,9},{2,18},{10... | collective-permute-start | bytes 1179656 | tf_op jit(solution)/shard_map/ppermute | solution.py:585
  65.7 12.8 %collective-permute-start.19 = (bf16[256,768]{1,0:T(8,128)(2,1)S(1)}, bf16[256,768]{1,0:T(8,128)(2,1)S(1)}, u32[]{:S(2)}, u32[]{:S(2)}) collective-permute-start(bf16[256,768]{1,0:T(8,128)(2,1)S(1)} %constant_dynamic-update-slice_fusion.second_ref.refs_2_.refs_5_), channel_id=1, source_target_pairs={{0,8},{8,0},{16,24},{24,16},{1,9},{9,1},{17,25},{25,17},{2,10},{10... | collective-permute-start | bytes 1179656 | tf_op jit(solution)/shard_map/ppermute | solution.py:582
  66.6 11.9 %collective-permute-start.18 = (bf16[256,768]{1,0:T(8,128)(2,1)S(1)}, bf16[256,768]{1,0:T(8,128)(2,1)S(1)}, u32[]{:S(2)}, u32[]{:S(2)}) collective-permute-start(bf16[256,768]{1,0:T(8,128)(2,1)S(1)} %constant_dynamic-update-slice_fusion.second_ref.refs_2_.refs_5_), channel_id=1, source_target_pairs={{0,16},{8,24},{16,0},{24,8},{1,17},{9,25},{17,1},{25,9},{2,18},{10... | collective-permute-start | bytes 1179656 | tf_op jit(solution)/shard_map/ppermute | solution.py:585
  78.5 11.2 %collective-permute-start.22 = (bf16[256,768]{1,0:T(8,128)(2,1)S(1)}, bf16[256,768]{1,0:T(8,128)(2,1)S(1)}, u32[]{:S(2)}, u32[]{:S(2)}) collective-permute-start(bf16[256,768]{1,0:T(8,128)(2,1)S(1)} %collective-permute-done.15.refs_6_), channel_id=1, source_target_pairs={{0,16},{8,24},{16,0},{24,8},{1,17},{9,25},{17,1},{25,9},{2,18},{10... | collective-permute-start | bytes 1179656 | tf_op jit(solution)/shard_map/ppermute | solution.py:585
  79.2 11.1 %collective-permute-start.23 = (bf16[256,768]{1,0:T(8,128)(2,1)S(1)}, bf16[256,768]{1,0:T(8,128)(2,1)S(1)}, u32[]{:S(2)}, u32[]{:S(2)}) collective-permute-start(bf16[256,768]{1,0:T(8,128)(2,1)S(1)} %collective-permute-done.18.refs_7_), channel_id=1, source_target_pairs={{0,8},{8,0},{16,24},{24,16},{1,9},{9,1},{17,25},{25,17},{2,10},{10... | collective-permute-start | bytes 1179656 | tf_op jit(solution)/shard_map/ppermute | solution.py:582
  80.1 11.2 %collective-permute-start.20 = (bf16[128,768]{1,0:T(8,128)(2,1)S(1)}, bf16[128,768]{1,0:T(8,128)(2,1)S(1)}, u32[]{:S(2)}, u32[]{:S(2)}) collective-permute-start(bf16[128,768]{1,0:T(8,128)(2,1)S(1)} %get-tuple-element.169), channel_id=1, source_target_pairs={{0,2},{1,3},{2,0},{3,1},{4,6},{5,7},{6,4},{7,5},{8,10},{9,11},{10,... | collective-permute-start | bytes 589832 | tf_op jit(solution)/shard_map/ppermute | solution.py:588
  80.1 11.3 %collective-permute-start.21 = (bf16[128,768]{1,0:T(8,128)(2,1)S(1)}, bf16[128,768]{1,0:T(8,128)(2,1)S(1)}, u32[]{:S(2)}, u32[]{:S(2)}) collective-permute-start(bf16[128,768]{1,0:T(8,128)(2,1)S(1)} %get-tuple-element.171), channel_id=1, source_target_pairs={{0,6},{1,7},{2,4},{3,5},{4,2},{5,3},{6,0},{7,1},{8,14},{9,15},{10,... | collective-permute-start | bytes 589832 | tf_op jit(solution)/shard_map/ppermute | solution.py:588
  87.6 15.0 %collective-permute-start.29 = (bf16[256,768]{1,0:T(8,128)(2,1)S(1)}, bf16[256,768]{1,0:T(8,128)(2,1)S(1)}, u32[]{:S(2)}, u32[]{:S(2)}) collective-permute-start(bf16[256,768]{1,0:T(8,128)(2,1)S(1)} %get-tuple-element.187.refs_0_), channel_id=1, source_target_pairs={{0,16},{8,24},{16,0},{24,8},{1,17},{9,25},{17,1},{25,9},{2,18},{10... | collective-permute-start | bytes 1179656 | tf_op jit(solution)/shard_map/ppermute | solution.py:585
  89.7 13.0 %collective-permute-start.28 = (bf16[256,768]{1,0:T(8,128)(2,1)S(1)}, bf16[256,768]{1,0:T(8,128)(2,1)S(1)}, u32[]{:S(2)}, u32[]{:S(2)}) collective-permute-start(bf16[256,768]{1,0:T(8,128)(2,1)S(1)} %get-tuple-element.187.refs_0_), channel_id=1, source_target_pairs={{0,8},{8,0},{16,24},{24,16},{1,9},{9,1},{17,25},{25,17},{2,10},{10... | collective-permute-start | bytes 1179656 | tf_op jit(solution)/shard_map/ppermute | solution.py:582
  101.0 11.0 %collective-permute-start.25 = (bf16[128,768]{1,0:T(8,128)(2,1)S(1)}, bf16[128,768]{1,0:T(8,128)(2,1)S(1)}, u32[]{:S(2)}, u32[]{:S(2)}) collective-permute-start(bf16[128,768]{1,0:T(8,128)(2,1)S(1)} %get-tuple-element.184), channel_id=1, source_target_pairs={{0,2},{1,3},{2,0},{3,1},{4,6},{5,7},{6,4},{7,5},{8,10},{9,11},{10,... | collective-permute-start | bytes 589832 | tf_op jit(solution)/shard_map/ppermute | solution.py:588
  101.0 11.0 %collective-permute-start.26 = (bf16[128,768]{1,0:T(8,128)(2,1)S(1)}, bf16[128,768]{1,0:T(8,128)(2,1)S(1)}, u32[]{:S(2)}, u32[]{:S(2)}) collective-permute-start(bf16[128,768]{1,0:T(8,128)(2,1)S(1)} %get-tuple-element.185), channel_id=1, source_target_pairs={{0,6},{1,7},{2,4},{3,5},{4,2},{5,3},{6,0},{7,1},{8,14},{9,15},{10,... | collective-permute-start | bytes 589832 | tf_op jit(solution)/shard_map/ppermute | solution.py:588
  117.1 12.2 %collective-permute-start.32 = (bf16[640,768]{1,0:T(8,128)(2,1)S(1)}, bf16[640,768]{1,0:T(8,128)(2,1)S(1)}, u32[]{:S(2)}, u32[]{:S(2)}) collective-permute-start(bf16[640,768]{1,0:T(8,128)(2,1)S(1)} %get-tuple-element.192.vo_ref.refs_1_), channel_id=1, source_target_pairs={{0,1},{1,0},{2,3},{3,2},{4,5},{5,4},{6,7},{7,6},{8,9},{9,8},{10,11... | collective-permute-start | bytes 2949128 | tf_op jit(solution)/shard_map/ppermute | solution.py:579
  117.1 11.5 %collective-permute-start.33 = (bf16[256,768]{1,0:T(8,128)(2,1)S(1)}, bf16[256,768]{1,0:T(8,128)(2,1)S(1)}, u32[]{:S(2)}, u32[]{:S(2)}) collective-permute-start(bf16[256,768]{1,0:T(8,128)(2,1)S(1)} %collective-permute-done.28.refs_2_), channel_id=1, source_target_pairs={{0,16},{8,24},{16,0},{24,8},{1,17},{9,25},{17,1},{25,9},{2,18},{10... | collective-permute-start | bytes 1179656 | tf_op jit(solution)/shard_map/ppermute | solution.py:585
  118.1 11.2 %collective-permute-start.34 = (bf16[256,768]{1,0:T(8,128)(2,1)S(1)}, bf16[256,768]{1,0:T(8,128)(2,1)S(1)}, u32[]{:S(2)}, u32[]{:S(2)}) collective-permute-start(bf16[256,768]{1,0:T(8,128)(2,1)S(1)} %collective-permute-done.30.refs_3_), channel_id=1, source_target_pairs={{0,8},{8,0},{16,24},{24,16},{1,9},{9,1},{17,25},{25,17},{2,10},{10... | collective-permute-start | bytes 1179656 | tf_op jit(solution)/shard_map/ppermute | solution.py:582
  133.1 16.8 %collective-permute-start.36 = (bf16[192,1536]{1,0:T(8,128)(2,1)S(1)}, bf16[192,1536]{1,0:T(8,128)(2,1)S(1)}, u32[]{:S(2)}, u32[]{:S(2)}) collective-permute-start(bf16[192,1536]{1,0:T(8,128)(2,1)S(1)} %get-tuple-element.202), channel_id=1, source_target_pairs={{0,16},{8,24},{16,0},{24,8},{1,17},{9,25},{17,1},{25,9},{2,18},{10... | collective-permute-start | bytes 1769480 | tf_op jit(solution)/shard_map/ppermute | solution.py:585
  134.3 15.7 %collective-permute-start.38 = (bf16[192,1536]{1,0:T(8,128)(2,1)S(1)}, bf16[192,1536]{1,0:T(8,128)(2,1)S(1)}, u32[]{:S(2)}, u32[]{:S(2)}) collective-permute-start(bf16[192,1536]{1,0:T(8,128)(2,1)S(1)} %get-tuple-element.203), channel_id=1, source_target_pairs={{0,8},{8,0},{16,24},{24,16},{1,9},{9,1},{17,25},{25,17},{2,10},{10... | collective-permute-start | bytes 1769480 | tf_op jit(solution)/shard_map/ppermute | solution.py:582
  135.1 14.9 %collective-permute-start.37 = (bf16[128,768]{1,0:T(8,128)(2,1)S(1)}, bf16[128,768]{1,0:T(8,128)(2,1)S(1)}, u32[]{:S(2)}, u32[]{:S(2)}) collective-permute-start(bf16[128,768]{1,0:T(8,128)(2,1)S(1)} %get-tuple-element.207), channel_id=1, source_target_pairs={{0,4},{1,5},{2,6},{3,7},{4,0},{5,1},{6,2},{7,3},{8,12},{9,13},{10,... | collective-permute-start | bytes 589832 | tf_op jit(solution)/shard_map/ppermute | solution.py:588
  150.2 12.4 %collective-permute-start.41 = (bf16[128,768]{1,0:T(8,128)(2,1)S(1)}, bf16[128,768]{1,0:T(8,128)(2,1)S(1)}, u32[]{:S(2)}, u32[]{:S(2)}) collective-permute-start(bf16[128,768]{1,0:T(8,128)(2,1)S(1)} %get-tuple-element.219), channel_id=1, source_target_pairs={{0,2},{1,3},{2,0},{3,1},{4,6},{5,7},{6,4},{7,5},{8,10},{9,11},{10,... | collective-permute-start | bytes 589832 | tf_op jit(solution)/shard_map/ppermute | solution.py:588
  151.5 11.3 %collective-permute-start.44 = (bf16[96,1536]{1,0:T(8,128)(2,1)S(1)}, bf16[96,1536]{1,0:T(8,128)(2,1)S(1)}, u32[]{:S(2)}, u32[]{:S(2)}) collective-permute-start(bf16[96,1536]{1,0:T(8,128)(2,1)S(1)} %get-tuple-element.218), channel_id=1, source_target_pairs={{0,16},{8,24},{16,0},{24,8},{1,17},{9,25},{17,1},{25,9},{2,18},{10... | collective-permute-start | bytes 884744 | tf_op jit(solution)/shard_map/ppermute | solution.py:585
  162.8 13.2 %collective-permute-start.45 = (bf16[256,768]{1,0:T(8,128)(2,1)S(1)}, bf16[256,768]{1,0:T(8,128)(2,1)}, u32[]{:S(2)}, u32[]{:S(2)}) collective-permute-start(bf16[256,768]{1,0:T(8,128)(2,1)S(1)} %pad_maximum_fusion.2), channel_id=1, source_target_pairs={{0,1},{1,0},{2,3},{3,2},{4,5},{5,4},{6,7},{7,6},{8,9},{9,8},{10,11... | collective-permute-start | bytes 1179656 | tf_op jit(solution)/shard_map/ppermute | solution.py:579
  163.6 15.6 %collective-permute-start.47 = (bf16[112,768]{1,0:T(8,128)(2,1)S(1)}, bf16[112,768]{1,0:T(8,128)(2,1)S(1)}, u32[]{:S(2)}, u32[]{:S(2)}) collective-permute-start(bf16[112,768]{1,0:T(8,128)(2,1)S(1)} %get-tuple-element.235), channel_id=1, source_target_pairs={{0,4},{1,5},{2,6},{3,7},{4,0},{5,1},{6,2},{7,3},{8,12},{9,13},{10,... | collective-permute-start | bytes 516104 | tf_op jit(solution)/shard_map/ppermute | solution.py:588
  165.6 13.6 %collective-permute-start.48 = (bf16[112,768]{1,0:T(8,128)(2,1)S(1)}, bf16[112,768]{1,0:T(8,128)(2,1)S(1)}, u32[]{:S(2)}, u32[]{:S(2)}) collective-permute-start(bf16[112,768]{1,0:T(8,128)(2,1)S(1)} %get-tuple-element.236), channel_id=1, source_target_pairs={{0,6},{1,7},{2,4},{3,5},{4,2},{5,3},{6,0},{7,1},{8,14},{9,15},{10,... | collective-permute-start | bytes 516104 | tf_op jit(solution)/shard_map/ppermute | solution.py:588
  167.4 12.1 %collective-permute-start.46 = (bf16[112,768]{1,0:T(8,128)(2,1)S(1)}, bf16[112,768]{1,0:T(8,128)(2,1)S(1)}, u32[]{:S(2)}, u32[]{:S(2)}) collective-permute-start(bf16[112,768]{1,0:T(8,128)(2,1)S(1)} %get-tuple-element.234.own_ref), channel_id=1, source_target_pairs={{0,2},{1,3},{2,0},{3,1},{4,6},{5,7},{6,4},{7,5},{8,10},{9,11},{10,... | collective-permute-start | bytes 516104 | tf_op jit(solution)/shard_map/ppermute | solution.py:588
  (37 other events, 262.9 us)

commit v6 on v5

--- a/solution.py
+++ b/solution.py
@@ -56,11 +56,11 @@
 
 
 def gelu_parts(v):
+    c = 0.7978845608
     square = v * v
-    bent = jnp.tanh(0.7978845608 * v * (1.0 + 0.044715 * square))
-    half = 0.5 * (1.0 + bent)
-    slope = half + 0.5 * v * (1.0 - bent * bent) * (0.7978845608 * (1.0 + 0.134145 * square))
-    return v * half, slope
+    half = 0.5 + 0.5 * jnp.tanh(v * (c + (c * 0.044715) * square))
+    value = v * half
+    return value, half + value * (1.0 - half) * (2.0 * c + (2.0 * c * 0.134145) * square)
 
 
 def gate_of(rows, router, picked):

time: 184 us -> 183 us (level)
  transfers between devices with their start and end apart: 49 -> 49, of which waited for: 20 -> 20; matrix products, arithmetic and copies ran while one was open for 5% -> 5% of each run, Pallas kernels for 34% -> 33%
where the time goes in v6:
time: 183 us; the launch traced here: 180 us
  Pallas kernels  68 us (37%)
  waiting for transfers between devices  50.8 us (28%)
  starting transfers between devices  46.8 us (26%)
  local copies, waits for them, and re-layouts  8.92 us (5%)
  other arithmetic  3.17 us (2%)
    ppermute x18, waiting for transfers between devices, far(): lax.ppermute(v, 'expert', [(i, i ^ 2 * k) for i in range(self.experts)])  35.7 us
    ppermute x18, starting transfers between devices, far(): lax.ppermute(v, 'expert', [(i, i ^ 2 * k) for i in range(self.experts)])  22.7 us
    ppermute x11, starting transfers between devices, y(): return lax.ppermute(v, 'dp', [(i, i ^ 2) for i in range(self.dp)])  14 us
    ppermute x11, waiting for transfers between devices, y(): return lax.ppermute(v, 'dp', [(i, i ^ 2) for i in range(self.dp)])  10.1 us
    pallas_call x2, Pallas kernels, expert(): pl.pallas_call(functools.partial(expert_kernel, len(sizes)), out_shape=tu...  9.89 us
    ppermute x10, starting transfers between devices, x(): return lax.ppermute(v, 'dp', [(i, i ^ 1) for i in range(self.dp)])  9.25 us
    pallas_call x1, Pallas kernels, expert_grads(): pl.pallas_call(functools.partial(expert_grad_kernel, len(sizes), bool(bef...  8.61 us
    pallas_call x1, Pallas kernels, per_device(): pl.pallas_call(functools.partial(attend_kernel, head), out_shape=tuple((p...  7.62 us
  transfers between devices with their start and end apart: 49, of which 20 were waited for; matrix products, arithmetic and copies ran while one was open for 5% of the time, Pallas kernels for 33%

profile of v6, /device:TPU:0, one launch (start us, length us, event | category | flops | bytes accessed | tf_op | source)
XLA Modules:
  0.0 180.4 jit_solution(15768538174010858115)
XLA Ops:
  0.6 1.6 pack.1
  2.2 5.0 %collective-permute-start.2 = (bf16[24,3200]{1,0:T(8,128)(2,1)}, bf16[24,3200]{1,0:T(8,128)(2,1)S(1)}, u32[]{:S(2)}, u32[]{:S(2)}) collective-permute-start(bf16[24,3200]{1,0:T(8,128)(2,1)} %pack.1), channel_id=1, source_target_pairs={{0,6},{1,7},{2,4},{3,5},{4,2},{5,3},{6,0},{7,1},{8,14},{9,15},{10,... | collective-permute-start | bytes 460808 | tf_op jit(solution)/shard_map/ppermute | solution.py:588
  12.3 1.6 route.1
  14.0 6.4 %collective-permute-done.1 = bf16[24,3200]{1,0:T(8,128)(2,1)S(1)} collective-permute-done((bf16[24,3200]{1,0:T(8,128)(2,1)}, bf16[24,3200]{1,0:T(8,128)(2,1)S(1)}, u32[]{:S(2)}, u32[]{:S(2)}) %collective-permute-start.1) | collective-permute-done | bytes 153632 | tf_op jit(solution)/shard_map/ppermute | solution.py:588
  22.3 1.6 collective-permute-start.5
  28.6 4.4 %collective-permute-done.4 = bf16[128,768]{1,0:T(8,128)(2,1)} collective-permute-done((bf16[128,768]{1,0:T(8,128)(2,1)}, bf16[128,768]{1,0:T(8,128)(2,1)}, u32[]{:S(2)}, u32[]{:S(2)}) %collective-permute-start.4) | collective-permute-done | bytes 196640 | tf_op jit(solution)/shard_map/ppermute | solution.py:588
  33.0 1.6 near.1
  36.7 10.7 %collective-permute-done.9 = bf16[128,768]{1,0:T(8,128)(2,1)S(1)} collective-permute-done((bf16[128,768]{1,0:T(8,128)(2,1)S(1)}, bf16[128,768]{1,0:T(8,128)(2,1)S(1)}, u32[]{:S(2)}, u32[]{:S(2)}) %collective-permute-start.9) | collective-permute-done | bytes 196640 | tf_op jit(solution)/shard_map/ppermute | solution.py:588
  47.4 3.5 %collective-permute-done.7.refs_8_.refs_12_ = bf16[192,1536]{1,0:T(8,128)(2,1)S(1)} collective-permute-done((bf16[192,1536]{1,0:T(8,128)(2,1)}, bf16[192,1536]{1,0:T(8,128)(2,1)S(1)}, u32[]{:S(2)}, u32[]{:S(2)}) %collective-permute-start.7) | collective-permute-done | bytes 589856 | tf_op jit(solution)/shard_map/ppermute | solution.py:585
  52.2 2.5 %collective-permute-start.13 = (bf16[128,768]{1,0:T(8,128)(2,1)S(1)}, bf16[128,768]{1,0:T(8,128)(2,1)S(1)}, u32[]{:S(2)}, u32[]{:S(2)}) collective-permute-start(bf16[128,768]{1,0:T(8,128)(2,1)S(1)} %get-tuple-element.157), channel_id=1, source_target_pairs={{0,6},{1,7},{2,4},{3,5},{4,2},{5,3},{6,0},{7,1},{8,14},{9,15},{10,... | collective-permute-start | bytes 589832 | tf_op jit(solution)/shard_map/ppermute | solution.py:588
  55.9 7.6 %attend.1 = (bf16[256,768]{1,0:T(8,128)(2,1)S(1)}, bf16[256,768]{1,0:T(8,128)(2,1)S(1)}, bf16[256,768]{1,0:T(8,128)(2,1)S(1)}, f32[12,256,256]{2,1,0:T(8,128)S(1...) custom-call(bf16[256,768]{1,0:T(8,128)(2,1)S(1)} %get-tuple-element., ...), custom_call_target="tpu_custom_call" | custom-call | tf_op jit(solution)/shard_map/attend/pallas_call | solution.py:825
  68.3 4.4 %load.1 = (bf16[768,3072]{1,0:T(8,128)(2,1)S(1)}, bf16[3072,768]{1,0:T(8,128)(2,1)S(1)}, f32[8,128]{1,0:T(8,128)}) custom-call(f32[8,128]{1,0:T(8,128)S(1)} %slice_bitcast_fusion.after_ref, bf16[1,768,3072]{2,1,0:T(8,128)(2,1)} %refs_6_.3, bf16[1,3072,768]{2,1,0:T(8,128)(2,1)} %refs_7_.1), custom_call_target="tpu_custom_call" | custom-call | tf_op jit(solution)/shard_map/load/pallas_call | solution.py:787
  72.7 2.6 %hidden_grads.1 = (f32[256,3072]{1,0:T(8,128)S(1)}, f32[256,3072]{1,0:T(8,128)S(1)}) custom-call(bf16[256,768]{1,0:T(8,128)(2,1)S(1)} %pad_maximum_fusion.first_ref.refs_2_.refs_4_, bf16[256,768]{1,0:T(8,128)(2,1)S(1)} %constant_dynamic-update-slice_fusion.second_ref.refs_2_.refs_5_, bf16[3072,768]{1,0:T(8,128)(2,1)S(1)} %get-tuple-element.166.w2_ref.refs_5_.refs_10_.refs_6_), custom_call_target="tpu_custom_call" | custom-call | tf_op jit(solution)/shard_map/hidden_grads/pallas_call | solution.py:857
  75.3 3.1 %collective-permute-done.17.refs_1_ = bf16[128,768]{1,0:T(8,128)(2,1)S(1)} collective-permute-done((bf16[128,768]{1,0:T(8,128)(2,1)S(1)}, bf16[128,768]{1,0:T(8,128)(2,1)S(1)}, u32[]{:S(2)}, u32[]{:S(2)}) %collective-permute-start.17) | collective-permute-done | bytes 196640 | tf_op jit(solution)/shard_map/ppermute | solution.py:588
  80.1 2.4 %collective-permute-start.21 = (bf16[128,768]{1,0:T(8,128)(2,1)S(1)}, bf16[128,768]{1,0:T(8,128)(2,1)S(1)}, u32[]{:S(2)}, u32[]{:S(2)}) collective-permute-start(bf16[128,768]{1,0:T(8,128)(2,1)S(1)} %get-tuple-element.171), channel_id=1, source_target_pairs={{0,6},{1,7},{2,4},{3,5},{4,2},{5,3},{6,0},{7,1},{8,14},{9,15},{10,... | collective-permute-start | bytes 589832 | tf_op jit(solution)/shard_map/ppermute | solution.py:588
  82.5 5.1 %expert.2 = (bf16[128,768]{1,0:T(8,128)(2,1)S(1)}, bf16[128,768]{1,0:T(8,128)(2,1)S(1)}, bf16[128,768]{1,0:T(8,128)(2,1)S(1)}, bf16[128,768]{1,0:T(8,128)(2,1)S(...) custom-call(s32[1]{0:T(128)} %bitcast.11.own_ref.refs_4_, bf16[128,768]{1,0:T(8,128)(2,1)S(1)} %get-tuple-element.160.refs_0_, ...), custom_call_target="tpu_custom_call" | custom-call | tf_op jit(solution)/shard_map/expert/pallas_call | solution.py:870
  91.4 4.8 %expert.3 = (bf16[128,768]{1,0:T(8,128)(2,1)S(1)}, bf16[128,768]{1,0:T(8,128)(2,1)S(1)}, bf16[128,768]{1,0:T(8,128)(2,1)S(1)}, bf16[128,768]{1,0:T(8,128)(2,1)S(...) custom-call(s32[1]{0:T(128)} %bitcast.11.own_ref.refs_4_, bf16[128,768]{1,0:T(8,128)(2,1)S(1)} %collective-permute-done.20.refs_0_, ...), custom_call_target="tpu_custom_call" | custom-call | tf_op jit(solution)/shard_map/expert/pallas_call | solution.py:870
  96.2 4.9 %collective-permute-done.24.refs_2_ = bf16[128,768]{1,0:T(8,128)(2,1)S(1)} collective-permute-done((bf16[128,768]{1,0:T(8,128)(2,1)S(1)}, bf16[128,768]{1,0:T(8,128)(2,1)S(1)}, u32[]{:S(2)}, u32[]{:S(2)}) %collective-permute-start.24) | collective-permute-done | bytes 196640 | tf_op jit(solution)/shard_map/ppermute | solution.py:588
  101.1 1.6 collective-permute-start.26
  103.8 3.5 %collective-permute-start.30 = (bf16[256,768]{1,0:T(8,128)(2,1)S(1)}, bf16[256,768]{1,0:T(8,128)(2,1)S(1)}, u32[]{:S(2)}, u32[]{:S(2)}) collective-permute-start(bf16[256,768]{1,0:T(8,128)(2,1)S(1)} %get-tuple-element.188.refs_1_), channel_id=1, source_target_pairs={{0,16},{8,24},{16,0},{24,8},{1,17},{9,25},{17,1},{25,9},{2,18},{10... | collective-permute-start | bytes 1179656 | tf_op jit(solution)/shard_map/ppermute | solution.py:585
  107.3 4.8 %collective-permute-done.25.refs_1_ = bf16[128,768]{1,0:T(8,128)(2,1)S(1)} collective-permute-done((bf16[128,768]{1,0:T(8,128)(2,1)S(1)}, bf16[128,768]{1,0:T(8,128)(2,1)S(1)}, u32[]{:S(2)}, u32[]{:S(2)}) %collective-permute-start.25) | collective-permute-done | bytes 196640 | tf_op jit(solution)/shard_map/ppermute | solution.py:588
  114.3 2.8 %middle.1 = (f32[256,768]{1,0:T(8,128)S(1)}, f32[1,768]{1,0:T(1,128)S(1)}, bf16[256,768]{1,0:T(8,128)(2,1)S(1)}, bf16[640,768]{1,0:T(8,128)(2,1)S(1)}) custom-call(bf16[128,768]{1,0:T(8,128)(2,1)S(1)} %get-tuple-element.180.refs_0_, bf16[128,768]{1,0:T(8,128)(2,1)S(1)} %collective-permute-done.25.refs_1_, ...), custom_call_target="tpu_custom_call" | custom-call | flops 1024 | bytes 1024 | tf_op jit(solution)/shard_map/middle/pallas_call | solution.py:960
  119.1 5.8 %score_grads.1 = (bf16[512,768]{1,0:T(8,128)(2,1)S(1)}, f32[12,1,512]{2,1,0:T(1,128)S(1)}) custom-call(bf16[256,768]{1,0:T(8,128)(2,1)S(1)} %get-tuple-element.193.mixed_grad_ref, bf16[256,768]{1,0:T(8,128)(2,1)S(1)} %get-tuple-element.194.v_ref, bf16[256,768]{1,0:T(8,128)(2,1)S(1)} %get-tuple-element.195.q_ref, ...), custom_call_target="tpu_custom_call" | custom-call | flops 1024 | bytes 1024 | tf_op jit(solution)/shard_map/score_grads/pallas_call | solution.py:993
  124.9 3.7 %collective-permute-done.33.refs_0_ = bf16[256,768]{1,0:T(8,128)(2,1)S(1)} collective-permute-done((bf16[256,768]{1,0:T(8,128)(2,1)S(1)}, bf16[256,768]{1,0:T(8,128)(2,1)S(1)}, u32[]{:S(2)}, u32[]{:S(2)}) %collective-permute-start.33) | collective-permute-done | bytes 393248 | tf_op jit(solution)/shard_map/ppermute | solution.py:585
  135.1 1.8 collective-permute-start.37
  136.9 3.9 %inputs.1 = (f32[256,768]{1,0:T(8,128)}, f32[16,768]{1,0:T(8,128)S(1)}) custom-call(bf16[512,768]{1,0:T(8,128)(2,1)S(1)} %get-tuple-element.200.qk_ref.refs_0_, bf16[640,768]{1,0:T(8,128)(2,1)S(1)} %get-tuple-element.192.vo_ref.refs_1_, bf16[256,768]{1,0:T(8,128)(2,1)S(1)} %copy-done.1, f32[1,768]{1,0:T(1,128)S(1)} %get-tuple-element.210.refs_3_, ...), custom_call_target="tpu_custom_call" | custom-call | flops 1024 | bytes 1024 | tf_op jit(solution)/shard_map/inputs/pallas_call | solution.py:1005
  143.0 6.6 %expert_grads.3 = (f32[768,768]{1,0:T(8,128)S(1)}, f32[768,768]{1,0:T(8,128)S(1)}) custom-call(s32[1]{0:T(128)} %bitcast.11.own_ref.refs_4_, s32[1]{0:T(128)} %bitcast.19.place_ref, bf16[256,768]{1,0:T(8,128)(2,1)S(1)} %get-tuple-element.187.refs_0_, bf16[256,768]{1,0:T(8,128)(2,1)S(1)} %get-tuple-element.188.refs_1_, ...), custom_call_target="tpu_custom_call" | custom-call | tf_op jit(solution)/shard_map/expert_grads/pallas_call | solution.py:931
  153.5 1.6 collective-permute-start.42
  155.1 6.9 %expert_grads.4 = (f32[1,768,768]{2,1,0:T(8,128)}, f32[1,768,768]{2,1,0:T(8,128)}) custom-call(s32[1]{0:T(128)} %bitcast.11.own_ref.refs_4_, s32[1]{0:T(128)} %bitcast.19.place_ref, bf16[256,768]{1,0:T(8,128)(2,1)} %copy-done.12, bf16[256,768]{1,0:T(8,128)(2,1)} %copy-done.15, bf16[256,768]{1,0:T(8,128)(2,1)} %copy-done.8, bf16[256,768]{1,0:T(8,128)(2,1)} %copy-done.11, ...), custom_call_target="tpu_custom_call" | custom-call | tf_op jit(solution)/shard_map/expert_grads/pallas_call | solution.py:944
  163.1 2.2 %collective-permute-start.47 = (bf16[112,768]{1,0:T(8,128)(2,1)S(1)}, bf16[112,768]{1,0:T(8,128)(2,1)S(1)}, u32[]{:S(2)}, u32[]{:S(2)}) collective-permute-start(bf16[112,768]{1,0:T(8,128)(2,1)S(1)} %get-tuple-element.235), channel_id=1, source_target_pairs={{0,4},{1,5},{2,6},{3,7},{4,0},{5,1},{6,2},{7,3},{8,12},{9,13},{10,... | collective-permute-start | bytes 516104 | tf_op jit(solution)/shard_map/ppermute | solution.py:588
  165.3 1.8 collective-permute-start.48
  167.0 8.6 %expert_grads.5 = (f32[1,768,768]{2,1,0:T(8,128)}, f32[1,768,768]{2,1,0:T(8,128)}) custom-call(s32[1]{0:T(128)} %bitcast.19.place_ref, bf16[256,768]{1,0:T(8,128)(2,1)} %copy-done.13, bf16[256,768]{1,0:T(8,128)(2,1)} %copy-done.14, bf16[256,768]{1,0:T(8,128)(2,1)} %copy-done.9, bf16[256,768]{1,0:T(8,128)(2,1)} %copy-done.10, s32[1]{0:T(128)} %bitcast.11.own_ref.refs_4_, ...), custom_call_target="tpu_custom_call" | custom-call | flops 1024 | bytes 1024 | tf_op jit(solution)/shard_map/expert_grads/pallas_call | solution.py:904
  (160 shorter events, 49.5 us)
Async XLA Ops:
  2.2 11.8 %collective-permute-start.2 = (bf16[24,3200]{1,0:T(8,128)(2,1)}, bf16[24,3200]{1,0:T(8,128)(2,1)S(1)}, u32[]{:S(2)}, u32[]{:S(2)}) collective-permute-start(bf16[24,3200]{1,0:T(8,128)(2,1)} %pack.1), channel_id=1, source_target_pairs={{0,6},{1,7},{2,4},{3,5},{4,2},{5,3},{6,0},{7,1},{8,14},{9,15},{10,... | collective-permute-start | bytes 460808 | tf_op jit(solution)/shard_map/ppermute | solution.py:588
  7.3 13.2 %collective-permute-start.1 = (bf16[24,3200]{1,0:T(8,128)(2,1)}, bf16[24,3200]{1,0:T(8,128)(2,1)S(1)}, u32[]{:S(2)}, u32[]{:S(2)}) collective-permute-start(bf16[24,3200]{1,0:T(8,128)(2,1)} %pack.1), channel_id=1, source_target_pairs={{0,4},{1,5},{2,6},{3,7},{4,0},{5,1},{6,2},{7,3},{8,12},{9,13},{10,... | collective-permute-start | bytes 460808 | tf_op jit(solution)/shard_map/ppermute | solution.py:588
  7.3 13.2 %collective-permute-start = (bf16[24,3200]{1,0:T(8,128)(2,1)}, bf16[24,3200]{1,0:T(8,128)(2,1)S(1)}, u32[]{:S(2)}, u32[]{:S(2)}) collective-permute-start(bf16[24,3200]{1,0:T(8,128)(2,1)} %pack.1), channel_id=1, source_target_pairs={{0,2},{1,3},{2,0},{3,1},{4,6},{5,7},{6,4},{7,5},{8,10},{9,11},{10,... | collective-permute-start | bytes 460808 | tf_op jit(solution)/shard_map/ppermute | solution.py:588
  13.9 11.4 %collective-permute-start.3 = (bf16[384,768]{1,0:T(8,128)(2,1)S(1)}, bf16[384,768]{1,0:T(8,128)(2,1)S(1)}, u32[]{:S(2)}, u32[]{:S(2)}) collective-permute-start(bf16[384,768]{1,0:T(8,128)(2,1)S(1)} %get-tuple-element.138), channel_id=1, source_target_pairs={{0,1},{1,0},{2,3},{3,2},{4,5},{5,4},{6,7},{7,6},{8,9},{9,8},{10,11... | collective-permute-start | bytes 1769480 | tf_op jit(solution)/shard_map/ppermute | solution.py:579
  34.6 17.0 %collective-permute-start.10 = (bf16[192,3200]{1,0:T(8,128)(2,1)}, bf16[192,3200]{1,0:T(8,128)(2,1)S(1)}, u32[]{:S(2)}, u32[]{:S(2)}) collective-permute-start(bf16[192,3200]{1,0:T(8,128)(2,1)} %get-tuple-element.148), channel_id=1, source_target_pairs={{0,1},{1,0},{2,3},{3,2},{4,5},{5,4},{6,7},{7,6},{8,9},{9,8},{10,11... | collective-permute-start | bytes 3686408 | tf_op jit(solution)/shard_map/ppermute | solution.py:579
  34.6 17.0 %collective-permute-start.8 = (bf16[192,1664]{1,0:T(8,128)(2,1)}, bf16[192,1664]{1,0:T(8,128)(2,1)S(1)}, u32[]{:S(2)}, u32[]{:S(2)}) collective-permute-start(bf16[192,1664]{1,0:T(8,128)(2,1)} %get-tuple-element.146), channel_id=1, source_target_pairs={{0,8},{8,0},{16,24},{24,16},{1,9},{9,1},{17,25},{25,17},{2,10},{10... | collective-permute-start | bytes 1916936 | tf_op jit(solution)/shard_map/ppermute | solution.py:582
  35.2 15.7 %collective-permute-start.7 = (bf16[192,1536]{1,0:T(8,128)(2,1)}, bf16[192,1536]{1,0:T(8,128)(2,1)S(1)}, u32[]{:S(2)}, u32[]{:S(2)}) collective-permute-start(bf16[192,1536]{1,0:T(8,128)(2,1)} %get-tuple-element.145), channel_id=1, source_target_pairs={{0,16},{8,24},{16,0},{24,8},{1,17},{9,25},{17,1},{25,9},{2,18},{10... | collective-permute-start | bytes 1769480 | tf_op jit(solution)/shard_map/ppermute | solution.py:585
  35.8 11.6 %collective-permute-start.9 = (bf16[128,768]{1,0:T(8,128)(2,1)S(1)}, bf16[128,768]{1,0:T(8,128)(2,1)S(1)}, u32[]{:S(2)}, u32[]{:S(2)}) collective-permute-start(bf16[128,768]{1,0:T(8,128)(2,1)S(1)} %copy-done.16), channel_id=1, source_target_pairs={{0,4},{1,5},{2,6},{3,7},{4,0},{5,1},{6,2},{7,3},{8,12},{9,13},{10,... | collective-permute-start | bytes 589832 | tf_op jit(solution)/shard_map/ppermute | solution.py:588
  52.2 11.4 %collective-permute-start.13 = (bf16[128,768]{1,0:T(8,128)(2,1)S(1)}, bf16[128,768]{1,0:T(8,128)(2,1)S(1)}, u32[]{:S(2)}, u32[]{:S(2)}) collective-permute-start(bf16[128,768]{1,0:T(8,128)(2,1)S(1)} %get-tuple-element.157), channel_id=1, source_target_pairs={{0,6},{1,7},{2,4},{3,5},{4,2},{5,3},{6,0},{7,1},{8,14},{9,15},{10,... | collective-permute-start | bytes 589832 | tf_op jit(solution)/shard_map/ppermute | solution.py:588
  54.7 10.8 %collective-permute-start.16 = (bf16[256,768]{1,0:T(8,128)(2,1)S(1)}, bf16[256,768]{1,0:T(8,128)(2,1)S(1)}, u32[]{:S(2)}, u32[]{:S(2)}) collective-permute-start(bf16[256,768]{1,0:T(8,128)(2,1)S(1)} %pad_maximum_fusion.first_ref.refs_2_.refs_4_), channel_id=1, source_target_pairs={{0,16},{8,24},{16,0},{24,8},{1,17},{9,25},{17,1},{25,9},{2,18},{10... | collective-permute-start | bytes 1179656 | tf_op jit(solution)/shard_map/ppermute | solution.py:585
  65.7 12.8 %collective-permute-start.19 = (bf16[256,768]{1,0:T(8,128)(2,1)S(1)}, bf16[256,768]{1,0:T(8,128)(2,1)S(1)}, u32[]{:S(2)}, u32[]{:S(2)}) collective-permute-start(bf16[256,768]{1,0:T(8,128)(2,1)S(1)} %constant_dynamic-update-slice_fusion.second_ref.refs_2_.refs_5_), channel_id=1, source_target_pairs={{0,8},{8,0},{16,24},{24,16},{1,9},{9,1},{17,25},{25,17},{2,10},{10... | collective-permute-start | bytes 1179656 | tf_op jit(solution)/shard_map/ppermute | solution.py:582
  66.6 11.9 %collective-permute-start.18 = (bf16[256,768]{1,0:T(8,128)(2,1)S(1)}, bf16[256,768]{1,0:T(8,128)(2,1)S(1)}, u32[]{:S(2)}, u32[]{:S(2)}) collective-permute-start(bf16[256,768]{1,0:T(8,128)(2,1)S(1)} %constant_dynamic-update-slice_fusion.second_ref.refs_2_.refs_5_), channel_id=1, source_target_pairs={{0,16},{8,24},{16,0},{24,8},{1,17},{9,25},{17,1},{25,9},{2,18},{10... | collective-permute-start | bytes 1179656 | tf_op jit(solution)/shard_map/ppermute | solution.py:585
  78.5 11.2 %collective-permute-start.22 = (bf16[256,768]{1,0:T(8,128)(2,1)S(1)}, bf16[256,768]{1,0:T(8,128)(2,1)S(1)}, u32[]{:S(2)}, u32[]{:S(2)}) collective-permute-start(bf16[256,768]{1,0:T(8,128)(2,1)S(1)} %collective-permute-done.15.refs_6_), channel_id=1, source_target_pairs={{0,16},{8,24},{16,0},{24,8},{1,17},{9,25},{17,1},{25,9},{2,18},{10... | collective-permute-start | bytes 1179656 | tf_op jit(solution)/shard_map/ppermute | solution.py:585
  79.2 11.1 %collective-permute-start.23 = (bf16[256,768]{1,0:T(8,128)(2,1)S(1)}, bf16[256,768]{1,0:T(8,128)(2,1)S(1)}, u32[]{:S(2)}, u32[]{:S(2)}) collective-permute-start(bf16[256,768]{1,0:T(8,128)(2,1)S(1)} %collective-permute-done.18.refs_7_), channel_id=1, source_target_pairs={{0,8},{8,0},{16,24},{24,16},{1,9},{9,1},{17,25},{25,17},{2,10},{10... | collective-permute-start | bytes 1179656 | tf_op jit(solution)/shard_map/ppermute | solution.py:582
  80.1 11.1 %collective-permute-start.20 = (bf16[128,768]{1,0:T(8,128)(2,1)S(1)}, bf16[128,768]{1,0:T(8,128)(2,1)S(1)}, u32[]{:S(2)}, u32[]{:S(2)}) collective-permute-start(bf16[128,768]{1,0:T(8,128)(2,1)S(1)} %get-tuple-element.169), channel_id=1, source_target_pairs={{0,2},{1,3},{2,0},{3,1},{4,6},{5,7},{6,4},{7,5},{8,10},{9,11},{10,... | collective-permute-start | bytes 589832 | tf_op jit(solution)/shard_map/ppermute | solution.py:588
  80.1 11.2 %collective-permute-start.21 = (bf16[128,768]{1,0:T(8,128)(2,1)S(1)}, bf16[128,768]{1,0:T(8,128)(2,1)S(1)}, u32[]{:S(2)}, u32[]{:S(2)}) collective-permute-start(bf16[128,768]{1,0:T(8,128)(2,1)S(1)} %get-tuple-element.171), channel_id=1, source_target_pairs={{0,6},{1,7},{2,4},{3,5},{4,2},{5,3},{6,0},{7,1},{8,14},{9,15},{10,... | collective-permute-start | bytes 589832 | tf_op jit(solution)/shard_map/ppermute | solution.py:588
  87.6 15.0 %collective-permute-start.29 = (bf16[256,768]{1,0:T(8,128)(2,1)S(1)}, bf16[256,768]{1,0:T(8,128)(2,1)S(1)}, u32[]{:S(2)}, u32[]{:S(2)}) collective-permute-start(bf16[256,768]{1,0:T(8,128)(2,1)S(1)} %get-tuple-element.187.refs_0_), channel_id=1, source_target_pairs={{0,16},{8,24},{16,0},{24,8},{1,17},{9,25},{17,1},{25,9},{2,18},{10... | collective-permute-start | bytes 1179656 | tf_op jit(solution)/shard_map/ppermute | solution.py:585
  89.7 13.0 %collective-permute-start.28 = (bf16[256,768]{1,0:T(8,128)(2,1)S(1)}, bf16[256,768]{1,0:T(8,128)(2,1)S(1)}, u32[]{:S(2)}, u32[]{:S(2)}) collective-permute-start(bf16[256,768]{1,0:T(8,128)(2,1)S(1)} %get-tuple-element.187.refs_0_), channel_id=1, source_target_pairs={{0,8},{8,0},{16,24},{24,16},{1,9},{9,1},{17,25},{25,17},{2,10},{10... | collective-permute-start | bytes 1179656 | tf_op jit(solution)/shard_map/ppermute | solution.py:582
  101.0 11.0 %collective-permute-start.25 = (bf16[128,768]{1,0:T(8,128)(2,1)S(1)}, bf16[128,768]{1,0:T(8,128)(2,1)S(1)}, u32[]{:S(2)}, u32[]{:S(2)}) collective-permute-start(bf16[128,768]{1,0:T(8,128)(2,1)S(1)} %get-tuple-element.184), channel_id=1, source_target_pairs={{0,2},{1,3},{2,0},{3,1},{4,6},{5,7},{6,4},{7,5},{8,10},{9,11},{10,... | collective-permute-start | bytes 589832 | tf_op jit(solution)/shard_map/ppermute | solution.py:588
  101.1 11.0 %collective-permute-start.26 = (bf16[128,768]{1,0:T(8,128)(2,1)S(1)}, bf16[128,768]{1,0:T(8,128)(2,1)S(1)}, u32[]{:S(2)}, u32[]{:S(2)}) collective-permute-start(bf16[128,768]{1,0:T(8,128)(2,1)S(1)} %get-tuple-element.185), channel_id=1, source_target_pairs={{0,6},{1,7},{2,4},{3,5},{4,2},{5,3},{6,0},{7,1},{8,14},{9,15},{10,... | collective-permute-start | bytes 589832 | tf_op jit(solution)/shard_map/ppermute | solution.py:588
  117.1 12.2 %collective-permute-start.32 = (bf16[640,768]{1,0:T(8,128)(2,1)S(1)}, bf16[640,768]{1,0:T(8,128)(2,1)S(1)}, u32[]{:S(2)}, u32[]{:S(2)}) collective-permute-start(bf16[640,768]{1,0:T(8,128)(2,1)S(1)} %get-tuple-element.192.vo_ref.refs_1_), channel_id=1, source_target_pairs={{0,1},{1,0},{2,3},{3,2},{4,5},{5,4},{6,7},{7,6},{8,9},{9,8},{10,11... | collective-permute-start | bytes 2949128 | tf_op jit(solution)/shard_map/ppermute | solution.py:579
  117.1 11.5 %collective-permute-start.33 = (bf16[256,768]{1,0:T(8,128)(2,1)S(1)}, bf16[256,768]{1,0:T(8,128)(2,1)S(1)}, u32[]{:S(2)}, u32[]{:S(2)}) collective-permute-start(bf16[256,768]{1,0:T(8,128)(2,1)S(1)} %collective-permute-done.28.refs_2_), channel_id=1, source_target_pairs={{0,16},{8,24},{16,0},{24,8},{1,17},{9,25},{17,1},{25,9},{2,18},{10... | collective-permute-start | bytes 1179656 | tf_op jit(solution)/shard_map/ppermute | solution.py:585
  118.1 11.2 %collective-permute-start.34 = (bf16[256,768]{1,0:T(8,128)(2,1)S(1)}, bf16[256,768]{1,0:T(8,128)(2,1)S(1)}, u32[]{:S(2)}, u32[]{:S(2)}) collective-permute-start(bf16[256,768]{1,0:T(8,128)(2,1)S(1)} %collective-permute-done.30.refs_3_), channel_id=1, source_target_pairs={{0,8},{8,0},{16,24},{24,16},{1,9},{9,1},{17,25},{25,17},{2,10},{10... | collective-permute-start | bytes 1179656 | tf_op jit(solution)/shard_map/ppermute | solution.py:582
  133.1 16.5 %collective-permute-start.36 = (bf16[192,1536]{1,0:T(8,128)(2,1)S(1)}, bf16[192,1536]{1,0:T(8,128)(2,1)S(1)}, u32[]{:S(2)}, u32[]{:S(2)}) collective-permute-start(bf16[192,1536]{1,0:T(8,128)(2,1)S(1)} %get-tuple-element.202), channel_id=1, source_target_pairs={{0,16},{8,24},{16,0},{24,8},{1,17},{9,25},{17,1},{25,9},{2,18},{10... | collective-permute-start | bytes 1769480 | tf_op jit(solution)/shard_map/ppermute | solution.py:585
  134.3 15.3 %collective-permute-start.38 = (bf16[192,1536]{1,0:T(8,128)(2,1)S(1)}, bf16[192,1536]{1,0:T(8,128)(2,1)S(1)}, u32[]{:S(2)}, u32[]{:S(2)}) collective-permute-start(bf16[192,1536]{1,0:T(8,128)(2,1)S(1)} %get-tuple-element.203), channel_id=1, source_target_pairs={{0,8},{8,0},{16,24},{24,16},{1,9},{9,1},{17,25},{25,17},{2,10},{10... | collective-permute-start | bytes 1769480 | tf_op jit(solution)/shard_map/ppermute | solution.py:582
  135.1 14.5 %collective-permute-start.37 = (bf16[128,768]{1,0:T(8,128)(2,1)S(1)}, bf16[128,768]{1,0:T(8,128)(2,1)S(1)}, u32[]{:S(2)}, u32[]{:S(2)}) collective-permute-start(bf16[128,768]{1,0:T(8,128)(2,1)S(1)} %get-tuple-element.207), channel_id=1, source_target_pairs={{0,4},{1,5},{2,6},{3,7},{4,0},{5,1},{6,2},{7,3},{8,12},{9,13},{10,... | collective-permute-start | bytes 589832 | tf_op jit(solution)/shard_map/ppermute | solution.py:588
  149.8 12.2 %collective-permute-start.41 = (bf16[128,768]{1,0:T(8,128)(2,1)S(1)}, bf16[128,768]{1,0:T(8,128)(2,1)S(1)}, u32[]{:S(2)}, u32[]{:S(2)}) collective-permute-start(bf16[128,768]{1,0:T(8,128)(2,1)S(1)} %get-tuple-element.219), channel_id=1, source_target_pairs={{0,2},{1,3},{2,0},{3,1},{4,6},{5,7},{6,4},{7,5},{8,10},{9,11},{10,... | collective-permute-start | bytes 589832 | tf_op jit(solution)/shard_map/ppermute | solution.py:588
  151.3 10.9 %collective-permute-start.44 = (bf16[96,1536]{1,0:T(8,128)(2,1)S(1)}, bf16[96,1536]{1,0:T(8,128)(2,1)S(1)}, u32[]{:S(2)}, u32[]{:S(2)}) collective-permute-start(bf16[96,1536]{1,0:T(8,128)(2,1)S(1)} %get-tuple-element.218), channel_id=1, source_target_pairs={{0,16},{8,24},{16,0},{24,8},{1,17},{9,25},{17,1},{25,9},{2,18},{10... | collective-permute-start | bytes 884744 | tf_op jit(solution)/shard_map/ppermute | solution.py:585
  162.3 13.3 %collective-permute-start.45 = (bf16[256,768]{1,0:T(8,128)(2,1)S(1)}, bf16[256,768]{1,0:T(8,128)(2,1)}, u32[]{:S(2)}, u32[]{:S(2)}) collective-permute-start(bf16[256,768]{1,0:T(8,128)(2,1)S(1)} %pad_maximum_fusion.2), channel_id=1, source_target_pairs={{0,1},{1,0},{2,3},{3,2},{4,5},{5,4},{6,7},{7,6},{8,9},{9,8},{10,11... | collective-permute-start | bytes 1179656 | tf_op jit(solution)/shard_map/ppermute | solution.py:579
  163.1 15.6 %collective-permute-start.47 = (bf16[112,768]{1,0:T(8,128)(2,1)S(1)}, bf16[112,768]{1,0:T(8,128)(2,1)S(1)}, u32[]{:S(2)}, u32[]{:S(2)}) collective-permute-start(bf16[112,768]{1,0:T(8,128)(2,1)S(1)} %get-tuple-element.235), channel_id=1, source_target_pairs={{0,4},{1,5},{2,6},{3,7},{4,0},{5,1},{6,2},{7,3},{8,12},{9,13},{10,... | collective-permute-start | bytes 516104 | tf_op jit(solution)/shard_map/ppermute | solution.py:588
  165.3 13.5 %collective-permute-start.48 = (bf16[112,768]{1,0:T(8,128)(2,1)S(1)}, bf16[112,768]{1,0:T(8,128)(2,1)S(1)}, u32[]{:S(2)}, u32[]{:S(2)}) collective-permute-start(bf16[112,768]{1,0:T(8,128)(2,1)S(1)} %get-tuple-element.236), channel_id=1, source_target_pairs={{0,6},{1,7},{2,4},{3,5},{4,2},{5,3},{6,0},{7,1},{8,14},{9,15},{10,... | collective-permute-start | bytes 516104 | tf_op jit(solution)/shard_map/ppermute | solution.py:588
  167.0 12.0 %collective-permute-start.46 = (bf16[112,768]{1,0:T(8,128)(2,1)S(1)}, bf16[112,768]{1,0:T(8,128)(2,1)S(1)}, u32[]{:S(2)}, u32[]{:S(2)}) collective-permute-start(bf16[112,768]{1,0:T(8,128)(2,1)S(1)} %get-tuple-element.234.own_ref), channel_id=1, source_target_pairs={{0,2},{1,3},{2,0},{3,1},{4,6},{5,7},{6,4},{7,5},{8,10},{9,11},{10,... | collective-permute-start | bytes 516104 | tf_op jit(solution)/shard_map/ppermute | solution.py:588
  (37 other events, 261.9 us)
